TPU v7x, 32 devices: a whole 2x2x4 slice. The times are simulated.
32 devices in a mesh: dp: 4 (over y, x), wide: 4 (over z), narrow: 2 (over core).
Axes of the slice: x: 2, y: 2, z: 4, core: 2. Of those that a mesh axis runs over, the one named last changes fastest.
Arguments:
- grad_parts: bfloat16 [8, 32, 73728], P(('dp', 'narrow'), 'wide'), may hold values from -8 to 8
- weight: bfloat16 [32, 73728], P('wide', ('dp', 'narrow')), may hold values from -12 to 12
- row_state: float32 [32], P('wide'), may hold values from 0.01 to 1
- col_state: float32 [73728], P(('dp', 'narrow')), may hold values from 0.01 to 1
Outputs:
- update: float32 [32, 73728], P('wide', ('dp', 'narrow'))
- new_row_state: float32 [32], P('wide')
- new_col_state: float32 [73728], P(('dp', 'narrow'))
All inputs are finite; a program needn't handle non-finite values.
Results may differ from a plain program's by a relative error of at most 0.0003.
Values sent between devices are 32-bit elements; how exact they have to be, the bound alone decides.
No kernel may reach another device: no remote copies, remote signals or barrier semaphores. Data moves between devices by JAX's collectives and lax.ppermute only.
A program may use at most 64 MiB of HBM per device.

v0:
```python
import jax
import jax.numpy as jnp
from jax import lax
from jax.sharding import PartitionSpec as P

FF = 73728
STEP = 100


def on_device(grad_parts, weight, row_state, col_state):
    local_part = grad_parts[0].astype(jnp.float32)
    grad = lax.psum_scatter(local_part, ("dp", "narrow"), scatter_dimension=1, tiled=True)
    rows_all = grad.shape[0] * lax.axis_size("wide")
    square = grad * grad + 1e-30
    col_part = jnp.sum(square, axis=0)
    row_part = jnp.sum(square, axis=1)
    weight_f = weight.astype(jnp.float32)
    weight_part = jnp.sum(weight_f * weight_f)
    col_sum = lax.psum(col_part, "wide")
    row_sum = lax.psum(row_part, ("dp", "narrow"))
    weight_total = lax.psum(weight_part, ("dp", "wide", "narrow"))
    beta = 1.0 - STEP ** (-0.8)
    new_row_state = beta * row_state + (1.0 - beta) * (row_sum / FF)
    new_col_state = beta * col_state + (1.0 - beta) * (col_sum / rows_all)
    factor = new_row_state[:, None] * new_col_state[None, :]
    scaled = grad / jnp.sqrt(factor)
    update_sum = lax.psum(jnp.sum(scaled * scaled), ("dp", "wide", "narrow"))
    clip = jnp.maximum(1.0, jnp.sqrt(update_sum / (rows_all * FF)))
    weight_rms = jnp.maximum(0.001, jnp.sqrt(weight_total / (rows_all * FF)))
    update = weight_rms * scaled / clip
    return (update, new_row_state, new_col_state)


def solution(mesh):
    return jax.shard_map(
        on_device,
        mesh=mesh,
        in_specs=(
            P(("dp", "narrow"), "wide", None),
            P("wide", ("dp", "narrow")),
            P("wide"),
            P(("dp", "narrow")),
        ),
        out_specs=(P("wide", ("dp", "narrow")), P("wide"), P(("dp", "narrow"))),
        check_vma=False,
    )
```

profile of v0, /device:TPU:0, one launch (start us, length us, event | category | flops | bytes accessed | tf_op | source)
XLA Modules:
  0.0 138.5 jit_solution(8737129168898251508)
XLA Ops:
  7.2 0.0 copy-start.1
  7.2 0.0 copy-start.2
  7.2 0.0 reduce-scatter.2.cloned.1.call-start
  7.2 2.9 %bitcast_convert_fusion = f32[8,73728]{1,0:T(8,128)} fusion(bf16[1,8,73728]{2,1,0:T(8,128)(2,1)} %param.4), kind=kLoop, calls=%fused_computation | loop fusion | flops 589824 | bytes 3538944 | tf_op jit(solution)/shard_map/convert_element_type | solution.py:11
  10.1 0.0 copy-start.4
  10.1 0.0 reduce-scatter.2.cloned.1.call-update
  10.1 0.0 copy-done.1
  10.1 0.7 multiply_reduce_fusion.1
  10.8 45.8 %reduce-scatter.2.cloned.1.call-done = f32[8,9216]{1,0:T(8,128)} async-done(((f32[8,73728]{1,0:T(8,128)}), f32[8,9216]{1,0:T(8,128)}) %reduce-scatter.2.cloned.1.call-update) | async-done | bytes 294928 | tf_op jit(solution)/shard_map/reduce_scatter | solution.py:12
  56.6 1.2 fusion.1
  57.8 19.3 %psum.30 = f32[9216]{0:T(1024)S(1)} all-reduce(f32[9216]{0:T(1024)S(1)} %get-tuple-element.4), channel_id=1, replica_groups=mesh['dp'=4,'wide'=4,'narrow'=2] {'wide'}, use_global_device_ids=true, to_apply=%region_6.0 | all-reduce | flops 9216 | bytes 73728 | tf_op jit(solution)/shard_map/psum | solution.py:19
  77.1 11.8 %psum.29 = f32[8]{0:T(128)S(1)} all-reduce(f32[8]{0:T(128)S(1)} %get-tuple-element.3), channel_id=1, replica_groups=mesh['dp'=4,'wide'=4,'narrow'=2] {'dp','narrow'}, use_global_device_ids=true, to_apply=%region_4.0 | all-reduce | flops 8 | bytes 64 | tf_op jit(solution)/shard_map/psum | solution.py:20
  89.0 0.0 copy-done.2
  89.0 0.0 copy-done.4
  89.0 0.0 copy-start
  89.0 0.0 copy-start.3
  89.0 1.7 %multiply_reduce_fusion = f32[]{:T(128)} fusion(f32[8,9216]{1,0:T(8,128)} %reduce-scatter.2.cloned.1.call-done, f32[9216]{0:T(1024)S(1)} %multiply_add_fusion.1, f32[8]{0:T(128)S(1)} %multiply_add_fusion.2), kind=kLoop, calls=%fused_computation.1 | loop fusion | flops 294911 | bytes 331812 | tf_op jit(solution)/shard_map/reduce_sum | solution.py:27
  90.8 37.7 %all-reduce = (f32[]{:T(128)}, f32[]{:T(128)}) all-reduce(f32[]{:T(128)} %multiply_reduce_fusion, f32[]{:T(128)} %multiply_reduce_fusion.1), channel_id=1, replica_groups=mesh['dp'=4,'wide'=4,'narrow'=2] {'dp','wide','narrow'}, use_global_device_ids=true, to_apply=%region_8.0 | all-reduce | flops 2 | bytes 16 | tf_op jit(solution)/shard_map/psum | solution.py:27
  129.8 1.8 %multiply_divide_fusion = f32[8,9216]{1,0:T(8,128)} fusion(f32[8,9216]{1,0:T(8,128)} %reduce-scatter.2.cloned.1.call-done, f32[]{:T(128)S(6)} %max_shard_map.7, f32[9216]{0:T(1024)S(1)} %multiply_add_fusion.1, f32[8]{0:T(128)S(1)} %multiply_add_fusion.2, f32[]{:T(128)S(6)} %max_shard_map.6), kind=kLoop, calls=%fused_computation.2 | loop fusion | flops 294912 | bytes 626728 | tf_op jit(solution)/shard_map/div | solution.py:30
  131.6 0.0 copy-done
  131.6 0.0 copy-done.3
  (2 shorter events, 0.0 us)
Async XLA Ops:
  7.2 3.0 %copy-start.1 = (bf16[8,9216]{1,0:T(8,128)(2,1)S(1)}, bf16[8,9216]{1,0:T(8,128)(2,1)}, u32[]{:S(2)}) copy-start(bf16[8,9216]{1,0:T(8,128)(2,1)} %param.5) | copy-start | bytes 442372
  7.2 81.8 %copy-start.2 = (f32[9216]{0:T(1024)S(1)}, f32[9216]{0:T(1024)}, u32[]{:S(2)}) copy-start(f32[9216]{0:T(1024)} %param.7) | copy-start | bytes 110596
  7.2 49.4 %reduce-scatter.2.cloned.1.call-start = ((), (), s32[]{:S(2)}) async-start(), calls=%async_computation.1 | async-start | bytes 2654208 | tf_op jit(solution)/shard_map/reduce_scatter | solution.py:12
  10.1 78.9 %copy-start.4 = (f32[8]{0:T(128)S(1)}, f32[8]{0:T(128)}, u32[]{:S(2)}) copy-start(f32[8]{0:T(128)} %param.6) | copy-start | bytes 100
  89.0 42.6 %copy-start = (f32[9216]{0:T(1024)}, f32[9216]{0:T(1024)S(1)}, u32[]{:S(2)}) copy-start(f32[9216]{0:T(1024)S(1)} %multiply_add_fusion.1) | copy-start | bytes 110596
  89.0 42.6 %copy-start.3 = (f32[8]{0:T(128)}, f32[8]{0:T(128)S(1)}, u32[]{:S(2)}) copy-start(f32[8]{0:T(128)S(1)} %multiply_add_fusion.2) | copy-start | bytes 100
Sparse Core Ops, SparseCore 0:
  11.4 45.1 reduce-scatter.1
where the time goes:
time: 139 us; the launch traced here: 138 us
  blocking collectives  68.9 us (50%)
  waiting for transfers between devices  45.8 us (33%)
  between operations  15.4 us (11%)
  other arithmetic  8.27 us (6%)
    reduce_scatter x1, waiting for transfers between devices, on_device(): lax.psum_scatter(local_part, ('dp', 'narrow'), scatter_dimension=1, tiled...  45.8 us
    psum x1, blocking collectives, on_device(): update_sum = lax.psum(jnp.sum(scaled * scaled), ('dp', 'wide', 'narrow'))  37.7 us
    psum x1, blocking collectives, on_device(): col_sum = lax.psum(col_part, 'wide')  19.3 us
    psum x1, blocking collectives, on_device(): row_sum = lax.psum(row_part, ('dp', 'narrow'))  11.8 us
    convert_element_type x1, other arithmetic, on_device(): local_part = grad_parts[0].astype(jnp.float32)  2.87 us
  transfers between devices with their start and end apart: 1, of which 1 were waited for; matrix products, arithmetic and copies ran while one was open for 0% of the time, Pallas kernels for 0%

commit v1 on v0

v1 whole, which is shorter than its diff:
```python
import jax
import jax.numpy as jnp
from jax import lax
from jax.experimental import pallas as pl
from jax.experimental.pallas import tpu as pltpu
from jax.sharding import PartitionSpec as P

FF = 73728
STEP = 100
BETA = 1.0 - STEP ** (-0.8)
LANES = 128
VMEM = pl.BlockSpec(memory_space=pltpu.VMEM)
HBM = pl.BlockSpec(memory_space=pltpu.HBM)


def bits_of(size):
    return [1 << b for b in range(size.bit_length() - 1)]


def send_to(x, axes, size, target):
    return lax.ppermute(x, axes, [(i, target(i)) for i in range(size)])


def wide_masks(wide):
    bits = bits_of(wide)
    return [now[:0:-1] + [sum(now)] * (len(now) - 1) + now[:1] for now in (bits[i : i + 2] for i in range(0, len(bits), 2))]


def tree(terms):
    while len(terms) > 1:
        terms = [sum(terms[i : i + 2][1:], terms[i]) for i in range(0, len(terms), 2)]
    return terms[0]


def iota(rows, axis):
    return lax.broadcasted_iota(jnp.int32, (rows, LANES), axis)


def to_lanes(column, first):
    rows = column.shape[0]
    return jnp.sum(jnp.where(iota(rows, 1) == iota(rows, 0) + first, column, 0.0), axis=0, keepdims=True)


def call(kernel, out_shapes, in_specs, *args, out_specs=None, scratch=()):
    return pl.pallas_call(
        kernel,
        out_shape=[jax.ShapeDtypeStruct(shape, jnp.float32) for shape in out_shapes],
        in_specs=in_specs,
        out_specs=out_specs or [VMEM] * len(out_shapes),
        scratch_shapes=scratch,
        compiler_params=pltpu.CompilerParams(vmem_limit_bytes=32 << 20),
    )(*args)


class Blocks:
    def __init__(self, dp, narrow, cols):
        self.narrow, self.cols = narrow, cols
        self.masks = bits_of(dp * narrow)[1:]
        tiles = cols // LANES
        cut = (tiles * 2 + 2) // 3 * LANES
        self.chunks = [(0, cut), (cut, cols - cut)]
        self.keys = [(t, c) for t in range(dp * narrow // 2) for c in range(2)]

    def width(self, key):
        return self.chunks[key[-1]][1]

    def home(self, t):
        steps = len(self.masks)
        return self.side(next((s for s in range(steps) if t >> s & 1), steps))

    def side(self, s):
        return (len(self.masks) - s + 1) & 1

    def mask(self, core, s):
        return self.masks[-1 - s] if core else self.masks[s]

    def target(self, device, s):
        return device ^ self.mask((device ^ self.side(s)) & 1, s) ^ 1

    def start(self, key):
        j, t, c = key
        group = lax.axis_index("dp") * self.narrow + lax.axis_index("narrow")
        group = group ^ j
        reach = [sum(self.mask(core, s) for s in range(len(self.masks)) if t >> s & 1) for core in range(2)]
        block = group ^ jnp.where(group % 2 == 1, reach[1], reach[0])
        return pl.multiple_of(block * self.cols + self.chunks[c][0], LANES)

    def places(self, keys):
        at, out = 0, []
        for key in keys:
            out.append(at)
            at += self.width(key)
        return out, at


def fetch_kernel(blocks, keys, part, out, raw, sem):
    spans = [pl.ds(at, blocks.width(key)) for key, at in zip(keys, blocks.places(keys)[0])]
    copies = [
        pltpu.make_async_copy(part.at[:, pl.ds(blocks.start(key), span.size)], raw.at[:, span], sem.at[i])
        for i, (key, span) in enumerate(zip(keys, spans))
    ]
    for copy in copies:
        copy.start()
    for copy, span in zip(copies, spans):
        copy.wait()
        out[:, span] = raw[:, span].astype(jnp.float32)


def load(blocks, refs, term, width):
    slot, at = term
    if slot == 0:
        return refs[0][:, pl.ds(blocks.start(at), width)].astype(jnp.float32)
    return refs[slot][:, at : at + width]


def merge_kernel(blocks, plan, *refs):
    out = refs[-1]
    at = 0
    for width, terms in plan:
        out[:, at : at + width] = tree([load(blocks, refs, term, width) for term in terms])
        at += width


def grad_kernel(plan_of, blocks, plan, *refs):
    grad_out, *cols_out = refs[plan_of:]
    at = 0
    for width, terms in plan:
        grad = tree([load(blocks, refs, term, width) for term in terms])
        grad_out[:, at : at + width] = grad
        for col_out in cols_out:
            col_out[:, at : at + width] = jnp.sum(grad * grad + 1e-30, axis=0, keepdims=True)
        at += width
    for col_out in cols_out:
        if col_out.shape[1] > at:
            col_out[:, at:] = jnp.zeros((1, col_out.shape[1] - at), jnp.float32)


def square_kernel(grad_in, col_out, row_out):
    square = grad_in[...] * grad_in[...] + 1e-30
    col_out[...] = jnp.sum(square, axis=0, keepdims=True)
    row_out[...] = to_lanes(jnp.sum(square, axis=1, keepdims=True), 0)


def fixed_kernel(weight, row_state, out, line):
    rows = weight.shape[0]
    squares = []
    for at in range(0, weight.shape[1], LANES):
        piece = weight[:, at : at + LANES].astype(jnp.float32)
        squares.append(piece * piece)
    squares = jnp.sum(tree(squares), keepdims=True)
    line[...] = jnp.zeros_like(line)
    line[:, :rows] = row_state[...]
    first = jnp.logical_and(lax.axis_index("dp") == 0, lax.axis_index("narrow") == 0)
    state = jnp.where(first, pltpu.roll(line[...], 2 * rows, 1), 0.0)
    out[...] = jnp.where(iota(1, 1) == 3 * rows, squares, state)


def column_kernel(state, grad_in, row_in, fixed_in, grad_out, message_out):
    rows = grad_in.shape[0]
    grad = grad_in[...] * lax.rsqrt(state[...])
    grad_out[...] = grad
    quot = jnp.sum(grad * grad, axis=1, keepdims=True)
    message = row_in[...] + fixed_in[...] + to_lanes(quot, rows)
    for i in range(message_out.shape[0]):
        message_out[i] = message


def final_kernel(rows_all, sums_in, grad_in, update_out, row_out, update, row_state, sem):
    rows = grad_in.shape[0]
    outer, wide, inner = sums_in.shape[:3]
    layers = [tree([sums_in[o, z, i] for o in range(outer) for i in range(inner)]) for z in range(wide)]
    total = jnp.concatenate(layers, axis=0)
    lane = iota(wide, 1)
    state = pltpu.roll(total, LANES - 2 * rows, 1)
    quot = pltpu.roll(total, LANES - rows, 1)
    new = jnp.where(lane < rows, BETA * state + (1.0 - BETA) * (total / FF), 1.0)
    update_sum = jnp.sum(jnp.where(lane < rows, quot / new, 0.0), keepdims=True)
    weight_sum = jnp.sum(jnp.where(lane == 3 * rows, total, 0.0), keepdims=True)
    clip = jnp.maximum(1.0, jnp.sqrt(update_sum / (rows_all * FF)))
    weight_rms = jnp.maximum(0.001, jnp.sqrt(weight_sum / (rows_all * FF)))
    own = jnp.sum(jnp.where(iota(wide, 0) == lax.axis_index("wide"), new, 0.0), axis=0, keepdims=True)
    row_state[...] = own[:, :rows]
    copies = [pltpu.make_async_copy(row_state, row_out, sem.at[0]), pltpu.make_async_copy(update, update_out, sem.at[1])]
    copies[0].start()
    column = jnp.sum(jnp.where(iota(rows, 1) == iota(rows, 0), own, 0.0), axis=1, keepdims=True)
    update[...] = grad_in[...] * (lax.rsqrt(column) * (weight_rms / clip))
    copies[1].start()
    for copy in copies:
        copy.wait()


def on_device(dp, wide, narrow, grad_parts, weight, row_state, col_state):
    part = grad_parts[0]
    rows, cols = weight.shape
    rows_all = rows * wide
    blocks = Blocks(dp, narrow, cols)
    group_axes = ("dp", "narrow")
    size = dp * narrow
    arrays = [part]
    held = {(t, c): [(0, (blocks.home(t), t, c))] for t, c in blocks.keys}

    def merge(kernel, widths, sums, shapes):
        used = [0] + sorted({slot for terms in sums for slot, _ in terms} - {0}, reverse=True)
        plan = [(width, [(used.index(slot), at) for slot, at in terms]) for width, terms in zip(widths, sums)]
        return call(lambda *refs: kernel(blocks, plan, *refs), shapes, [VMEM] * len(used), *[arrays[u] for u in used])

    def pack(keys, sums):
        return merge(merge_kernel, [blocks.width(key) for key in keys], sums, [(rows, blocks.places(keys)[1])])[0]

    def fetch(keys):
        shape = (rows, blocks.places(keys)[1])
        return call(
            lambda *refs: fetch_kernel(blocks, keys, *refs),
            [shape],
            [HBM],
            pltpu.with_memory_space_constraint(part, pltpu.HBM),
            scratch=[pltpu.VMEM(shape, part.dtype), pltpu.SemaphoreType.DMA((len(keys),))],
        )[0]

    def receive(keys, send, target):
        arrays.append(send_to(send, group_axes, size, target))
        return [(key, (len(arrays) - 1, at)) for key, at in zip(keys, blocks.places(keys)[0])]

    def other(device):
        return device ^ 1

    groups = (
        [key for key in held if key[1] == 0 and key[0] & 1],
        [key for key in held if key[1] == 1],
        [key for key in held if key[1] == 0 and not key[0] & 1],
    )
    for i, keys in enumerate(groups):
        given = [(1 ^ blocks.home(t), t, c) for t, c in keys]
        send = pack(keys, [[(0, key)] for key in given]) if i else fetch(given)
        for key, term in receive(keys, send, other):
            held[key].append(term)
    for s in range(len(blocks.masks)):
        for c in range(2):
            keys = [key for key in held if key[0] >> s & 1 and key[1] == c]
            got = receive(keys, pack(keys, [held.pop(key) for key in keys]), lambda i: blocks.target(i, s))
            got = [((t ^ 1 << s, c), term) for (t, c), term in got]
            away = [(key, term) for key, term in got if blocks.home(key[0]) != blocks.side(s + 1)]
            if away:
                keys = [key for key, _ in away]
                got = [pair for pair in got if pair not in away]
                got += receive(keys, pack(keys, [[term] for _, term in away]), other)
            for key, term in got:
                held[key].append(term)
    left = sorted(held)
    first, *rounds = wide_masks(wide)
    inputs = 1 + len({slot for key in left for slot, _ in held[key]} - {0})
    grad, *sends = merge(
        lambda *refs: grad_kernel(inputs, *refs),
        [blocks.width(key) for key in left],
        [held[key] for key in left],
        [(rows, cols)] + [(1, cols + LANES * (len(first) - 1 - i)) for i in range(len(first))],
    )

    def send_wide(x, mask):
        return send_to(x, ("wide", "narrow"), wide * narrow, lambda i: i ^ mask)

    terms = [send_wide(x, mask * narrow ^ 1)[:, :cols] for x, mask in zip(sends, first)]
    grad = send_to(grad, group_axes, size, other)
    col_sum, row_part = call(square_kernel, [(1, cols), (1, LANES)], [VMEM], grad)
    col_sum = tree(terms + [col_sum])
    for masks in rounds:
        col_sum = tree([send_wide(col_sum, mask * narrow) for mask in masks] + [col_sum])
    new_col_state = BETA * col_state[None] + (1.0 - BETA) * (col_sum / rows_all)
    fixed = call(
        fixed_kernel,
        [(1, LANES)],
        [VMEM] * 2,
        weight, row_state[None],
        scratch=[pltpu.VMEM((1, LANES), jnp.float32)],
    )[0]

    single = dp * wide * narrow <= 64
    group = dp * narrow * (wide if single else 1)
    grad, message = call(
        column_kernel,
        [(rows, cols), (group, 1, LANES)],
        [VMEM] * 4,
        new_col_state, grad, row_part, fixed,
    )
    if single:
        sums = lax.all_to_all(message, ("dp", "wide", "narrow"), 0, 0)
        sums = sums.reshape(dp, wide, narrow, 1, LANES)
    else:
        sums = jnp.sum(lax.all_to_all(message, ("dp", "narrow"), 0, 0), axis=0)
        sums = lax.all_to_all(jnp.broadcast_to(sums, (wide, 1, LANES)), "wide", 0, 0)
        sums = sums.reshape(1, wide, 1, 1, LANES)
    update, new_row_state = call(
        lambda *refs: final_kernel(rows_all, *refs),
        [(rows, cols), (1, rows)],
        [VMEM] * 2,
        sums, grad,
        out_specs=[HBM] * 2,
        scratch=[pltpu.VMEM((rows, cols), jnp.float32), pltpu.VMEM((1, rows), jnp.float32), pltpu.SemaphoreType.DMA((2,))],
    )
    return (update, new_row_state[0], new_col_state[0])


def solution(mesh):
    dp, wide, narrow = (mesh.shape[axis] for axis in ("dp", "wide", "narrow"))

    def body(*args):
        return on_device(dp, wide, narrow, *args)

    return jax.shard_map(
        body,
        mesh=mesh,
        in_specs=(
            P(("dp", "narrow"), "wide", None),
            P("wide", ("dp", "narrow")),
            P("wide"),
            P(("dp", "narrow")),
        ),
        out_specs=(P("wide", ("dp", "narrow")), P("wide"), P(("dp", "narrow"))),
        check_vma=False,
    )
```

time: 139 us -> 40.4 us (0.29)
  blocking collectives: 68.9 us -> 12.2 us
  waiting for transfers between devices: 45.8 us -> 9.91 us
  between operations: 15.4 us -> 0.77 us
  starting transfers between devices: 0.04 us -> 14.2 us
  other arithmetic: 8.27 us -> 0.1 us
  Pallas kernels: 0 us -> 3.02 us
    psum x3 -> x0, blocking collectives: 68.9 us -> none  [the longest x1 37.7 us: on_device(): update_sum = lax.psum(jnp.sum(scaled * scaled), ('dp', 'wide', 'narrow'))]
    reduce_scatter x1 -> x0, waiting for transfers between devices: 45.8 us -> none  [on_device(): lax.psum_scatter(local_part, ('dp', 'narrow'), scatter_dimension=1, tiled...]
    ppermute x0 -> x13, starting transfers between devices: none -> 14.2 us  [send_to(): return lax.ppermute(x, axes, [(i, target(i)) for i in range(size)])]
    all_to_all x0 -> x1, blocking collectives: none -> 12.2 us  [on_device(): sums = lax.all_to_all(message, ('dp', 'wide', 'narrow'), 0, 0)]
    ppermute x0 -> x13, waiting for transfers between devices: none -> 9.91 us  [send_to(): return lax.ppermute(x, axes, [(i, target(i)) for i in range(size)])]
    reduce_sum x3 -> x0, other arithmetic: 3.59 us -> none  [the longest x1 1.72 us: on_device(): update_sum = lax.psum(jnp.sum(scaled * scaled), ('dp', 'wide', 'narrow'))]
    pallas_call x0 -> x14, Pallas kernels: none -> 3.02 us  [call(): pl.pallas_call(kernel, out_shape=[jax.ShapeDtypeStruct(shape, jnp.float32...]
    convert_element_type x1 -> x0, other arithmetic: 2.87 us -> none  [on_device(): local_part = grad_parts[0].astype(jnp.float32)]
  transfers between devices with their start and end apart: 1 -> 13, of which waited for: 1 -> 4; matrix products, arithmetic and copies ran while one was open for 0% -> 0% of each run, Pallas kernels for 0% -> 2%
where the time goes in v1:
time: 40.4 us; the launch traced here: 40.2 us
  starting transfers between devices  14.2 us (35%)
  blocking collectives  12.2 us (30%)
  waiting for transfers between devices  9.91 us (25%)
  Pallas kernels  3.02 us (7%)
  between operations  0.77 us (2%)
    ppermute x13, starting transfers between devices, send_to(): return lax.ppermute(x, axes, [(i, target(i)) for i in range(size)])  14.2 us
    all_to_all x1, blocking collectives, on_device(): sums = lax.all_to_all(message, ('dp', 'wide', 'narrow'), 0, 0)  12.2 us
    ppermute x13, waiting for transfers between devices, send_to(): return lax.ppermute(x, axes, [(i, target(i)) for i in range(size)])  9.91 us
    pallas_call x14, Pallas kernels, call(): pl.pallas_call(kernel, out_shape=[jax.ShapeDtypeStruct(shape, jnp.float32...  3.02 us
  transfers between devices with their start and end apart: 13, of which 4 were waited for; matrix products, arithmetic and copies ran while one was open for 0% of the time, Pallas kernels for 2%

profile of v1, /device:TPU:0, one launch (start us, length us, event | category | flops | bytes accessed | tf_op | source)
XLA Modules:
  0.0 40.2 jit_solution(6317273225737345880)
XLA Ops:
  0.6 1.1 %shard_map.70 = f32[8,12288]{1,0:T(8,128)S(1)} custom-call(bf16[8,73728]{1,0:T(8,128)(2,1)} %bitcast.6), custom_call_target="tpu_custom_call" | custom-call | tf_op jit(solution)/shard_map/pallas_call | solution.py:45
  1.7 0.5 %collective-permute-start.3 = (f32[8,12288]{1,0:T(8,128)S(1)}, f32[8,12288]{1,0:T(8,128)S(1)}, u32[]{:S(2)}, u32[]{:S(2)}) collective-permute-start(f32[8,12288]{1,0:T(8,128)S(1)} %shard_map.70), channel_id=1, source_target_pairs={{0,1},{1,0},{8,9},{9,8},{16,17},{17,16},{24,25},{25,24},{2,3},{3,2... | collective-permute-start | bytes 1179656 | tf_op jit(solution)/shard_map/ppermute | solution.py:21
  2.3 0.3 collective-permute-start
  2.6 0.4 collective-permute-start.5
  3.0 0.6 %collective-permute-done.3.refs_1_ = f32[8,12288]{1,0:T(8,128)S(1)} collective-permute-done((f32[8,12288]{1,0:T(8,128)S(1)}, f32[8,12288]{1,0:T(8,128)S(1)}, u32[]{:S(2)}, u32[]{:S(2)}) %collective-permute-start.3) | collective-permute-done | bytes 393248 | tf_op jit(solution)/shard_map/ppermute | solution.py:21
  3.6 2.7 %collective-permute-start.4 = (f32[8,12288]{1,0:T(8,128)S(1)}, f32[8,12288]{1,0:T(8,128)S(1)}, u32[]{:S(2)}, u32[]{:S(2)}) collective-permute-start(f32[8,12288]{1,0:T(8,128)S(1)} %shard_map.71), channel_id=1, source_target_pairs={{0,17},{1,8},{8,25},{9,0},{16,1},{17,24},{24,9},{25,16},{2,19},{3,... | collective-permute-start | bytes 1179656 | tf_op jit(solution)/shard_map/ppermute | solution.py:21
  6.3 0.0 collective-permute-done.refs_1_.refs_2_.refs_6_
  6.3 1.5 %collective-permute-start.1 = (f32[8,6144]{1,0:T(8,128)S(1)}, f32[8,6144]{1,0:T(8,128)S(1)}, u32[]{:S(2)}, u32[]{:S(2)}) collective-permute-start(f32[8,6144]{1,0:T(8,128)S(1)} %shard_map.68), channel_id=1, source_target_pairs={{0,17},{1,8},{8,25},{9,0},{16,1},{17,24},{24,9},{25,16},{2,19},{3,... | collective-permute-start | bytes 589832 | tf_op jit(solution)/shard_map/ppermute | solution.py:21
  7.9 0.0 collective-permute-done.5.refs_2_.refs_5_
  7.9 3.9 %collective-permute-done.4.refs_1_ = f32[8,12288]{1,0:T(8,128)S(1)} collective-permute-done((f32[8,12288]{1,0:T(8,128)S(1)}, f32[8,12288]{1,0:T(8,128)S(1)}, u32[]{:S(2)}, u32[]{:S(2)}) %collective-permute-start.4) | collective-permute-done | bytes 393248 | tf_op jit(solution)/shard_map/ppermute | solution.py:21
  11.8 2.1 %collective-permute-start.6 = (f32[8,6144]{1,0:T(8,128)S(1)}, f32[8,6144]{1,0:T(8,128)S(1)}, u32[]{:S(2)}, u32[]{:S(2)}) collective-permute-start(f32[8,6144]{1,0:T(8,128)S(1)} %shard_map.73), channel_id=1, source_target_pairs={{0,17},{1,8},{8,25},{9,0},{16,1},{17,24},{24,9},{25,16},{2,19},{3,... | collective-permute-start | bytes 589832 | tf_op jit(solution)/shard_map/ppermute | solution.py:21
  13.9 0.1 collective-permute-start.8
  14.0 0.0 collective-permute-done.1.refs_1_
  14.1 1.6 %collective-permute-start.2 = (f32[8,3072]{1,0:T(8,128)S(1)}, f32[8,3072]{1,0:T(8,128)S(1)}, u32[]{:S(2)}, u32[]{:S(2)}) collective-permute-start(f32[8,3072]{1,0:T(8,128)S(1)} %shard_map.69), channel_id=1, source_target_pairs={{0,17},{1,8},{8,25},{9,0},{16,1},{17,24},{24,9},{25,16},{2,19},{3,... | collective-permute-start | bytes 294920 | tf_op jit(solution)/shard_map/ppermute | solution.py:21
  15.7 0.0 copy-start.1
  15.7 0.0 copy-start.3
  15.7 0.4 %collective-permute-start.7 = (f32[8,3072]{1,0:T(8,128)S(1)}, f32[8,3072]{1,0:T(8,128)S(1)}, u32[]{:S(2)}, u32[]{:S(2)}) collective-permute-start(f32[8,3072]{1,0:T(8,128)S(1)} %shard_map.74), channel_id=1, source_target_pairs={{0,1},{1,0},{8,9},{9,8},{16,17},{17,16},{24,25},{25,24},{2,3},{3,2... | collective-permute-start | bytes 294920 | tf_op jit(solution)/shard_map/ppermute | solution.py:21
  16.2 2.1 %collective-permute-done.2.refs_1_ = f32[8,3072]{1,0:T(8,128)S(1)} collective-permute-done((f32[8,3072]{1,0:T(8,128)S(1)}, f32[8,3072]{1,0:T(8,128)S(1)}, u32[]{:S(2)}, u32[]{:S(2)}) %collective-permute-start.2) | collective-permute-done | bytes 98336 | tf_op jit(solution)/shard_map/ppermute | solution.py:21
  18.3 0.2 shard_map.76
  18.5 0.5 %collective-permute-start.12 = (f32[8,9216]{1,0:T(8,128)S(1)}, f32[8,9216]{1,0:T(8,128)S(1)}, u32[]{:S(2)}, u32[]{:S(2)}) collective-permute-start(f32[8,9216]{1,0:T(8,128)S(1)} %get-tuple-element.16), channel_id=1, source_target_pairs={{0,1},{1,0},{8,9},{9,8},{16,17},{17,16},{24,25},{25,24},{2,3},{3,2... | collective-permute-start | bytes 884744 | tf_op jit(solution)/shard_map/ppermute | solution.py:21
  18.9 2.5 %collective-permute-start.9 = (f32[1,9472]{1,0:T(1,128)S(1)}, f32[1,9472]{1,0:T(1,128)S(1)}, u32[]{:S(2)}, u32[]{:S(2)}) collective-permute-start(f32[1,9472]{1,0:T(1,128)S(1)} %get-tuple-element.13), channel_id=1, source_target_pairs={{0,5},{1,4},{2,7},{3,6},{4,1},{5,0},{6,3},{7,2},{8,13},{9,12},{10,... | collective-permute-start | bytes 113672 | tf_op jit(solution)/shard_map/ppermute | solution.py:21
  21.4 1.4 %collective-permute-start.10 = (f32[1,9344]{1,0:T(1,128)S(1)}, f32[1,9344]{1,0:T(1,128)S(1)}, u32[]{:S(2)}, u32[]{:S(2)}) collective-permute-start(f32[1,9344]{1,0:T(1,128)S(1)} %get-tuple-element.14), channel_id=1, source_target_pairs={{0,7},{1,6},{2,5},{3,4},{4,3},{5,2},{6,1},{7,0},{8,15},{9,14},{10,... | collective-permute-start | bytes 112136 | tf_op jit(solution)/shard_map/ppermute | solution.py:21
  22.8 0.2 collective-permute-start.11
  23.1 0.2 shard_map.78.fixed_in
  23.3 0.3 shard_map.77
  23.5 3.2 %collective-permute-done.11 = f32[1,9216]{1,0:T(1,128)S(1)} collective-permute-done((f32[1,9216]{1,0:T(1,128)S(1)}, f32[1,9216]{1,0:T(1,128)S(1)}, u32[]{:S(2)}, u32[]{:S(2)}) %collective-permute-start.11) | collective-permute-done | bytes 36896 | tf_op jit(solution)/shard_map/ppermute | solution.py:21
  26.7 0.0 collective-permute-done.10
  26.8 0.1 multiply_add_fusion.state
  26.9 0.0 copy-start.2
  26.9 0.2 shard_map.79
  27.1 12.2 %all_to_all.5 = f32[32,1,128]{2,1,0:T(1,128)S(1)} all-to-all(f32[32,1,128]{2,1,0:T(1,128)S(1)} %get-tuple-element.19), channel_id=1, replica_groups=mesh['dp'=4,'wide'=4,'narrow'=2] {'dp','wide','narrow'}, dimensions={0} | all-to-all | bytes 32768 | tf_op jit(solution)/shard_map/all_to_all | solution.py:286
  39.3 1.0 %shard_map.80 = (f32[8,9216]{1,0:T(8,128)}, f32[1,8]{1,0:T(1,128)}) custom-call(f32[4,4,2,1,128]{4,3,2,1,0:T(1,128)S(1)} %bitcast.17, f32[8,9216]{1,0:T(8,128)S(1)} %get-tuple-element.20.refs_1_), custom_call_target="tpu_custom_call" | custom-call | tf_op jit(solution)/shard_map/pallas_call | solution.py:45
  (21 shorter events, 0.2 us)
Async XLA Ops:
  0.6 1.6 %copy-start = (bf16[1,8,73728]{2,1,0:T(8,128)(2,1)S(1)}, bf16[1,8,73728]{2,1,0:T(8,128)(2,1)}, u32[]{:S(2)}) copy-start(bf16[1,8,73728]{2,1,0:T(8,128)(2,1)} %param.4) | copy-start | bytes 3538948
  1.7 1.9 %collective-permute-start.3 = (f32[8,12288]{1,0:T(8,128)S(1)}, f32[8,12288]{1,0:T(8,128)S(1)}, u32[]{:S(2)}, u32[]{:S(2)}) collective-permute-start(f32[8,12288]{1,0:T(8,128)S(1)} %shard_map.70), channel_id=1, source_target_pairs={{0,1},{1,0},{8,9},{9,8},{16,17},{17,16},{24,25},{25,24},{2,3},{3,2... | collective-permute-start | bytes 1179656 | tf_op jit(solution)/shard_map/ppermute | solution.py:21
  2.3 4.0 %collective-permute-start = (f32[8,12288]{1,0:T(8,128)S(1)}, f32[8,12288]{1,0:T(8,128)S(1)}, u32[]{:S(2)}, u32[]{:S(2)}) collective-permute-start(f32[8,12288]{1,0:T(8,128)S(1)} %shard_map.67), channel_id=1, source_target_pairs={{0,1},{1,0},{8,9},{9,8},{16,17},{17,16},{24,25},{25,24},{2,3},{3,2... | collective-permute-start | bytes 1179656 | tf_op jit(solution)/shard_map/ppermute | solution.py:21
  2.6 5.3 %collective-permute-start.5 = (f32[8,12288]{1,0:T(8,128)S(1)}, f32[8,12288]{1,0:T(8,128)S(1)}, u32[]{:S(2)}, u32[]{:S(2)}) collective-permute-start(f32[8,12288]{1,0:T(8,128)S(1)} %shard_map.72), channel_id=1, source_target_pairs={{0,1},{1,0},{8,9},{9,8},{16,17},{17,16},{24,25},{25,24},{2,3},{3,2... | collective-permute-start | bytes 1179656 | tf_op jit(solution)/shard_map/ppermute | solution.py:21
  3.6 8.1 %collective-permute-start.4 = (f32[8,12288]{1,0:T(8,128)S(1)}, f32[8,12288]{1,0:T(8,128)S(1)}, u32[]{:S(2)}, u32[]{:S(2)}) collective-permute-start(f32[8,12288]{1,0:T(8,128)S(1)} %shard_map.71), channel_id=1, source_target_pairs={{0,17},{1,8},{8,25},{9,0},{16,1},{17,24},{24,9},{25,16},{2,19},{3,... | collective-permute-start | bytes 1179656 | tf_op jit(solution)/shard_map/ppermute | solution.py:21
  6.3 7.7 %collective-permute-start.1 = (f32[8,6144]{1,0:T(8,128)S(1)}, f32[8,6144]{1,0:T(8,128)S(1)}, u32[]{:S(2)}, u32[]{:S(2)}) collective-permute-start(f32[8,6144]{1,0:T(8,128)S(1)} %shard_map.68), channel_id=1, source_target_pairs={{0,17},{1,8},{8,25},{9,0},{16,1},{17,24},{24,9},{25,16},{2,19},{3,... | collective-permute-start | bytes 589832 | tf_op jit(solution)/shard_map/ppermute | solution.py:21
  11.8 6.5 %collective-permute-start.6 = (f32[8,6144]{1,0:T(8,128)S(1)}, f32[8,6144]{1,0:T(8,128)S(1)}, u32[]{:S(2)}, u32[]{:S(2)}) collective-permute-start(f32[8,6144]{1,0:T(8,128)S(1)} %shard_map.73), channel_id=1, source_target_pairs={{0,17},{1,8},{8,25},{9,0},{16,1},{17,24},{24,9},{25,16},{2,19},{3,... | collective-permute-start | bytes 589832 | tf_op jit(solution)/shard_map/ppermute | solution.py:21
  13.9 4.4 %collective-permute-start.8 = (f32[8,6144]{1,0:T(8,128)S(1)}, f32[8,6144]{1,0:T(8,128)S(1)}, u32[]{:S(2)}, u32[]{:S(2)}) collective-permute-start(f32[8,6144]{1,0:T(8,128)S(1)} %shard_map.75), channel_id=1, source_target_pairs={{0,1},{1,0},{8,9},{9,8},{16,17},{17,16},{24,25},{25,24},{2,3},{3,2... | collective-permute-start | bytes 589832 | tf_op jit(solution)/shard_map/ppermute | solution.py:21
  14.1 4.2 %collective-permute-start.2 = (f32[8,3072]{1,0:T(8,128)S(1)}, f32[8,3072]{1,0:T(8,128)S(1)}, u32[]{:S(2)}, u32[]{:S(2)}) collective-permute-start(f32[8,3072]{1,0:T(8,128)S(1)} %shard_map.69), channel_id=1, source_target_pairs={{0,17},{1,8},{8,25},{9,0},{16,1},{17,24},{24,9},{25,16},{2,19},{3,... | collective-permute-start | bytes 294920 | tf_op jit(solution)/shard_map/ppermute | solution.py:21
  15.7 7.4 %copy-start.4 = (f32[9216]{0:T(1024)S(1)}, f32[9216]{0:T(1024)}, u32[]{:S(2)}) copy-start(f32[9216]{0:T(1024)} %param.7) | copy-start | bytes 110596
  15.7 7.4 %copy-start.1 = (bf16[8,9216]{1,0:T(8,128)(2,1)S(1)}, bf16[8,9216]{1,0:T(8,128)(2,1)}, u32[]{:S(2)}) copy-start(bf16[8,9216]{1,0:T(8,128)(2,1)} %weight.1) | copy-start | bytes 442372
  15.7 7.4 %copy-start.3 = (f32[8]{0:T(128)S(1)}, f32[8]{0:T(128)}, u32[]{:S(2)}) copy-start(f32[8]{0:T(128)} %param.6) | copy-start | bytes 100
  15.7 2.5 %collective-permute-start.7 = (f32[8,3072]{1,0:T(8,128)S(1)}, f32[8,3072]{1,0:T(8,128)S(1)}, u32[]{:S(2)}, u32[]{:S(2)}) collective-permute-start(f32[8,3072]{1,0:T(8,128)S(1)} %shard_map.74), channel_id=1, source_target_pairs={{0,1},{1,0},{8,9},{9,8},{16,17},{17,16},{24,25},{25,24},{2,3},{3,2... | collective-permute-start | bytes 294920 | tf_op jit(solution)/shard_map/ppermute | solution.py:21
  18.5 4.8 %collective-permute-start.12 = (f32[8,9216]{1,0:T(8,128)S(1)}, f32[8,9216]{1,0:T(8,128)S(1)}, u32[]{:S(2)}, u32[]{:S(2)}) collective-permute-start(f32[8,9216]{1,0:T(8,128)S(1)} %get-tuple-element.16), channel_id=1, source_target_pairs={{0,1},{1,0},{8,9},{9,8},{16,17},{17,16},{24,25},{25,24},{2,3},{3,2... | collective-permute-start | bytes 884744 | tf_op jit(solution)/shard_map/ppermute | solution.py:21
  18.9 7.8 %collective-permute-start.9 = (f32[1,9472]{1,0:T(1,128)S(1)}, f32[1,9472]{1,0:T(1,128)S(1)}, u32[]{:S(2)}, u32[]{:S(2)}) collective-permute-start(f32[1,9472]{1,0:T(1,128)S(1)} %get-tuple-element.13), channel_id=1, source_target_pairs={{0,5},{1,4},{2,7},{3,6},{4,1},{5,0},{6,3},{7,2},{8,13},{9,12},{10,... | collective-permute-start | bytes 113672 | tf_op jit(solution)/shard_map/ppermute | solution.py:21
  21.4 5.3 %collective-permute-start.10 = (f32[1,9344]{1,0:T(1,128)S(1)}, f32[1,9344]{1,0:T(1,128)S(1)}, u32[]{:S(2)}, u32[]{:S(2)}) collective-permute-start(f32[1,9344]{1,0:T(1,128)S(1)} %get-tuple-element.14), channel_id=1, source_target_pairs={{0,7},{1,6},{2,5},{3,4},{4,3},{5,2},{6,1},{7,0},{8,15},{9,14},{10,... | collective-permute-start | bytes 112136 | tf_op jit(solution)/shard_map/ppermute | solution.py:21
  22.8 3.9 %collective-permute-start.11 = (f32[1,9216]{1,0:T(1,128)S(1)}, f32[1,9216]{1,0:T(1,128)S(1)}, u32[]{:S(2)}, u32[]{:S(2)}) collective-permute-start(f32[1,9216]{1,0:T(1,128)S(1)} %get-tuple-element.15), channel_id=1, source_target_pairs={{0,3},{1,2},{2,1},{3,0},{4,7},{5,6},{6,5},{7,4},{8,11},{9,10},{10,... | collective-permute-start | bytes 110600 | tf_op jit(solution)/shard_map/ppermute | solution.py:21
  26.9 13.4 %copy-start.2 = (f32[1,9216]{1,0:T(1,128)}, f32[1,9216]{1,0:T(1,128)S(1)}, u32[]{:S(2)}) copy-start(f32[1,9216]{1,0:T(1,128)S(1)} %multiply_add_fusion.state) | copy-start | bytes 110596

commit v2 on v1

--- a/solution.py
+++ b/solution.py
@@ -9,6 +9,7 @@
 STEP = 100
 BETA = 1.0 - STEP ** (-0.8)
 LANES = 128
+PIECES = 2
 VMEM = pl.BlockSpec(memory_space=pltpu.VMEM)
 HBM = pl.BlockSpec(memory_space=pltpu.HBM)
 
@@ -23,7 +24,7 @@
 
 def wide_masks(wide):
     bits = bits_of(wide)
-    return [now[:0:-1] + [sum(now)] * (len(now) - 1) + now[:1] for now in (bits[i : i + 2] for i in range(0, len(bits), 2))]
+    return [[sum(now)] * (len(now) - 1) + now[::-1] for now in (bits[i : i + 2] for i in range(0, len(bits), 2))]
 
 
 def tree(terms):
@@ -41,12 +42,12 @@
     return jnp.sum(jnp.where(iota(rows, 1) == iota(rows, 0) + first, column, 0.0), axis=0, keepdims=True)
 
 
-def call(kernel, out_shapes, in_specs, *args, out_specs=None, scratch=()):
+def call(kernel, out_shapes, in_specs, *args, scratch=()):
     return pl.pallas_call(
         kernel,
         out_shape=[jax.ShapeDtypeStruct(shape, jnp.float32) for shape in out_shapes],
         in_specs=in_specs,
-        out_specs=out_specs or [VMEM] * len(out_shapes),
+        out_specs=[VMEM] * len(out_shapes),
         scratch_shapes=scratch,
         compiler_params=pltpu.CompilerParams(vmem_limit_bytes=32 << 20),
     )(*args)
@@ -94,11 +95,14 @@
 
 
 def fetch_kernel(blocks, keys, part, out, raw, sem):
-    spans = [pl.ds(at, blocks.width(key)) for key, at in zip(keys, blocks.places(keys)[0])]
-    copies = [
-        pltpu.make_async_copy(part.at[:, pl.ds(blocks.start(key), span.size)], raw.at[:, span], sem.at[i])
-        for i, (key, span) in enumerate(zip(keys, spans))
-    ]
+    spans, copies = [], []
+    for key, at in zip(keys, blocks.places(keys)[0]):
+        start, tiles = blocks.start(key), blocks.width(key) // LANES
+        cuts = [tiles * i // PIECES * LANES for i in range(PIECES + 1)]
+        for a, b in zip(cuts, cuts[1:]):
+            spans.append(pl.ds(at + a, b - a))
+            source = part.at[:, pl.ds(pl.multiple_of(start + a, LANES), b - a)]
+            copies.append(pltpu.make_async_copy(source, raw.at[:, spans[-1]], sem.at[len(copies)]))
     for copy in copies:
         copy.start()
     for copy, span in zip(copies, spans):
@@ -161,32 +165,27 @@
     grad_out[...] = grad
     quot = jnp.sum(grad * grad, axis=1, keepdims=True)
     message = row_in[...] + fixed_in[...] + to_lanes(quot, rows)
-    for i in range(message_out.shape[0]):
-        message_out[i] = message
-
-
-def final_kernel(rows_all, sums_in, grad_in, update_out, row_out, update, row_state, sem):
+    message_out[...] = jnp.broadcast_to(message, message_out.shape)
+
+
+def final_kernel(rows_all, wide, inner, sums_in, grad_in, update_out, row_out):
     rows = grad_in.shape[0]
-    outer, wide, inner = sums_in.shape[:3]
-    layers = [tree([sums_in[o, z, i] for o in range(outer) for i in range(inner)]) for z in range(wide)]
-    total = jnp.concatenate(layers, axis=0)
-    lane = iota(wide, 1)
+    count = wide * inner
+    total = tree([sums_in[i : i + count] for i in range(0, sums_in.shape[0], count)])
+    total = tree([pltpu.roll(total, count - k, 0) if k else total for k in range(inner)])
+    lane, layer = iota(count, 1), iota(count, 0)
+    valid = jnp.logical_and(lane < rows, layer % inner == 0)
     state = pltpu.roll(total, LANES - 2 * rows, 1)
     quot = pltpu.roll(total, LANES - rows, 1)
-    new = jnp.where(lane < rows, BETA * state + (1.0 - BETA) * (total / FF), 1.0)
-    update_sum = jnp.sum(jnp.where(lane < rows, quot / new, 0.0), keepdims=True)
-    weight_sum = jnp.sum(jnp.where(lane == 3 * rows, total, 0.0), keepdims=True)
+    new = jnp.where(valid, BETA * state + (1.0 - BETA) * (total / FF), 1.0)
+    update_sum = jnp.sum(jnp.where(valid, quot / new, 0.0), keepdims=True)
+    weight_sum = jnp.sum(jnp.where(jnp.logical_and(lane == 3 * rows, layer % inner == 0), total, 0.0), keepdims=True)
     clip = jnp.maximum(1.0, jnp.sqrt(update_sum / (rows_all * FF)))
     weight_rms = jnp.maximum(0.001, jnp.sqrt(weight_sum / (rows_all * FF)))
-    own = jnp.sum(jnp.where(iota(wide, 0) == lax.axis_index("wide"), new, 0.0), axis=0, keepdims=True)
-    row_state[...] = own[:, :rows]
-    copies = [pltpu.make_async_copy(row_state, row_out, sem.at[0]), pltpu.make_async_copy(update, update_out, sem.at[1])]
-    copies[0].start()
+    own = jnp.sum(jnp.where(layer == lax.axis_index("wide") * inner, new, 0.0), axis=0, keepdims=True)
+    row_out[...] = own[:, :rows]
     column = jnp.sum(jnp.where(iota(rows, 1) == iota(rows, 0), own, 0.0), axis=1, keepdims=True)
-    update[...] = grad_in[...] * (lax.rsqrt(column) * (weight_rms / clip))
-    copies[1].start()
-    for copy in copies:
-        copy.wait()
+    update_out[...] = grad_in[...] * (lax.rsqrt(column) * (weight_rms / clip))
 
 
 def on_device(dp, wide, narrow, grad_parts, weight, row_state, col_state):
@@ -214,7 +213,7 @@
             [shape],
             [HBM],
             pltpu.with_memory_space_constraint(part, pltpu.HBM),
-            scratch=[pltpu.VMEM(shape, part.dtype), pltpu.SemaphoreType.DMA((len(keys),))],
+            scratch=[pltpu.VMEM(shape, part.dtype), pltpu.SemaphoreType.DMA((PIECES * len(keys),))],
         )[0]
 
     def receive(keys, send, target):
@@ -278,24 +277,20 @@
     group = dp * narrow * (wide if single else 1)
     grad, message = call(
         column_kernel,
-        [(rows, cols), (group, 1, LANES)],
+        [(rows, cols), (group, LANES)],
         [VMEM] * 4,
         new_col_state, grad, row_part, fixed,
     )
     if single:
-        sums = lax.all_to_all(message, ("dp", "wide", "narrow"), 0, 0)
-        sums = sums.reshape(dp, wide, narrow, 1, LANES)
+        sums = lax.all_to_all(message, ("dp", "wide", "narrow"), 0, 0, tiled=True)
     else:
-        sums = jnp.sum(lax.all_to_all(message, ("dp", "narrow"), 0, 0), axis=0)
-        sums = lax.all_to_all(jnp.broadcast_to(sums, (wide, 1, LANES)), "wide", 0, 0)
-        sums = sums.reshape(1, wide, 1, 1, LANES)
+        sums = jnp.sum(lax.all_to_all(message, ("dp", "narrow"), 0, 0, tiled=True), axis=0, keepdims=True)
+        sums = lax.all_to_all(jnp.broadcast_to(sums, (wide, LANES)), "wide", 0, 0, tiled=True)
     update, new_row_state = call(
-        lambda *refs: final_kernel(rows_all, *refs),
+        lambda *refs: final_kernel(rows_all, wide, narrow if single else 1, *refs),
         [(rows, cols), (1, rows)],
         [VMEM] * 2,
         sums, grad,
-        out_specs=[HBM] * 2,
-        scratch=[pltpu.VMEM((rows, cols), jnp.float32), pltpu.VMEM((1, rows), jnp.float32), pltpu.SemaphoreType.DMA((2,))],
     )
     return (update, new_row_state[0], new_col_state[0])
 

time: 40.4 us -> 39.6 us (0.980)
  blocking collectives: 12.2 us -> 11.4 us
    all_to_all x1, blocking collectives: 12.2 us -> 11.4 us  [on_device(): sums = lax.all_to_all(message, ('dp', 'wide', 'narrow'), 0, 0, tiled=True)]
  transfers between devices with their start and end apart: 13 -> 13, of which waited for: 4 -> 5; matrix products, arithmetic and copies ran while one was open for 0% -> 0% of each run, Pallas kernels for 2% -> 2%
where the time goes in v2:
time: 39.6 us; the launch traced here: 39.4 us
  starting transfers between devices  14.2 us (36%)
  blocking collectives  11.4 us (29%)
  waiting for transfers between devices  10 us (25%)
  Pallas kernels  2.93 us (7%)
  between operations  0.76 us (2%)
    ppermute x13, starting transfers between devices, send_to(): return lax.ppermute(x, axes, [(i, target(i)) for i in range(size)])  14.2 us
    all_to_all x1, blocking collectives, on_device(): sums = lax.all_to_all(message, ('dp', 'wide', 'narrow'), 0, 0, tiled=True)  11.4 us
    ppermute x13, waiting for transfers between devices, send_to(): return lax.ppermute(x, axes, [(i, target(i)) for i in range(size)])  10 us
    pallas_call x14, Pallas kernels, call(): pl.pallas_call(kernel, out_shape=[jax.ShapeDtypeStruct(shape, jnp.float32...  2.93 us
  transfers between devices with their start and end apart: 13, of which 5 were waited for; matrix products, arithmetic and copies ran while one was open for 0% of the time, Pallas kernels for 2%

profile of v2, /device:TPU:0, one launch (start us, length us, event | category | flops | bytes accessed | tf_op | source)
XLA Modules:
  0.0 39.4 jit_solution(6661418632957668688)
XLA Ops:
  0.6 1.0 %shard_map.70 = f32[8,12288]{1,0:T(8,128)S(1)} custom-call(bf16[8,73728]{1,0:T(8,128)(2,1)} %bitcast.9), custom_call_target="tpu_custom_call" | custom-call | tf_op jit(solution)/shard_map/pallas_call | solution.py:46
  1.7 0.5 %collective-permute-start.3 = (f32[8,12288]{1,0:T(8,128)S(1)}, f32[8,12288]{1,0:T(8,128)S(1)}, u32[]{:S(2)}, u32[]{:S(2)}) collective-permute-start(f32[8,12288]{1,0:T(8,128)S(1)} %shard_map.70), channel_id=1, source_target_pairs={{0,1},{1,0},{8,9},{9,8},{16,17},{17,16},{24,25},{25,24},{2,3},{3,2... | collective-permute-start | bytes 1179656 | tf_op jit(solution)/shard_map/ppermute | solution.py:22
  2.2 0.3 collective-permute-start
  2.6 0.3 collective-permute-start.5
  2.9 0.6 %collective-permute-done.3.refs_1_ = f32[8,12288]{1,0:T(8,128)S(1)} collective-permute-done((f32[8,12288]{1,0:T(8,128)S(1)}, f32[8,12288]{1,0:T(8,128)S(1)}, u32[]{:S(2)}, u32[]{:S(2)}) %collective-permute-start.3) | collective-permute-done | bytes 393248 | tf_op jit(solution)/shard_map/ppermute | solution.py:22
  3.6 2.7 %collective-permute-start.4 = (f32[8,12288]{1,0:T(8,128)S(1)}, f32[8,12288]{1,0:T(8,128)S(1)}, u32[]{:S(2)}, u32[]{:S(2)}) collective-permute-start(f32[8,12288]{1,0:T(8,128)S(1)} %shard_map.71), channel_id=1, source_target_pairs={{0,17},{1,8},{8,25},{9,0},{16,1},{17,24},{24,9},{25,16},{2,19},{3,... | collective-permute-start | bytes 1179656 | tf_op jit(solution)/shard_map/ppermute | solution.py:22
  6.3 0.0 collective-permute-done.refs_1_.refs_2_.refs_6_
  6.3 1.5 %collective-permute-start.1 = (f32[8,6144]{1,0:T(8,128)S(1)}, f32[8,6144]{1,0:T(8,128)S(1)}, u32[]{:S(2)}, u32[]{:S(2)}) collective-permute-start(f32[8,6144]{1,0:T(8,128)S(1)} %shard_map.68), channel_id=1, source_target_pairs={{0,17},{1,8},{8,25},{9,0},{16,1},{17,24},{24,9},{25,16},{2,19},{3,... | collective-permute-start | bytes 589832 | tf_op jit(solution)/shard_map/ppermute | solution.py:22
  7.8 0.0 collective-permute-done.5.refs_2_.refs_5_
  7.8 3.9 %collective-permute-done.4.refs_1_ = f32[8,12288]{1,0:T(8,128)S(1)} collective-permute-done((f32[8,12288]{1,0:T(8,128)S(1)}, f32[8,12288]{1,0:T(8,128)S(1)}, u32[]{:S(2)}, u32[]{:S(2)}) %collective-permute-start.4) | collective-permute-done | bytes 393248 | tf_op jit(solution)/shard_map/ppermute | solution.py:22
  11.7 2.1 %collective-permute-start.6 = (f32[8,6144]{1,0:T(8,128)S(1)}, f32[8,6144]{1,0:T(8,128)S(1)}, u32[]{:S(2)}, u32[]{:S(2)}) collective-permute-start(f32[8,6144]{1,0:T(8,128)S(1)} %shard_map.73), channel_id=1, source_target_pairs={{0,17},{1,8},{8,25},{9,0},{16,1},{17,24},{24,9},{25,16},{2,19},{3,... | collective-permute-start | bytes 589832 | tf_op jit(solution)/shard_map/ppermute | solution.py:22
  13.9 0.1 collective-permute-start.8
  14.0 0.0 collective-permute-done.1.refs_1_
  14.0 1.6 %collective-permute-start.2 = (f32[8,3072]{1,0:T(8,128)S(1)}, f32[8,3072]{1,0:T(8,128)S(1)}, u32[]{:S(2)}, u32[]{:S(2)}) collective-permute-start(f32[8,3072]{1,0:T(8,128)S(1)} %shard_map.69), channel_id=1, source_target_pairs={{0,17},{1,8},{8,25},{9,0},{16,1},{17,24},{24,9},{25,16},{2,19},{3,... | collective-permute-start | bytes 294920 | tf_op jit(solution)/shard_map/ppermute | solution.py:22
  15.7 0.0 copy-start.1
  15.7 0.0 copy-start.3
  15.7 0.4 %collective-permute-start.7 = (f32[8,3072]{1,0:T(8,128)S(1)}, f32[8,3072]{1,0:T(8,128)S(1)}, u32[]{:S(2)}, u32[]{:S(2)}) collective-permute-start(f32[8,3072]{1,0:T(8,128)S(1)} %shard_map.74), channel_id=1, source_target_pairs={{0,1},{1,0},{8,9},{9,8},{16,17},{17,16},{24,25},{25,24},{2,3},{3,2... | collective-permute-start | bytes 294920 | tf_op jit(solution)/shard_map/ppermute | solution.py:22
  16.1 2.1 %collective-permute-done.2.refs_1_ = f32[8,3072]{1,0:T(8,128)S(1)} collective-permute-done((f32[8,3072]{1,0:T(8,128)S(1)}, f32[8,3072]{1,0:T(8,128)S(1)}, u32[]{:S(2)}, u32[]{:S(2)}) %collective-permute-start.2) | collective-permute-done | bytes 98336 | tf_op jit(solution)/shard_map/ppermute | solution.py:22
  18.2 0.2 shard_map.76
  18.4 0.5 %collective-permute-start.12 = (f32[8,9216]{1,0:T(8,128)S(1)}, f32[8,9216]{1,0:T(8,128)S(1)}, u32[]{:S(2)}, u32[]{:S(2)}) collective-permute-start(f32[8,9216]{1,0:T(8,128)S(1)} %get-tuple-element.16), channel_id=1, source_target_pairs={{0,1},{1,0},{8,9},{9,8},{16,17},{17,16},{24,25},{25,24},{2,3},{3,2... | collective-permute-start | bytes 884744 | tf_op jit(solution)/shard_map/ppermute | solution.py:22
  18.9 3.5 %collective-permute-start.9 = (f32[1,9472]{1,0:T(1,128)S(1)}, f32[1,9472]{1,0:T(1,128)S(1)}, u32[]{:S(2)}, u32[]{:S(2)}) collective-permute-start(f32[1,9472]{1,0:T(1,128)S(1)} %get-tuple-element.13), channel_id=1, source_target_pairs={{0,7},{1,6},{2,5},{3,4},{4,3},{5,2},{6,1},{7,0},{8,15},{9,14},{10,... | collective-permute-start | bytes 113672 | tf_op jit(solution)/shard_map/ppermute | solution.py:22
  22.4 0.0 collective-permute-start.10
  22.4 0.6 %collective-permute-start.11 = (f32[1,9216]{1,0:T(1,128)S(1)}, f32[1,9216]{1,0:T(1,128)S(1)}, u32[]{:S(2)}, u32[]{:S(2)}) collective-permute-start(f32[1,9216]{1,0:T(1,128)S(1)} %get-tuple-element.15), channel_id=1, source_target_pairs={{0,3},{1,2},{2,1},{3,0},{4,7},{5,6},{6,5},{7,4},{8,11},{9,10},{10,... | collective-permute-start | bytes 110600 | tf_op jit(solution)/shard_map/ppermute | solution.py:22
  23.0 0.2 shard_map.78.fixed_in
  23.2 0.3 shard_map.77
  23.5 2.3 %collective-permute-done.11 = f32[1,9216]{1,0:T(1,128)S(1)} collective-permute-done((f32[1,9216]{1,0:T(1,128)S(1)}, f32[1,9216]{1,0:T(1,128)S(1)}, u32[]{:S(2)}, u32[]{:S(2)}) %collective-permute-start.11) | collective-permute-done | bytes 36896 | tf_op jit(solution)/shard_map/ppermute | solution.py:22
  25.8 1.0 %collective-permute-done.10 = f32[1,9344]{1,0:T(1,128)S(1)} collective-permute-done((f32[1,9344]{1,0:T(1,128)S(1)}, f32[1,9344]{1,0:T(1,128)S(1)}, u32[]{:S(2)}, u32[]{:S(2)}) %collective-permute-start.10) | collective-permute-done | bytes 37408 | tf_op jit(solution)/shard_map/ppermute | solution.py:22
  26.8 0.1 multiply_add_fusion.state
  26.9 0.0 copy-start.2
  26.9 0.2 shard_map.79
  27.1 11.4 %all_to_all.11 = f32[32,1,128]{2,1,0:T(1,128)S(1)} all-to-all(f32[32,1,128]{2,1,0:T(1,128)S(1)} %bitcast.21), channel_id=1, replica_groups=mesh['dp'=4,'wide'=4,'narrow'=2] {'dp','wide','narrow'}, dimensions={0} | all-to-all | bytes 32768 | tf_op jit(solution)/shard_map/all_to_all | solution.py:285
  38.5 1.0 %shard_map.80 = (f32[8,9216]{1,0:T(8,128)}, f32[1,8]{1,0:T(1,128)}) custom-call(f32[32,128]{1,0:T(8,128)S(1)} %bitcast.20, f32[8,9216]{1,0:T(8,128)S(1)} %get-tuple-element.20.refs_1_), custom_call_target="tpu_custom_call" | custom-call | tf_op jit(solution)/shard_map/pallas_call | solution.py:46
  (21 shorter events, 0.2 us)
Async XLA Ops:
  0.6 1.6 %copy-start = (bf16[1,8,73728]{2,1,0:T(8,128)(2,1)S(1)}, bf16[1,8,73728]{2,1,0:T(8,128)(2,1)}, u32[]{:S(2)}) copy-start(bf16[1,8,73728]{2,1,0:T(8,128)(2,1)} %param.4) | copy-start | bytes 3538948
  1.7 1.9 %collective-permute-start.3 = (f32[8,12288]{1,0:T(8,128)S(1)}, f32[8,12288]{1,0:T(8,128)S(1)}, u32[]{:S(2)}, u32[]{:S(2)}) collective-permute-start(f32[8,12288]{1,0:T(8,128)S(1)} %shard_map.70), channel_id=1, source_target_pairs={{0,1},{1,0},{8,9},{9,8},{16,17},{17,16},{24,25},{25,24},{2,3},{3,2... | collective-permute-start | bytes 1179656 | tf_op jit(solution)/shard_map/ppermute | solution.py:22
  2.2 4.0 %collective-permute-start = (f32[8,12288]{1,0:T(8,128)S(1)}, f32[8,12288]{1,0:T(8,128)S(1)}, u32[]{:S(2)}, u32[]{:S(2)}) collective-permute-start(f32[8,12288]{1,0:T(8,128)S(1)} %shard_map.67), channel_id=1, source_target_pairs={{0,1},{1,0},{8,9},{9,8},{16,17},{17,16},{24,25},{25,24},{2,3},{3,2... | collective-permute-start | bytes 1179656 | tf_op jit(solution)/shard_map/ppermute | solution.py:22
  2.6 5.2 %collective-permute-start.5 = (f32[8,12288]{1,0:T(8,128)S(1)}, f32[8,12288]{1,0:T(8,128)S(1)}, u32[]{:S(2)}, u32[]{:S(2)}) collective-permute-start(f32[8,12288]{1,0:T(8,128)S(1)} %shard_map.72), channel_id=1, source_target_pairs={{0,1},{1,0},{8,9},{9,8},{16,17},{17,16},{24,25},{25,24},{2,3},{3,2... | collective-permute-start | bytes 1179656 | tf_op jit(solution)/shard_map/ppermute | solution.py:22
  3.6 8.1 %collective-permute-start.4 = (f32[8,12288]{1,0:T(8,128)S(1)}, f32[8,12288]{1,0:T(8,128)S(1)}, u32[]{:S(2)}, u32[]{:S(2)}) collective-permute-start(f32[8,12288]{1,0:T(8,128)S(1)} %shard_map.71), channel_id=1, source_target_pairs={{0,17},{1,8},{8,25},{9,0},{16,1},{17,24},{24,9},{25,16},{2,19},{3,... | collective-permute-start | bytes 1179656 | tf_op jit(solution)/shard_map/ppermute | solution.py:22
  6.3 7.7 %collective-permute-start.1 = (f32[8,6144]{1,0:T(8,128)S(1)}, f32[8,6144]{1,0:T(8,128)S(1)}, u32[]{:S(2)}, u32[]{:S(2)}) collective-permute-start(f32[8,6144]{1,0:T(8,128)S(1)} %shard_map.68), channel_id=1, source_target_pairs={{0,17},{1,8},{8,25},{9,0},{16,1},{17,24},{24,9},{25,16},{2,19},{3,... | collective-permute-start | bytes 589832 | tf_op jit(solution)/shard_map/ppermute | solution.py:22
  11.7 6.5 %collective-permute-start.6 = (f32[8,6144]{1,0:T(8,128)S(1)}, f32[8,6144]{1,0:T(8,128)S(1)}, u32[]{:S(2)}, u32[]{:S(2)}) collective-permute-start(f32[8,6144]{1,0:T(8,128)S(1)} %shard_map.73), channel_id=1, source_target_pairs={{0,17},{1,8},{8,25},{9,0},{16,1},{17,24},{24,9},{25,16},{2,19},{3,... | collective-permute-start | bytes 589832 | tf_op jit(solution)/shard_map/ppermute | solution.py:22
  13.9 4.4 %collective-permute-start.8 = (f32[8,6144]{1,0:T(8,128)S(1)}, f32[8,6144]{1,0:T(8,128)S(1)}, u32[]{:S(2)}, u32[]{:S(2)}) collective-permute-start(f32[8,6144]{1,0:T(8,128)S(1)} %shard_map.75), channel_id=1, source_target_pairs={{0,1},{1,0},{8,9},{9,8},{16,17},{17,16},{24,25},{25,24},{2,3},{3,2... | collective-permute-start | bytes 589832 | tf_op jit(solution)/shard_map/ppermute | solution.py:22
  14.0 4.2 %collective-permute-start.2 = (f32[8,3072]{1,0:T(8,128)S(1)}, f32[8,3072]{1,0:T(8,128)S(1)}, u32[]{:S(2)}, u32[]{:S(2)}) collective-permute-start(f32[8,3072]{1,0:T(8,128)S(1)} %shard_map.69), channel_id=1, source_target_pairs={{0,17},{1,8},{8,25},{9,0},{16,1},{17,24},{24,9},{25,16},{2,19},{3,... | collective-permute-start | bytes 294920 | tf_op jit(solution)/shard_map/ppermute | solution.py:22
  15.6 7.3 %copy-start.4 = (f32[9216]{0:T(1024)S(1)}, f32[9216]{0:T(1024)}, u32[]{:S(2)}) copy-start(f32[9216]{0:T(1024)} %param.7) | copy-start | bytes 110596
  15.7 7.3 %copy-start.1 = (bf16[8,9216]{1,0:T(8,128)(2,1)S(1)}, bf16[8,9216]{1,0:T(8,128)(2,1)}, u32[]{:S(2)}) copy-start(bf16[8,9216]{1,0:T(8,128)(2,1)} %weight.1) | copy-start | bytes 442372
  15.7 7.3 %copy-start.3 = (f32[8]{0:T(128)S(1)}, f32[8]{0:T(128)}, u32[]{:S(2)}) copy-start(f32[8]{0:T(128)} %param.6) | copy-start | bytes 100
  15.7 2.5 %collective-permute-start.7 = (f32[8,3072]{1,0:T(8,128)S(1)}, f32[8,3072]{1,0:T(8,128)S(1)}, u32[]{:S(2)}, u32[]{:S(2)}) collective-permute-start(f32[8,3072]{1,0:T(8,128)S(1)} %shard_map.74), channel_id=1, source_target_pairs={{0,1},{1,0},{8,9},{9,8},{16,17},{17,16},{24,25},{25,24},{2,3},{3,2... | collective-permute-start | bytes 294920 | tf_op jit(solution)/shard_map/ppermute | solution.py:22
  18.4 4.8 %collective-permute-start.12 = (f32[8,9216]{1,0:T(8,128)S(1)}, f32[8,9216]{1,0:T(8,128)S(1)}, u32[]{:S(2)}, u32[]{:S(2)}) collective-permute-start(f32[8,9216]{1,0:T(8,128)S(1)} %get-tuple-element.16), channel_id=1, source_target_pairs={{0,1},{1,0},{8,9},{9,8},{16,17},{17,16},{24,25},{25,24},{2,3},{3,2... | collective-permute-start | bytes 884744 | tf_op jit(solution)/shard_map/ppermute | solution.py:22
  18.9 7.9 %collective-permute-start.9 = (f32[1,9472]{1,0:T(1,128)S(1)}, f32[1,9472]{1,0:T(1,128)S(1)}, u32[]{:S(2)}, u32[]{:S(2)}) collective-permute-start(f32[1,9472]{1,0:T(1,128)S(1)} %get-tuple-element.13), channel_id=1, source_target_pairs={{0,7},{1,6},{2,5},{3,4},{4,3},{5,2},{6,1},{7,0},{8,15},{9,14},{10,... | collective-permute-start | bytes 113672 | tf_op jit(solution)/shard_map/ppermute | solution.py:22
  22.4 4.4 %collective-permute-start.10 = (f32[1,9344]{1,0:T(1,128)S(1)}, f32[1,9344]{1,0:T(1,128)S(1)}, u32[]{:S(2)}, u32[]{:S(2)}) collective-permute-start(f32[1,9344]{1,0:T(1,128)S(1)} %get-tuple-element.14), channel_id=1, source_target_pairs={{0,5},{1,4},{2,7},{3,6},{4,1},{5,0},{6,3},{7,2},{8,13},{9,12},{10,... | collective-permute-start | bytes 112136 | tf_op jit(solution)/shard_map/ppermute | solution.py:22
  22.4 3.4 %collective-permute-start.11 = (f32[1,9216]{1,0:T(1,128)S(1)}, f32[1,9216]{1,0:T(1,128)S(1)}, u32[]{:S(2)}, u32[]{:S(2)}) collective-permute-start(f32[1,9216]{1,0:T(1,128)S(1)} %get-tuple-element.15), channel_id=1, source_target_pairs={{0,3},{1,2},{2,1},{3,0},{4,7},{5,6},{6,5},{7,4},{8,11},{9,10},{10,... | collective-permute-start | bytes 110600 | tf_op jit(solution)/shard_map/ppermute | solution.py:22
  26.9 12.5 %copy-start.2 = (f32[1,9216]{1,0:T(1,128)}, f32[1,9216]{1,0:T(1,128)S(1)}, u32[]{:S(2)}) copy-start(f32[1,9216]{1,0:T(1,128)S(1)} %multiply_add_fusion.state) | copy-start | bytes 110596

commit v3 on v2

--- a/solution.py
+++ b/solution.py
@@ -57,50 +57,37 @@
     def __init__(self, dp, narrow, cols):
         self.narrow, self.cols = narrow, cols
         self.masks = bits_of(dp * narrow)[1:]
-        tiles = cols // LANES
-        cut = (tiles * 2 + 2) // 3 * LANES
-        self.chunks = [(0, cut), (cut, cols - cut)]
-        self.keys = [(t, c) for t in range(dp * narrow // 2) for c in range(2)]
-
-    def width(self, key):
-        return self.chunks[key[-1]][1]
-
-    def home(self, t):
-        steps = len(self.masks)
-        return self.side(next((s for s in range(steps) if t >> s & 1), steps))
-
-    def side(self, s):
-        return (len(self.masks) - s + 1) & 1
+        self.steps = len(self.masks)
+        self.all = range(dp * narrow // 2)
 
     def mask(self, core, s):
         return self.masks[-1 - s] if core else self.masks[s]
 
-    def target(self, device, s):
-        return device ^ self.mask((device ^ self.side(s)) & 1, s) ^ 1
-
-    def start(self, key):
-        j, t, c = key
+    def home(self, t):
+        return self.side(next((s for s in range(self.steps) if t >> s & 1), self.steps))
+
+    def side(self, s):
+        return (self.steps - s + 1) & 1
+
+    def target(self, device, s, cross):
+        return device ^ self.mask((device ^ self.side(s)) & 1, s) ^ cross
+
+    def start(self, j, t):
         group = lax.axis_index("dp") * self.narrow + lax.axis_index("narrow")
         group = group ^ j
-        reach = [sum(self.mask(core, s) for s in range(len(self.masks)) if t >> s & 1) for core in range(2)]
+        reach = [sum(self.mask(core, s) for s in range(self.steps) if t >> s & 1) for core in range(2)]
         block = group ^ jnp.where(group % 2 == 1, reach[1], reach[0])
-        return pl.multiple_of(block * self.cols + self.chunks[c][0], LANES)
-
-    def places(self, keys):
-        at, out = 0, []
-        for key in keys:
-            out.append(at)
-            at += self.width(key)
-        return out, at
+        return pl.multiple_of(block * self.cols, LANES)
 
 
 def fetch_kernel(blocks, keys, part, out, raw, sem):
     spans, copies = [], []
-    for key, at in zip(keys, blocks.places(keys)[0]):
-        start, tiles = blocks.start(key), blocks.width(key) // LANES
-        cuts = [tiles * i // PIECES * LANES for i in range(PIECES + 1)]
+    tiles = blocks.cols // LANES
+    cuts = [tiles * i // PIECES * LANES for i in range(PIECES + 1)]
+    for i, key in enumerate(keys):
+        start = blocks.start(*key)
         for a, b in zip(cuts, cuts[1:]):
-            spans.append(pl.ds(at + a, b - a))
+            spans.append(pl.ds(i * blocks.cols + a, b - a))
             source = part.at[:, pl.ds(pl.multiple_of(start + a, LANES), b - a)]
             copies.append(pltpu.make_async_copy(source, raw.at[:, spans[-1]], sem.at[len(copies)]))
     for copy in copies:
@@ -110,33 +97,29 @@
         out[:, span] = raw[:, span].astype(jnp.float32)
 
 
-def load(blocks, refs, term, width):
+def load(blocks, refs, term):
     slot, at = term
     if slot == 0:
-        return refs[0][:, pl.ds(blocks.start(at), width)].astype(jnp.float32)
-    return refs[slot][:, at : at + width]
+        return refs[0][:, pl.ds(blocks.start(*at), blocks.cols)].astype(jnp.float32)
+    return refs[slot][:, at * blocks.cols : (at + 1) * blocks.cols]
 
 
 def merge_kernel(blocks, plan, *refs):
     out = refs[-1]
-    at = 0
-    for width, terms in plan:
-        out[:, at : at + width] = tree([load(blocks, refs, term, width) for term in terms])
-        at += width
-
-
-def grad_kernel(plan_of, blocks, plan, *refs):
-    grad_out, *cols_out = refs[plan_of:]
-    at = 0
-    for width, terms in plan:
-        grad = tree([load(blocks, refs, term, width) for term in terms])
-        grad_out[:, at : at + width] = grad
-        for col_out in cols_out:
-            col_out[:, at : at + width] = jnp.sum(grad * grad + 1e-30, axis=0, keepdims=True)
-        at += width
+    for i, terms in enumerate(plan):
+        out[:, i * blocks.cols : (i + 1) * blocks.cols] = tree([load(blocks, refs, term) for term in terms])
+
+
+def grad_kernel(inputs, blocks, plan, *refs):
+    grad_out, *cols_out = refs[inputs:]
+    cols = blocks.cols
+    grad = tree([load(blocks, refs, term) for term in plan[0]])
+    grad_out[...] = grad
+    col = jnp.sum(grad * grad + 1e-30, axis=0, keepdims=True)
     for col_out in cols_out:
-        if col_out.shape[1] > at:
-            col_out[:, at:] = jnp.zeros((1, col_out.shape[1] - at), jnp.float32)
+        col_out[:, :cols] = col
+        if col_out.shape[1] > cols:
+            col_out[:, cols:] = jnp.zeros((1, col_out.shape[1] - cols), jnp.float32)
 
 
 def square_kernel(grad_in, col_out, row_out):
@@ -196,18 +179,18 @@
     group_axes = ("dp", "narrow")
     size = dp * narrow
     arrays = [part]
-    held = {(t, c): [(0, (blocks.home(t), t, c))] for t, c in blocks.keys}
-
-    def merge(kernel, widths, sums, shapes):
+    held = {t: [(0, (blocks.home(t), t))] for t in blocks.all}
+
+    def merge(kernel, sums, shapes):
         used = [0] + sorted({slot for terms in sums for slot, _ in terms} - {0}, reverse=True)
-        plan = [(width, [(used.index(slot), at) for slot, at in terms]) for width, terms in zip(widths, sums)]
+        plan = [[(used.index(slot), at) for slot, at in terms] for terms in sums]
         return call(lambda *refs: kernel(blocks, plan, *refs), shapes, [VMEM] * len(used), *[arrays[u] for u in used])
 
-    def pack(keys, sums):
-        return merge(merge_kernel, [blocks.width(key) for key in keys], sums, [(rows, blocks.places(keys)[1])])[0]
+    def pack(sums):
+        return merge(merge_kernel, sums, [(rows, len(sums) * cols)])[0]
 
     def fetch(keys):
-        shape = (rows, blocks.places(keys)[1])
+        shape = (rows, len(keys) * cols)
         return call(
             lambda *refs: fetch_kernel(blocks, keys, *refs),
             [shape],
@@ -216,42 +199,38 @@
             scratch=[pltpu.VMEM(shape, part.dtype), pltpu.SemaphoreType.DMA((PIECES * len(keys),))],
         )[0]
 
-    def receive(keys, send, target):
+    def receive(send, target):
         arrays.append(send_to(send, group_axes, size, target))
-        return [(key, (len(arrays) - 1, at)) for key, at in zip(keys, blocks.places(keys)[0])]
+        return [(len(arrays) - 1, at) for at in range(send.shape[1] // cols)]
 
     def other(device):
         return device ^ 1
 
-    groups = (
-        [key for key in held if key[1] == 0 and key[0] & 1],
-        [key for key in held if key[1] == 1],
-        [key for key in held if key[1] == 0 and not key[0] & 1],
-    )
-    for i, keys in enumerate(groups):
-        given = [(1 ^ blocks.home(t), t, c) for t, c in keys]
-        send = pack(keys, [[(0, key)] for key in given]) if i else fetch(given)
-        for key, term in receive(keys, send, other):
-            held[key].append(term)
-    for s in range(len(blocks.masks)):
-        for c in range(2):
-            keys = [key for key in held if key[0] >> s & 1 and key[1] == c]
-            got = receive(keys, pack(keys, [held.pop(key) for key in keys]), lambda i: blocks.target(i, s))
-            got = [((t ^ 1 << s, c), term) for (t, c), term in got]
-            away = [(key, term) for key, term in got if blocks.home(key[0]) != blocks.side(s + 1)]
-            if away:
-                keys = [key for key, _ in away]
-                got = [pair for pair in got if pair not in away]
-                got += receive(keys, pack(keys, [[term] for _, term in away]), other)
-            for key, term in got:
-                held[key].append(term)
-    left = sorted(held)
+    def stages(s):
+        groups = {}
+        for t in blocks.all:
+            if t & (2 << s) - 1 == 1 << s:
+                cross = blocks.side(s) ^ blocks.home(t ^ 1 << s)
+                groups.setdefault((t >> s == 1, 1 - cross), []).append(t)
+        return [(ts, 1 - straight) for (_, straight), ts in sorted(groups.items())]
+
+    even = [t for t in blocks.all if t and t % 2 == 0]
+    groups = [ts for ts, _ in stages(0)] + [even, [0]]
+    for i, ts in enumerate(group for group in groups if group):
+        given = [(1 ^ blocks.home(t), t) for t in ts]
+        send = pack([[(0, key)] for key in given]) if i else fetch(given)
+        for t, term in zip(ts, receive(send, other)):
+            held[t].append(term)
+    for s in range(blocks.steps):
+        for ts, cross in stages(s):
+            send = pack([held.pop(t) for t in ts])
+            for t, term in zip(ts, receive(send, lambda i: blocks.target(i, s, cross))):
+                held[t ^ 1 << s].append(term)
     first, *rounds = wide_masks(wide)
-    inputs = 1 + len({slot for key in left for slot, _ in held[key]} - {0})
+    inputs = 1 + len({slot for slot, _ in held[0]} - {0})
     grad, *sends = merge(
         lambda *refs: grad_kernel(inputs, *refs),
-        [blocks.width(key) for key in left],
-        [held[key] for key in left],
+        [held[0]],
         [(rows, cols)] + [(1, cols + LANES * (len(first) - 1 - i)) for i in range(len(first))],
     )
 

time: 39.6 us -> 38.2 us (0.965)
  starting transfers between devices: 14.2 us -> 12.3 us
  waiting for transfers between devices: 10 us -> 10.8 us
    ppermute x13 -> x11, starting transfers between devices: 14.2 us -> 12.3 us  [send_to(): return lax.ppermute(x, axes, [(i, target(i)) for i in range(size)])]
    ppermute x13 -> x11, waiting for transfers between devices: 10 us -> 10.8 us  [send_to(): return lax.ppermute(x, axes, [(i, target(i)) for i in range(size)])]
    pallas_call x14 -> x12, Pallas kernels: 2.93 us -> 2.93 us  [call(): pl.pallas_call(kernel, out_shape=[jax.ShapeDtypeStruct(shape, jnp.float32...]
  transfers between devices with their start and end apart: 13 -> 11, of which waited for: 5 -> 6; matrix products, arithmetic and copies ran while one was open for 0% -> 0% of each run, Pallas kernels for 2% -> 2%
where the time goes in v3:
time: 38.2 us; the launch traced here: 38.1 us
  starting transfers between devices  12.3 us (32%)
  blocking collectives  11.2 us (29%)
  waiting for transfers between devices  10.8 us (28%)
  Pallas kernels  2.93 us (8%)
  between operations  0.75 us (2%)
    ppermute x11, starting transfers between devices, send_to(): return lax.ppermute(x, axes, [(i, target(i)) for i in range(size)])  12.3 us
    all_to_all x1, blocking collectives, on_device(): sums = lax.all_to_all(message, ('dp', 'wide', 'narrow'), 0, 0, tiled=True)  11.2 us
    ppermute x11, waiting for transfers between devices, send_to(): return lax.ppermute(x, axes, [(i, target(i)) for i in range(size)])  10.8 us
    pallas_call x12, Pallas kernels, call(): pl.pallas_call(kernel, out_shape=[jax.ShapeDtypeStruct(shape, jnp.float32...  2.93 us
  transfers between devices with their start and end apart: 11, of which 6 were waited for; matrix products, arithmetic and copies ran while one was open for 0% of the time, Pallas kernels for 2%

profile of v3, /device:TPU:0, one launch (start us, length us, event | category | flops | bytes accessed | tf_op | source)
XLA Modules:
  0.0 38.1 jit_solution(13146454962322549136)
XLA Ops:
  0.6 1.1 %shard_map.67 = f32[8,9216]{1,0:T(8,128)S(1)} custom-call(bf16[8,73728]{1,0:T(8,128)(2,1)} %bitcast.9), custom_call_target="tpu_custom_call" | custom-call | tf_op jit(solution)/shard_map/pallas_call | solution.py:46
  1.7 0.5 %collective-permute-start = (f32[8,9216]{1,0:T(8,128)S(1)}, f32[8,9216]{1,0:T(8,128)S(1)}, u32[]{:S(2)}, u32[]{:S(2)}) collective-permute-start(f32[8,9216]{1,0:T(8,128)S(1)} %shard_map.67), channel_id=1, source_target_pairs={{0,1},{1,0},{8,9},{9,8},{16,17},{17,16},{24,25},{25,24},{2,3},{3,2... | collective-permute-start | bytes 884744 | tf_op jit(solution)/shard_map/ppermute | solution.py:22
  2.2 0.3 collective-permute-start.4
  2.5 0.4 collective-permute-start.2
  2.9 0.5 %collective-permute-done.refs_1_ = f32[8,9216]{1,0:T(8,128)S(1)} collective-permute-done((f32[8,9216]{1,0:T(8,128)S(1)}, f32[8,9216]{1,0:T(8,128)S(1)}, u32[]{:S(2)}, u32[]{:S(2)}) %collective-permute-start) | collective-permute-done | bytes 294944 | tf_op jit(solution)/shard_map/ppermute | solution.py:22
  3.5 2.7 %collective-permute-start.1 = (f32[8,9216]{1,0:T(8,128)S(1)}, f32[8,9216]{1,0:T(8,128)S(1)}, u32[]{:S(2)}, u32[]{:S(2)}) collective-permute-start(f32[8,9216]{1,0:T(8,128)S(1)} %shard_map.68), channel_id=1, source_target_pairs={{0,17},{1,8},{8,25},{9,0},{16,1},{17,24},{24,9},{25,16},{2,19},{3,... | collective-permute-start | bytes 884744 | tf_op jit(solution)/shard_map/ppermute | solution.py:22
  6.2 0.4 %collective-permute-start.6 = (f32[8,9216]{1,0:T(8,128)S(1)}, f32[8,9216]{1,0:T(8,128)S(1)}, u32[]{:S(2)}, u32[]{:S(2)}) collective-permute-start(f32[8,9216]{1,0:T(8,128)S(1)} %shard_map.73), channel_id=1, source_target_pairs={{0,1},{1,0},{8,9},{9,8},{16,17},{17,16},{24,25},{25,24},{2,3},{3,2... | collective-permute-start | bytes 884744 | tf_op jit(solution)/shard_map/ppermute | solution.py:22
  6.6 0.0 collective-permute-done.4.refs_1_
  6.6 1.6 %collective-permute-start.5 = (f32[8,9216]{1,0:T(8,128)S(1)}, f32[8,9216]{1,0:T(8,128)S(1)}, u32[]{:S(2)}, u32[]{:S(2)}) collective-permute-start(f32[8,9216]{1,0:T(8,128)S(1)} %shard_map.72), channel_id=1, source_target_pairs={{0,16},{1,9},{8,24},{9,1},{16,0},{17,25},{24,8},{25,17},{2,18},{3,... | collective-permute-start | bytes 884744 | tf_op jit(solution)/shard_map/ppermute | solution.py:22
  8.2 2.3 %collective-permute-done.1.refs_1_ = f32[8,9216]{1,0:T(8,128)S(1)} collective-permute-done((f32[8,9216]{1,0:T(8,128)S(1)}, f32[8,9216]{1,0:T(8,128)S(1)}, u32[]{:S(2)}, u32[]{:S(2)}) %collective-permute-start.1) | collective-permute-done | bytes 294944 | tf_op jit(solution)/shard_map/ppermute | solution.py:22
  10.6 0.0 copy-start.4
  10.6 0.0 copy-start.1
  10.6 0.0 copy-start.3
  10.6 1.8 %collective-permute-start.3 = (f32[8,9216]{1,0:T(8,128)S(1)}, f32[8,9216]{1,0:T(8,128)S(1)}, u32[]{:S(2)}, u32[]{:S(2)}) collective-permute-start(f32[8,9216]{1,0:T(8,128)S(1)} %shard_map.70), channel_id=1, source_target_pairs={{0,17},{1,8},{8,25},{9,0},{16,1},{17,24},{24,9},{25,16},{2,19},{3,... | collective-permute-start | bytes 884744 | tf_op jit(solution)/shard_map/ppermute | solution.py:22
  12.4 0.0 collective-permute-done.6.refs_3_
  12.4 1.8 %collective-permute-done.5.refs_2_ = f32[8,9216]{1,0:T(8,128)S(1)} collective-permute-done((f32[8,9216]{1,0:T(8,128)S(1)}, f32[8,9216]{1,0:T(8,128)S(1)}, u32[]{:S(2)}, u32[]{:S(2)}) %collective-permute-start.5) | collective-permute-done | bytes 294944 | tf_op jit(solution)/shard_map/ppermute | solution.py:22
  14.3 2.6 %collective-permute-done.3.refs_1_ = f32[8,9216]{1,0:T(8,128)S(1)} collective-permute-done((f32[8,9216]{1,0:T(8,128)S(1)}, f32[8,9216]{1,0:T(8,128)S(1)}, u32[]{:S(2)}, u32[]{:S(2)}) %collective-permute-start.3) | collective-permute-done | bytes 294944 | tf_op jit(solution)/shard_map/ppermute | solution.py:22
  16.8 0.1 shard_map.74
  17.0 0.5 %collective-permute-start.10 = (f32[8,9216]{1,0:T(8,128)S(1)}, f32[8,9216]{1,0:T(8,128)S(1)}, u32[]{:S(2)}, u32[]{:S(2)}) collective-permute-start(f32[8,9216]{1,0:T(8,128)S(1)} %get-tuple-element.16), channel_id=1, source_target_pairs={{0,1},{1,0},{8,9},{9,8},{16,17},{17,16},{24,25},{25,24},{2,3},{3,2... | collective-permute-start | bytes 884744 | tf_op jit(solution)/shard_map/ppermute | solution.py:22
  17.5 3.8 %collective-permute-start.7 = (f32[1,9472]{1,0:T(1,128)S(1)}, f32[1,9472]{1,0:T(1,128)S(1)}, u32[]{:S(2)}, u32[]{:S(2)}) collective-permute-start(f32[1,9472]{1,0:T(1,128)S(1)} %get-tuple-element.13), channel_id=1, source_target_pairs={{0,7},{1,6},{2,5},{3,4},{4,3},{5,2},{6,1},{7,0},{8,15},{9,14},{10,... | collective-permute-start | bytes 113672 | tf_op jit(solution)/shard_map/ppermute | solution.py:22
  21.3 0.0 collective-permute-start.8
  21.3 0.3 collective-permute-start.9
  21.6 0.2 shard_map.76.fixed_in
  21.8 0.0 collective-permute-done.10.grad_in
  21.8 0.3 shard_map.75
  22.1 2.7 %collective-permute-done.9 = f32[1,9216]{1,0:T(1,128)S(1)} collective-permute-done((f32[1,9216]{1,0:T(1,128)S(1)}, f32[1,9216]{1,0:T(1,128)S(1)}, u32[]{:S(2)}, u32[]{:S(2)}) %collective-permute-start.9) | collective-permute-done | bytes 36896 | tf_op jit(solution)/shard_map/ppermute | solution.py:22
  24.7 0.9 %collective-permute-done.8 = f32[1,9344]{1,0:T(1,128)S(1)} collective-permute-done((f32[1,9344]{1,0:T(1,128)S(1)}, f32[1,9344]{1,0:T(1,128)S(1)}, u32[]{:S(2)}, u32[]{:S(2)}) %collective-permute-start.8) | collective-permute-done | bytes 37408 | tf_op jit(solution)/shard_map/ppermute | solution.py:22
  25.6 0.1 multiply_add_fusion.state
  25.7 0.0 copy-start.2
  25.8 0.2 shard_map.77
  25.9 11.2 %all_to_all.11 = f32[32,1,128]{2,1,0:T(1,128)S(1)} all-to-all(f32[32,1,128]{2,1,0:T(1,128)S(1)} %bitcast.19), channel_id=1, replica_groups=mesh['dp'=4,'wide'=4,'narrow'=2] {'dp','wide','narrow'}, dimensions={0} | all-to-all | bytes 32768 | tf_op jit(solution)/shard_map/all_to_all | solution.py:264
  37.1 1.0 %shard_map.78 = (f32[8,9216]{1,0:T(8,128)}, f32[1,8]{1,0:T(1,128)}) custom-call(f32[32,128]{1,0:T(8,128)S(1)} %bitcast.18, f32[8,9216]{1,0:T(8,128)S(1)} %get-tuple-element.20.refs_1_), custom_call_target="tpu_custom_call" | custom-call | tf_op jit(solution)/shard_map/pallas_call | solution.py:46
  (15 shorter events, 0.2 us)
Async XLA Ops:
  0.6 1.6 %copy-start = (bf16[1,8,73728]{2,1,0:T(8,128)(2,1)S(1)}, bf16[1,8,73728]{2,1,0:T(8,128)(2,1)}, u32[]{:S(2)}) copy-start(bf16[1,8,73728]{2,1,0:T(8,128)(2,1)} %param.4) | copy-start | bytes 3538948
  1.7 1.7 %collective-permute-start = (f32[8,9216]{1,0:T(8,128)S(1)}, f32[8,9216]{1,0:T(8,128)S(1)}, u32[]{:S(2)}, u32[]{:S(2)}) collective-permute-start(f32[8,9216]{1,0:T(8,128)S(1)} %shard_map.67), channel_id=1, source_target_pairs={{0,1},{1,0},{8,9},{9,8},{16,17},{17,16},{24,25},{25,24},{2,3},{3,2... | collective-permute-start | bytes 884744 | tf_op jit(solution)/shard_map/ppermute | solution.py:22
  2.2 4.3 %collective-permute-start.4 = (f32[8,9216]{1,0:T(8,128)S(1)}, f32[8,9216]{1,0:T(8,128)S(1)}, u32[]{:S(2)}, u32[]{:S(2)}) collective-permute-start(f32[8,9216]{1,0:T(8,128)S(1)} %shard_map.71), channel_id=1, source_target_pairs={{0,1},{1,0},{8,9},{9,8},{16,17},{17,16},{24,25},{25,24},{2,3},{3,2... | collective-permute-start | bytes 884744 | tf_op jit(solution)/shard_map/ppermute | solution.py:22
  2.5 5.7 %collective-permute-start.2 = (f32[8,9216]{1,0:T(8,128)S(1)}, f32[8,9216]{1,0:T(8,128)S(1)}, u32[]{:S(2)}, u32[]{:S(2)}) collective-permute-start(f32[8,9216]{1,0:T(8,128)S(1)} %shard_map.69), channel_id=1, source_target_pairs={{0,1},{1,0},{8,9},{9,8},{16,17},{17,16},{24,25},{25,24},{2,3},{3,2... | collective-permute-start | bytes 884744 | tf_op jit(solution)/shard_map/ppermute | solution.py:22
  3.5 7.1 %collective-permute-start.1 = (f32[8,9216]{1,0:T(8,128)S(1)}, f32[8,9216]{1,0:T(8,128)S(1)}, u32[]{:S(2)}, u32[]{:S(2)}) collective-permute-start(f32[8,9216]{1,0:T(8,128)S(1)} %shard_map.68), channel_id=1, source_target_pairs={{0,17},{1,8},{8,25},{9,0},{16,1},{17,24},{24,9},{25,16},{2,19},{3,... | collective-permute-start | bytes 884744 | tf_op jit(solution)/shard_map/ppermute | solution.py:22
  6.2 6.3 %collective-permute-start.6 = (f32[8,9216]{1,0:T(8,128)S(1)}, f32[8,9216]{1,0:T(8,128)S(1)}, u32[]{:S(2)}, u32[]{:S(2)}) collective-permute-start(f32[8,9216]{1,0:T(8,128)S(1)} %shard_map.73), channel_id=1, source_target_pairs={{0,1},{1,0},{8,9},{9,8},{16,17},{17,16},{24,25},{25,24},{2,3},{3,2... | collective-permute-start | bytes 884744 | tf_op jit(solution)/shard_map/ppermute | solution.py:22
  6.6 7.7 %collective-permute-start.5 = (f32[8,9216]{1,0:T(8,128)S(1)}, f32[8,9216]{1,0:T(8,128)S(1)}, u32[]{:S(2)}, u32[]{:S(2)}) collective-permute-start(f32[8,9216]{1,0:T(8,128)S(1)} %shard_map.72), channel_id=1, source_target_pairs={{0,16},{1,9},{8,24},{9,1},{16,0},{17,25},{24,8},{25,17},{2,18},{3,... | collective-permute-start | bytes 884744 | tf_op jit(solution)/shard_map/ppermute | solution.py:22
  10.6 11.0 %copy-start.4 = (f32[9216]{0:T(1024)S(1)}, f32[9216]{0:T(1024)}, u32[]{:S(2)}) copy-start(f32[9216]{0:T(1024)} %param.7) | copy-start | bytes 110596
  10.6 11.0 %copy-start.1 = (bf16[8,9216]{1,0:T(8,128)(2,1)S(1)}, bf16[8,9216]{1,0:T(8,128)(2,1)}, u32[]{:S(2)}) copy-start(bf16[8,9216]{1,0:T(8,128)(2,1)} %weight.1) | copy-start | bytes 442372
  10.6 11.0 %copy-start.3 = (f32[8]{0:T(128)S(1)}, f32[8]{0:T(128)}, u32[]{:S(2)}) copy-start(f32[8]{0:T(128)} %param.6) | copy-start | bytes 100
  10.6 6.2 %collective-permute-start.3 = (f32[8,9216]{1,0:T(8,128)S(1)}, f32[8,9216]{1,0:T(8,128)S(1)}, u32[]{:S(2)}, u32[]{:S(2)}) collective-permute-start(f32[8,9216]{1,0:T(8,128)S(1)} %shard_map.70), channel_id=1, source_target_pairs={{0,17},{1,8},{8,25},{9,0},{16,1},{17,24},{24,9},{25,16},{2,19},{3,... | collective-permute-start | bytes 884744 | tf_op jit(solution)/shard_map/ppermute | solution.py:22
  17.0 4.8 %collective-permute-start.10 = (f32[8,9216]{1,0:T(8,128)S(1)}, f32[8,9216]{1,0:T(8,128)S(1)}, u32[]{:S(2)}, u32[]{:S(2)}) collective-permute-start(f32[8,9216]{1,0:T(8,128)S(1)} %get-tuple-element.16), channel_id=1, source_target_pairs={{0,1},{1,0},{8,9},{9,8},{16,17},{17,16},{24,25},{25,24},{2,3},{3,2... | collective-permute-start | bytes 884744 | tf_op jit(solution)/shard_map/ppermute | solution.py:22
  17.5 8.2 %collective-permute-start.7 = (f32[1,9472]{1,0:T(1,128)S(1)}, f32[1,9472]{1,0:T(1,128)S(1)}, u32[]{:S(2)}, u32[]{:S(2)}) collective-permute-start(f32[1,9472]{1,0:T(1,128)S(1)} %get-tuple-element.13), channel_id=1, source_target_pairs={{0,7},{1,6},{2,5},{3,4},{4,3},{5,2},{6,1},{7,0},{8,15},{9,14},{10,... | collective-permute-start | bytes 113672 | tf_op jit(solution)/shard_map/ppermute | solution.py:22
  21.3 4.4 %collective-permute-start.8 = (f32[1,9344]{1,0:T(1,128)S(1)}, f32[1,9344]{1,0:T(1,128)S(1)}, u32[]{:S(2)}, u32[]{:S(2)}) collective-permute-start(f32[1,9344]{1,0:T(1,128)S(1)} %get-tuple-element.14), channel_id=1, source_target_pairs={{0,5},{1,4},{2,7},{3,6},{4,1},{5,0},{6,3},{7,2},{8,13},{9,12},{10,... | collective-permute-start | bytes 112136 | tf_op jit(solution)/shard_map/ppermute | solution.py:22
  21.3 3.4 %collective-permute-start.9 = (f32[1,9216]{1,0:T(1,128)S(1)}, f32[1,9216]{1,0:T(1,128)S(1)}, u32[]{:S(2)}, u32[]{:S(2)}) collective-permute-start(f32[1,9216]{1,0:T(1,128)S(1)} %get-tuple-element.15), channel_id=1, source_target_pairs={{0,3},{1,2},{2,1},{3,0},{4,7},{5,6},{6,5},{7,4},{8,11},{9,10},{10,... | collective-permute-start | bytes 110600 | tf_op jit(solution)/shard_map/ppermute | solution.py:22
  25.7 12.3 %copy-start.2 = (f32[1,9216]{1,0:T(1,128)}, f32[1,9216]{1,0:T(1,128)S(1)}, u32[]{:S(2)}) copy-start(f32[1,9216]{1,0:T(1,128)S(1)} %multiply_add_fusion.state) | copy-start | bytes 110596

commit v4 on v3

--- a/solution.py
+++ b/solution.py
@@ -22,9 +22,16 @@
     return lax.ppermute(x, axes, [(i, target(i)) for i in range(size)])
 
 
-def wide_masks(wide):
-    bits = bits_of(wide)
-    return [[sum(now)] * (len(now) - 1) + now[::-1] for now in (bits[i : i + 2] for i in range(0, len(bits), 2))]
+def wide_rounds(wide):
+    step, rounds = 1, []
+    while step < wide:
+        rounds.append((step, min(4, wide // step)))
+        step *= rounds[-1][1]
+    return rounds
+
+
+def wide_sum(terms, own):
+    return tree(terms[::2] + terms[1::2] + [own])
 
 
 def tree(terms):
@@ -226,23 +233,29 @@
             send = pack([held.pop(t) for t in ts])
             for t, term in zip(ts, receive(send, lambda i: blocks.target(i, s, cross))):
                 held[t ^ 1 << s].append(term)
-    first, *rounds = wide_masks(wide)
+    first, *rounds = wide_rounds(wide)
     inputs = 1 + len({slot for slot, _ in held[0]} - {0})
     grad, *sends = merge(
         lambda *refs: grad_kernel(inputs, *refs),
         [held[0]],
-        [(rows, cols)] + [(1, cols + LANES * (len(first) - 1 - i)) for i in range(len(first))],
+        [(rows, cols)] + [(1, cols + LANES * (first[1] - 1 - k)) for k in range(1, first[1])],
     )
 
-    def send_wide(x, mask):
-        return send_to(x, ("wide", "narrow"), wide * narrow, lambda i: i ^ mask)
-
-    terms = [send_wide(x, mask * narrow ^ 1)[:, :cols] for x, mask in zip(sends, first)]
+    def send_wide(x, step, width, shift, cross):
+        def target(i):
+            z, n = divmod(i, narrow)
+            place = z // step % width
+            z += ((place + shift) % width - place) * step
+            return z * narrow + (n ^ cross)
+
+        return send_to(x, ("wide", "narrow"), wide * narrow, target)
+
+    terms = [send_wide(x, *first, k + 1, 1)[:, :cols] for k, x in enumerate(sends)]
     grad = send_to(grad, group_axes, size, other)
     col_sum, row_part = call(square_kernel, [(1, cols), (1, LANES)], [VMEM], grad)
-    col_sum = tree(terms + [col_sum])
-    for masks in rounds:
-        col_sum = tree([send_wide(col_sum, mask * narrow) for mask in masks] + [col_sum])
+    col_sum = wide_sum(terms, col_sum)
+    for step, width in rounds:
+        col_sum = wide_sum([send_wide(col_sum, step, width, k, 0) for k in range(1, width)], col_sum)
     new_col_state = BETA * col_state[None] + (1.0 - BETA) * (col_sum / rows_all)
     fixed = call(
         fixed_kernel,

time: 38.2 us -> 38.8 us (1.016)
  waiting for transfers between devices: 10.8 us -> 8.88 us
  starting transfers between devices: 12.3 us -> 13.6 us
  blocking collectives: 11.2 us -> 12.3 us
    ppermute x11, waiting for transfers between devices: 10.8 us -> 8.88 us  [send_to(): return lax.ppermute(x, axes, [(i, target(i)) for i in range(size)])]
    ppermute x11, starting transfers between devices: 12.3 us -> 13.6 us  [send_to(): return lax.ppermute(x, axes, [(i, target(i)) for i in range(size)])]
    all_to_all x1, blocking collectives: 11.2 us -> 12.3 us  [on_device(): sums = lax.all_to_all(message, ('dp', 'wide', 'narrow'), 0, 0, tiled=True)]
  transfers between devices with their start and end apart: 11 -> 11, of which waited for: 6 -> 5; matrix products, arithmetic and copies ran while one was open for 0% -> 0% of each run, Pallas kernels for 2% -> 2%
where the time goes in v4:
time: 38.8 us; the launch traced here: 38.6 us
  starting transfers between devices  13.6 us (35%)
  blocking collectives  12.3 us (32%)
  waiting for transfers between devices  8.88 us (23%)
  Pallas kernels  2.93 us (8%)
  between operations  0.75 us (2%)
    ppermute x11, starting transfers between devices, send_to(): return lax.ppermute(x, axes, [(i, target(i)) for i in range(size)])  13.6 us
    all_to_all x1, blocking collectives, on_device(): sums = lax.all_to_all(message, ('dp', 'wide', 'narrow'), 0, 0, tiled=True)  12.3 us
    ppermute x11, waiting for transfers between devices, send_to(): return lax.ppermute(x, axes, [(i, target(i)) for i in range(size)])  8.88 us
    pallas_call x12, Pallas kernels, call(): pl.pallas_call(kernel, out_shape=[jax.ShapeDtypeStruct(shape, jnp.float32...  2.93 us
  transfers between devices with their start and end apart: 11, of which 5 were waited for; matrix products, arithmetic and copies ran while one was open for 0% of the time, Pallas kernels for 2%

profile of v4, /device:TPU:0, one launch (start us, length us, event | category | flops | bytes accessed | tf_op | source)
XLA Modules:
  0.0 38.6 jit_solution(10960668510699041899)
XLA Ops:
  0.6 1.1 %shard_map.67 = f32[8,9216]{1,0:T(8,128)S(1)} custom-call(bf16[8,73728]{1,0:T(8,128)(2,1)} %bitcast.9), custom_call_target="tpu_custom_call" | custom-call | tf_op jit(solution)/shard_map/pallas_call | solution.py:53
  1.7 0.5 %collective-permute-start = (f32[8,9216]{1,0:T(8,128)S(1)}, f32[8,9216]{1,0:T(8,128)S(1)}, u32[]{:S(2)}, u32[]{:S(2)}) collective-permute-start(f32[8,9216]{1,0:T(8,128)S(1)} %shard_map.67), channel_id=1, source_target_pairs={{0,1},{1,0},{8,9},{9,8},{16,17},{17,16},{24,25},{25,24},{2,3},{3,2... | collective-permute-start | bytes 884744 | tf_op jit(solution)/shard_map/ppermute | solution.py:22
  2.2 0.3 collective-permute-start.4
  2.5 0.4 collective-permute-start.2
  2.9 0.5 %collective-permute-done.refs_1_ = f32[8,9216]{1,0:T(8,128)S(1)} collective-permute-done((f32[8,9216]{1,0:T(8,128)S(1)}, f32[8,9216]{1,0:T(8,128)S(1)}, u32[]{:S(2)}, u32[]{:S(2)}) %collective-permute-start) | collective-permute-done | bytes 294944 | tf_op jit(solution)/shard_map/ppermute | solution.py:22
  3.5 2.7 %collective-permute-start.1 = (f32[8,9216]{1,0:T(8,128)S(1)}, f32[8,9216]{1,0:T(8,128)S(1)}, u32[]{:S(2)}, u32[]{:S(2)}) collective-permute-start(f32[8,9216]{1,0:T(8,128)S(1)} %shard_map.68), channel_id=1, source_target_pairs={{0,17},{1,8},{8,25},{9,0},{16,1},{17,24},{24,9},{25,16},{2,19},{3,... | collective-permute-start | bytes 884744 | tf_op jit(solution)/shard_map/ppermute | solution.py:22
  6.2 0.4 %collective-permute-start.6 = (f32[8,9216]{1,0:T(8,128)S(1)}, f32[8,9216]{1,0:T(8,128)S(1)}, u32[]{:S(2)}, u32[]{:S(2)}) collective-permute-start(f32[8,9216]{1,0:T(8,128)S(1)} %shard_map.73), channel_id=1, source_target_pairs={{0,1},{1,0},{8,9},{9,8},{16,17},{17,16},{24,25},{25,24},{2,3},{3,2... | collective-permute-start | bytes 884744 | tf_op jit(solution)/shard_map/ppermute | solution.py:22
  6.6 0.0 collective-permute-done.4.refs_1_
  6.6 1.6 %collective-permute-start.5 = (f32[8,9216]{1,0:T(8,128)S(1)}, f32[8,9216]{1,0:T(8,128)S(1)}, u32[]{:S(2)}, u32[]{:S(2)}) collective-permute-start(f32[8,9216]{1,0:T(8,128)S(1)} %shard_map.72), channel_id=1, source_target_pairs={{0,16},{1,9},{8,24},{9,1},{16,0},{17,25},{24,8},{25,17},{2,18},{3,... | collective-permute-start | bytes 884744 | tf_op jit(solution)/shard_map/ppermute | solution.py:22
  8.2 2.3 %collective-permute-done.1.refs_1_ = f32[8,9216]{1,0:T(8,128)S(1)} collective-permute-done((f32[8,9216]{1,0:T(8,128)S(1)}, f32[8,9216]{1,0:T(8,128)S(1)}, u32[]{:S(2)}, u32[]{:S(2)}) %collective-permute-start.1) | collective-permute-done | bytes 294944 | tf_op jit(solution)/shard_map/ppermute | solution.py:22
  10.6 0.0 copy-start.4
  10.6 0.0 copy-start.1
  10.6 0.0 copy-start.3
  10.6 1.8 %collective-permute-start.3 = (f32[8,9216]{1,0:T(8,128)S(1)}, f32[8,9216]{1,0:T(8,128)S(1)}, u32[]{:S(2)}, u32[]{:S(2)}) collective-permute-start(f32[8,9216]{1,0:T(8,128)S(1)} %shard_map.70), channel_id=1, source_target_pairs={{0,17},{1,8},{8,25},{9,0},{16,1},{17,24},{24,9},{25,16},{2,19},{3,... | collective-permute-start | bytes 884744 | tf_op jit(solution)/shard_map/ppermute | solution.py:22
  12.4 0.0 collective-permute-done.6.refs_3_
  12.4 1.8 %collective-permute-done.5.refs_2_ = f32[8,9216]{1,0:T(8,128)S(1)} collective-permute-done((f32[8,9216]{1,0:T(8,128)S(1)}, f32[8,9216]{1,0:T(8,128)S(1)}, u32[]{:S(2)}, u32[]{:S(2)}) %collective-permute-start.5) | collective-permute-done | bytes 294944 | tf_op jit(solution)/shard_map/ppermute | solution.py:22
  14.3 2.6 %collective-permute-done.3.refs_1_ = f32[8,9216]{1,0:T(8,128)S(1)} collective-permute-done((f32[8,9216]{1,0:T(8,128)S(1)}, f32[8,9216]{1,0:T(8,128)S(1)}, u32[]{:S(2)}, u32[]{:S(2)}) %collective-permute-start.3) | collective-permute-done | bytes 294944 | tf_op jit(solution)/shard_map/ppermute | solution.py:22
  16.8 0.1 shard_map.74
  17.0 0.5 %collective-permute-start.10 = (f32[8,9216]{1,0:T(8,128)S(1)}, f32[8,9216]{1,0:T(8,128)S(1)}, u32[]{:S(2)}, u32[]{:S(2)}) collective-permute-start(f32[8,9216]{1,0:T(8,128)S(1)} %get-tuple-element.16), channel_id=1, source_target_pairs={{0,1},{1,0},{8,9},{9,8},{16,17},{17,16},{24,25},{25,24},{2,3},{3,2... | collective-permute-start | bytes 884744 | tf_op jit(solution)/shard_map/ppermute | solution.py:22
  17.5 1.8 %collective-permute-start.7 = (f32[1,9472]{1,0:T(1,128)S(1)}, f32[1,9472]{1,0:T(1,128)S(1)}, u32[]{:S(2)}, u32[]{:S(2)}) collective-permute-start(f32[1,9472]{1,0:T(1,128)S(1)} %get-tuple-element.13), channel_id=1, source_target_pairs={{0,3},{1,2},{2,5},{3,4},{4,7},{5,6},{6,1},{7,0},{8,11},{9,10},{10,... | collective-permute-start | bytes 113672 | tf_op jit(solution)/shard_map/ppermute | solution.py:22
  19.3 2.3 %collective-permute-start.9 = (f32[1,9344]{1,0:T(1,128)S(1)}, f32[1,9344]{1,0:T(1,128)S(1)}, u32[]{:S(2)}, u32[]{:S(2)}) collective-permute-start(f32[1,9344]{1,0:T(1,128)S(1)} %get-tuple-element.15), channel_id=1, source_target_pairs={{0,5},{1,4},{2,7},{3,6},{4,1},{5,0},{6,3},{7,2},{8,13},{9,12},{10,... | collective-permute-start | bytes 112136 | tf_op jit(solution)/shard_map/ppermute | solution.py:22
  21.6 1.3 %collective-permute-start.8 = (f32[1,9216]{1,0:T(1,128)S(1)}, f32[1,9216]{1,0:T(1,128)S(1)}, u32[]{:S(2)}, u32[]{:S(2)}) collective-permute-start(f32[1,9216]{1,0:T(1,128)S(1)} %get-tuple-element.14), channel_id=1, source_target_pairs={{0,7},{1,6},{2,1},{3,0},{4,3},{5,2},{6,5},{7,4},{8,15},{9,14},{10,... | collective-permute-start | bytes 110600 | tf_op jit(solution)/shard_map/ppermute | solution.py:22
  22.9 0.2 shard_map.76.fixed_in
  23.1 0.3 shard_map.75
  23.4 1.6 %collective-permute-done.8 = f32[1,9216]{1,0:T(1,128)S(1)} collective-permute-done((f32[1,9216]{1,0:T(1,128)S(1)}, f32[1,9216]{1,0:T(1,128)S(1)}, u32[]{:S(2)}, u32[]{:S(2)}) %collective-permute-start.8) | collective-permute-done | bytes 36896 | tf_op jit(solution)/shard_map/ppermute | solution.py:22
  25.0 0.0 collective-permute-done.9
  25.0 0.0 collective-permute-done.7
  25.0 0.1 multiply_add_fusion.state
  25.1 0.0 copy-start.2
  25.1 0.2 shard_map.77
  25.3 12.3 %all_to_all.11 = f32[32,1,128]{2,1,0:T(1,128)S(1)} all-to-all(f32[32,1,128]{2,1,0:T(1,128)S(1)} %bitcast.19), channel_id=1, replica_groups=mesh['dp'=4,'wide'=4,'narrow'=2] {'dp','wide','narrow'}, dimensions={0} | all-to-all | bytes 32768 | tf_op jit(solution)/shard_map/all_to_all | solution.py:277
  37.7 1.0 %shard_map.78 = (f32[8,9216]{1,0:T(8,128)}, f32[1,8]{1,0:T(1,128)}) custom-call(f32[32,128]{1,0:T(8,128)S(1)} %bitcast.18, f32[8,9216]{1,0:T(8,128)S(1)} %get-tuple-element.20.refs_1_), custom_call_target="tpu_custom_call" | custom-call | tf_op jit(solution)/shard_map/pallas_call | solution.py:53
  (15 shorter events, 0.2 us)
Async XLA Ops:
  0.6 1.6 %copy-start = (bf16[1,8,73728]{2,1,0:T(8,128)(2,1)S(1)}, bf16[1,8,73728]{2,1,0:T(8,128)(2,1)}, u32[]{:S(2)}) copy-start(bf16[1,8,73728]{2,1,0:T(8,128)(2,1)} %param.4) | copy-start | bytes 3538948
  1.7 1.7 %collective-permute-start = (f32[8,9216]{1,0:T(8,128)S(1)}, f32[8,9216]{1,0:T(8,128)S(1)}, u32[]{:S(2)}, u32[]{:S(2)}) collective-permute-start(f32[8,9216]{1,0:T(8,128)S(1)} %shard_map.67), channel_id=1, source_target_pairs={{0,1},{1,0},{8,9},{9,8},{16,17},{17,16},{24,25},{25,24},{2,3},{3,2... | collective-permute-start | bytes 884744 | tf_op jit(solution)/shard_map/ppermute | solution.py:22
  2.2 4.3 %collective-permute-start.4 = (f32[8,9216]{1,0:T(8,128)S(1)}, f32[8,9216]{1,0:T(8,128)S(1)}, u32[]{:S(2)}, u32[]{:S(2)}) collective-permute-start(f32[8,9216]{1,0:T(8,128)S(1)} %shard_map.71), channel_id=1, source_target_pairs={{0,1},{1,0},{8,9},{9,8},{16,17},{17,16},{24,25},{25,24},{2,3},{3,2... | collective-permute-start | bytes 884744 | tf_op jit(solution)/shard_map/ppermute | solution.py:22
  2.5 5.7 %collective-permute-start.2 = (f32[8,9216]{1,0:T(8,128)S(1)}, f32[8,9216]{1,0:T(8,128)S(1)}, u32[]{:S(2)}, u32[]{:S(2)}) collective-permute-start(f32[8,9216]{1,0:T(8,128)S(1)} %shard_map.69), channel_id=1, source_target_pairs={{0,1},{1,0},{8,9},{9,8},{16,17},{17,16},{24,25},{25,24},{2,3},{3,2... | collective-permute-start | bytes 884744 | tf_op jit(solution)/shard_map/ppermute | solution.py:22
  3.5 7.1 %collective-permute-start.1 = (f32[8,9216]{1,0:T(8,128)S(1)}, f32[8,9216]{1,0:T(8,128)S(1)}, u32[]{:S(2)}, u32[]{:S(2)}) collective-permute-start(f32[8,9216]{1,0:T(8,128)S(1)} %shard_map.68), channel_id=1, source_target_pairs={{0,17},{1,8},{8,25},{9,0},{16,1},{17,24},{24,9},{25,16},{2,19},{3,... | collective-permute-start | bytes 884744 | tf_op jit(solution)/shard_map/ppermute | solution.py:22
  6.2 6.3 %collective-permute-start.6 = (f32[8,9216]{1,0:T(8,128)S(1)}, f32[8,9216]{1,0:T(8,128)S(1)}, u32[]{:S(2)}, u32[]{:S(2)}) collective-permute-start(f32[8,9216]{1,0:T(8,128)S(1)} %shard_map.73), channel_id=1, source_target_pairs={{0,1},{1,0},{8,9},{9,8},{16,17},{17,16},{24,25},{25,24},{2,3},{3,2... | collective-permute-start | bytes 884744 | tf_op jit(solution)/shard_map/ppermute | solution.py:22
  6.6 7.7 %collective-permute-start.5 = (f32[8,9216]{1,0:T(8,128)S(1)}, f32[8,9216]{1,0:T(8,128)S(1)}, u32[]{:S(2)}, u32[]{:S(2)}) collective-permute-start(f32[8,9216]{1,0:T(8,128)S(1)} %shard_map.72), channel_id=1, source_target_pairs={{0,16},{1,9},{8,24},{9,1},{16,0},{17,25},{24,8},{25,17},{2,18},{3,... | collective-permute-start | bytes 884744 | tf_op jit(solution)/shard_map/ppermute | solution.py:22
  10.6 12.3 %copy-start.4 = (f32[9216]{0:T(1024)S(1)}, f32[9216]{0:T(1024)}, u32[]{:S(2)}) copy-start(f32[9216]{0:T(1024)} %param.7) | copy-start | bytes 110596
  10.6 12.3 %copy-start.1 = (bf16[8,9216]{1,0:T(8,128)(2,1)S(1)}, bf16[8,9216]{1,0:T(8,128)(2,1)}, u32[]{:S(2)}) copy-start(bf16[8,9216]{1,0:T(8,128)(2,1)} %weight.1) | copy-start | bytes 442372
  10.6 12.3 %copy-start.3 = (f32[8]{0:T(128)S(1)}, f32[8]{0:T(128)}, u32[]{:S(2)}) copy-start(f32[8]{0:T(128)} %param.6) | copy-start | bytes 100
  10.6 6.2 %collective-permute-start.3 = (f32[8,9216]{1,0:T(8,128)S(1)}, f32[8,9216]{1,0:T(8,128)S(1)}, u32[]{:S(2)}, u32[]{:S(2)}) collective-permute-start(f32[8,9216]{1,0:T(8,128)S(1)} %shard_map.70), channel_id=1, source_target_pairs={{0,17},{1,8},{8,25},{9,0},{16,1},{17,24},{24,9},{25,16},{2,19},{3,... | collective-permute-start | bytes 884744 | tf_op jit(solution)/shard_map/ppermute | solution.py:22
  17.0 6.1 %collective-permute-start.10 = (f32[8,9216]{1,0:T(8,128)S(1)}, f32[8,9216]{1,0:T(8,128)S(1)}, u32[]{:S(2)}, u32[]{:S(2)}) collective-permute-start(f32[8,9216]{1,0:T(8,128)S(1)} %get-tuple-element.16), channel_id=1, source_target_pairs={{0,1},{1,0},{8,9},{9,8},{16,17},{17,16},{24,25},{25,24},{2,3},{3,2... | collective-permute-start | bytes 884744 | tf_op jit(solution)/shard_map/ppermute | solution.py:22
  17.5 7.5 %collective-permute-start.7 = (f32[1,9472]{1,0:T(1,128)S(1)}, f32[1,9472]{1,0:T(1,128)S(1)}, u32[]{:S(2)}, u32[]{:S(2)}) collective-permute-start(f32[1,9472]{1,0:T(1,128)S(1)} %get-tuple-element.13), channel_id=1, source_target_pairs={{0,3},{1,2},{2,5},{3,4},{4,7},{5,6},{6,1},{7,0},{8,11},{9,10},{10,... | collective-permute-start | bytes 113672 | tf_op jit(solution)/shard_map/ppermute | solution.py:22
  19.3 5.7 %collective-permute-start.9 = (f32[1,9344]{1,0:T(1,128)S(1)}, f32[1,9344]{1,0:T(1,128)S(1)}, u32[]{:S(2)}, u32[]{:S(2)}) collective-permute-start(f32[1,9344]{1,0:T(1,128)S(1)} %get-tuple-element.15), channel_id=1, source_target_pairs={{0,5},{1,4},{2,7},{3,6},{4,1},{5,0},{6,3},{7,2},{8,13},{9,12},{10,... | collective-permute-start | bytes 112136 | tf_op jit(solution)/shard_map/ppermute | solution.py:22
  21.6 3.4 %collective-permute-start.8 = (f32[1,9216]{1,0:T(1,128)S(1)}, f32[1,9216]{1,0:T(1,128)S(1)}, u32[]{:S(2)}, u32[]{:S(2)}) collective-permute-start(f32[1,9216]{1,0:T(1,128)S(1)} %get-tuple-element.14), channel_id=1, source_target_pairs={{0,7},{1,6},{2,1},{3,0},{4,3},{5,2},{6,5},{7,4},{8,15},{9,14},{10,... | collective-permute-start | bytes 110600 | tf_op jit(solution)/shard_map/ppermute | solution.py:22
  25.1 13.5 %copy-start.2 = (f32[1,9216]{1,0:T(1,128)}, f32[1,9216]{1,0:T(1,128)S(1)}, u32[]{:S(2)}) copy-start(f32[1,9216]{1,0:T(1,128)S(1)} %multiply_add_fusion.state) | copy-start | bytes 110596

commit v5 on v3

--- a/solution.py
+++ b/solution.py
@@ -9,9 +9,7 @@
 STEP = 100
 BETA = 1.0 - STEP ** (-0.8)
 LANES = 128
-PIECES = 2
 VMEM = pl.BlockSpec(memory_space=pltpu.VMEM)
-HBM = pl.BlockSpec(memory_space=pltpu.HBM)
 
 
 def bits_of(size):
@@ -78,23 +76,6 @@
         reach = [sum(self.mask(core, s) for s in range(self.steps) if t >> s & 1) for core in range(2)]
         block = group ^ jnp.where(group % 2 == 1, reach[1], reach[0])
         return pl.multiple_of(block * self.cols, LANES)
-
-
-def fetch_kernel(blocks, keys, part, out, raw, sem):
-    spans, copies = [], []
-    tiles = blocks.cols // LANES
-    cuts = [tiles * i // PIECES * LANES for i in range(PIECES + 1)]
-    for i, key in enumerate(keys):
-        start = blocks.start(*key)
-        for a, b in zip(cuts, cuts[1:]):
-            spans.append(pl.ds(i * blocks.cols + a, b - a))
-            source = part.at[:, pl.ds(pl.multiple_of(start + a, LANES), b - a)]
-            copies.append(pltpu.make_async_copy(source, raw.at[:, spans[-1]], sem.at[len(copies)]))
-    for copy in copies:
-        copy.start()
-    for copy, span in zip(copies, spans):
-        copy.wait()
-        out[:, span] = raw[:, span].astype(jnp.float32)
 
 
 def load(blocks, refs, term):
@@ -189,16 +170,6 @@
     def pack(sums):
         return merge(merge_kernel, sums, [(rows, len(sums) * cols)])[0]
 
-    def fetch(keys):
-        shape = (rows, len(keys) * cols)
-        return call(
-            lambda *refs: fetch_kernel(blocks, keys, *refs),
-            [shape],
-            [HBM],
-            pltpu.with_memory_space_constraint(part, pltpu.HBM),
-            scratch=[pltpu.VMEM(shape, part.dtype), pltpu.SemaphoreType.DMA((PIECES * len(keys),))],
-        )[0]
-
     def receive(send, target):
         arrays.append(send_to(send, group_axes, size, target))
         return [(len(arrays) - 1, at) for at in range(send.shape[1] // cols)]
@@ -216,9 +187,8 @@
 
     even = [t for t in blocks.all if t and t % 2 == 0]
     groups = [ts for ts, _ in stages(0)] + [even, [0]]
-    for i, ts in enumerate(group for group in groups if group):
-        given = [(1 ^ blocks.home(t), t) for t in ts]
-        send = pack([[(0, key)] for key in given]) if i else fetch(given)
+    for ts in (group for group in groups if group):
+        send = pack([[(0, (1 ^ blocks.home(t), t))] for t in ts])
         for t, term in zip(ts, receive(send, other)):
             held[t].append(term)
     for s in range(blocks.steps):

time: 38.2 us -> 38.5 us (level)
  local copies, waits for them, and re-layouts: 0.03 us -> 1.29 us
  Pallas kernels: 2.93 us -> 1.89 us
    unnamed x10, local copies, waits for them, and re-layouts: 0.03 us -> 1.29 us
    pallas_call x12, Pallas kernels: 2.93 us -> 1.89 us  [call(): pl.pallas_call(kernel, out_shape=[jax.ShapeDtypeStruct(shape, jnp.float32...]
  transfers between devices with their start and end apart: 11 -> 11, of which waited for: 6 -> 6; matrix products, arithmetic and copies ran while one was open for 0% -> 0% of each run, Pallas kernels for 2% -> 1%
where the time goes in v5:
time: 38.5 us; the launch traced here: 38.3 us
  starting transfers between devices  12.3 us (32%)
  blocking collectives  11.2 us (29%)
  waiting for transfers between devices  10.8 us (28%)
  Pallas kernels  1.89 us (5%)
  local copies, waits for them, and re-layouts  1.29 us (3%)
  between operations  0.75 us (2%)
    ppermute x11, starting transfers between devices, send_to(): return lax.ppermute(x, axes, [(i, target(i)) for i in range(size)])  12.3 us
    all_to_all x1, blocking collectives, on_device(): sums = lax.all_to_all(message, ('dp', 'wide', 'narrow'), 0, 0, tiled=True)  11.2 us
    ppermute x11, waiting for transfers between devices, send_to(): return lax.ppermute(x, axes, [(i, target(i)) for i in range(size)])  10.8 us
    pallas_call x12, Pallas kernels, call(): pl.pallas_call(kernel, out_shape=[jax.ShapeDtypeStruct(shape, jnp.float32...  1.89 us
    unnamed x10, local copies, waits for them, and re-layouts  1.29 us
  transfers between devices with their start and end apart: 11, of which 6 were waited for; matrix products, arithmetic and copies ran while one was open for 0% of the time, Pallas kernels for 1%

profile of v5, /device:TPU:0, one launch (start us, length us, event | category | flops | bytes accessed | tf_op | source)
XLA Modules:
  0.0 38.3 jit_solution(12015240137851193472)
XLA Ops:
  0.6 1.3 %copy-done = bf16[1,8,73728]{2,1,0:T(8,128)(2,1)S(1)} copy-done((bf16[1,8,73728]{2,1,0:T(8,128)(2,1)S(1)}, bf16[1,8,73728]{2,1,0:T(8,128)(2,1)}, u32[]{:S(2)}) %copy-start) | copy-done | bytes 1179672
  1.9 0.5 %collective-permute-start = (f32[8,9216]{1,0:T(8,128)S(1)}, f32[8,9216]{1,0:T(8,128)S(1)}, u32[]{:S(2)}, u32[]{:S(2)}) collective-permute-start(f32[8,9216]{1,0:T(8,128)S(1)} %shard_map.67), channel_id=1, source_target_pairs={{0,1},{1,0},{8,9},{9,8},{16,17},{17,16},{24,25},{25,24},{2,3},{3,2... | collective-permute-start | bytes 884744 | tf_op jit(solution)/shard_map/ppermute | solution.py:20
  2.5 0.1 collective-permute-start.4
  2.6 0.5 %collective-permute-start.2 = (f32[8,9216]{1,0:T(8,128)S(1)}, f32[8,9216]{1,0:T(8,128)S(1)}, u32[]{:S(2)}, u32[]{:S(2)}) collective-permute-start(f32[8,9216]{1,0:T(8,128)S(1)} %shard_map.69), channel_id=1, source_target_pairs={{0,1},{1,0},{8,9},{9,8},{16,17},{17,16},{24,25},{25,24},{2,3},{3,2... | collective-permute-start | bytes 884744 | tf_op jit(solution)/shard_map/ppermute | solution.py:20
  3.1 0.5 %collective-permute-done.refs_1_ = f32[8,9216]{1,0:T(8,128)S(1)} collective-permute-done((f32[8,9216]{1,0:T(8,128)S(1)}, f32[8,9216]{1,0:T(8,128)S(1)}, u32[]{:S(2)}, u32[]{:S(2)}) %collective-permute-start) | collective-permute-done | bytes 294944 | tf_op jit(solution)/shard_map/ppermute | solution.py:20
  3.7 2.7 %collective-permute-start.1 = (f32[8,9216]{1,0:T(8,128)S(1)}, f32[8,9216]{1,0:T(8,128)S(1)}, u32[]{:S(2)}, u32[]{:S(2)}) collective-permute-start(f32[8,9216]{1,0:T(8,128)S(1)} %shard_map.68), channel_id=1, source_target_pairs={{0,17},{1,8},{8,25},{9,0},{16,1},{17,24},{24,9},{25,16},{2,19},{3,... | collective-permute-start | bytes 884744 | tf_op jit(solution)/shard_map/ppermute | solution.py:20
  6.4 0.4 %collective-permute-start.6 = (f32[8,9216]{1,0:T(8,128)S(1)}, f32[8,9216]{1,0:T(8,128)S(1)}, u32[]{:S(2)}, u32[]{:S(2)}) collective-permute-start(f32[8,9216]{1,0:T(8,128)S(1)} %shard_map.73), channel_id=1, source_target_pairs={{0,1},{1,0},{8,9},{9,8},{16,17},{17,16},{24,25},{25,24},{2,3},{3,2... | collective-permute-start | bytes 884744 | tf_op jit(solution)/shard_map/ppermute | solution.py:20
  6.8 0.0 collective-permute-done.4.refs_1_
  6.8 1.6 %collective-permute-start.5 = (f32[8,9216]{1,0:T(8,128)S(1)}, f32[8,9216]{1,0:T(8,128)S(1)}, u32[]{:S(2)}, u32[]{:S(2)}) collective-permute-start(f32[8,9216]{1,0:T(8,128)S(1)} %shard_map.72), channel_id=1, source_target_pairs={{0,16},{1,9},{8,24},{9,1},{16,0},{17,25},{24,8},{25,17},{2,18},{3,... | collective-permute-start | bytes 884744 | tf_op jit(solution)/shard_map/ppermute | solution.py:20
  8.4 0.0 collective-permute-done.2.refs_2_
  8.4 2.3 %collective-permute-done.1.refs_1_ = f32[8,9216]{1,0:T(8,128)S(1)} collective-permute-done((f32[8,9216]{1,0:T(8,128)S(1)}, f32[8,9216]{1,0:T(8,128)S(1)}, u32[]{:S(2)}, u32[]{:S(2)}) %collective-permute-start.1) | collective-permute-done | bytes 294944 | tf_op jit(solution)/shard_map/ppermute | solution.py:20
  10.8 0.0 copy-start.4
  10.8 0.0 copy-start.1
  10.8 0.0 copy-start.3
  10.8 1.8 %collective-permute-start.3 = (f32[8,9216]{1,0:T(8,128)S(1)}, f32[8,9216]{1,0:T(8,128)S(1)}, u32[]{:S(2)}, u32[]{:S(2)}) collective-permute-start(f32[8,9216]{1,0:T(8,128)S(1)} %shard_map.70), channel_id=1, source_target_pairs={{0,17},{1,8},{8,25},{9,0},{16,1},{17,24},{24,9},{25,16},{2,19},{3,... | collective-permute-start | bytes 884744 | tf_op jit(solution)/shard_map/ppermute | solution.py:20
  12.6 0.0 collective-permute-done.6.refs_3_
  12.6 1.8 %collective-permute-done.5.refs_2_ = f32[8,9216]{1,0:T(8,128)S(1)} collective-permute-done((f32[8,9216]{1,0:T(8,128)S(1)}, f32[8,9216]{1,0:T(8,128)S(1)}, u32[]{:S(2)}, u32[]{:S(2)}) %collective-permute-start.5) | collective-permute-done | bytes 294944 | tf_op jit(solution)/shard_map/ppermute | solution.py:20
  14.5 2.6 %collective-permute-done.3.refs_1_ = f32[8,9216]{1,0:T(8,128)S(1)} collective-permute-done((f32[8,9216]{1,0:T(8,128)S(1)}, f32[8,9216]{1,0:T(8,128)S(1)}, u32[]{:S(2)}, u32[]{:S(2)}) %collective-permute-start.3) | collective-permute-done | bytes 294944 | tf_op jit(solution)/shard_map/ppermute | solution.py:20
  17.1 0.1 shard_map.74
  17.2 0.5 %collective-permute-start.10 = (f32[8,9216]{1,0:T(8,128)S(1)}, f32[8,9216]{1,0:T(8,128)S(1)}, u32[]{:S(2)}, u32[]{:S(2)}) collective-permute-start(f32[8,9216]{1,0:T(8,128)S(1)} %get-tuple-element.16), channel_id=1, source_target_pairs={{0,1},{1,0},{8,9},{9,8},{16,17},{17,16},{24,25},{25,24},{2,3},{3,2... | collective-permute-start | bytes 884744 | tf_op jit(solution)/shard_map/ppermute | solution.py:20
  17.7 3.8 %collective-permute-start.7 = (f32[1,9472]{1,0:T(1,128)S(1)}, f32[1,9472]{1,0:T(1,128)S(1)}, u32[]{:S(2)}, u32[]{:S(2)}) collective-permute-start(f32[1,9472]{1,0:T(1,128)S(1)} %get-tuple-element.13), channel_id=1, source_target_pairs={{0,7},{1,6},{2,5},{3,4},{4,3},{5,2},{6,1},{7,0},{8,15},{9,14},{10,... | collective-permute-start | bytes 113672 | tf_op jit(solution)/shard_map/ppermute | solution.py:20
  21.5 0.0 collective-permute-start.8
  21.5 0.3 collective-permute-start.9
  21.9 0.2 shard_map.76.fixed_in
  22.0 0.3 shard_map.75
  22.3 2.7 %collective-permute-done.9 = f32[1,9216]{1,0:T(1,128)S(1)} collective-permute-done((f32[1,9216]{1,0:T(1,128)S(1)}, f32[1,9216]{1,0:T(1,128)S(1)}, u32[]{:S(2)}, u32[]{:S(2)}) %collective-permute-start.9) | collective-permute-done | bytes 36896 | tf_op jit(solution)/shard_map/ppermute | solution.py:20
  25.0 0.9 %collective-permute-done.8 = f32[1,9344]{1,0:T(1,128)S(1)} collective-permute-done((f32[1,9344]{1,0:T(1,128)S(1)}, f32[1,9344]{1,0:T(1,128)S(1)}, u32[]{:S(2)}, u32[]{:S(2)}) %collective-permute-start.8) | collective-permute-done | bytes 37408 | tf_op jit(solution)/shard_map/ppermute | solution.py:20
  25.9 0.1 multiply_add_fusion.state
  26.0 0.0 copy-start.2
  26.0 0.2 shard_map.77
  26.2 11.2 %all_to_all.11 = f32[32,1,128]{2,1,0:T(1,128)S(1)} all-to-all(f32[32,1,128]{2,1,0:T(1,128)S(1)} %bitcast.19), channel_id=1, replica_groups=mesh['dp'=4,'wide'=4,'narrow'=2] {'dp','wide','narrow'}, dimensions={0} | all-to-all | bytes 32768 | tf_op jit(solution)/shard_map/all_to_all | solution.py:234
  37.3 1.0 %shard_map.78 = (f32[8,9216]{1,0:T(8,128)}, f32[1,8]{1,0:T(1,128)}) custom-call(f32[32,128]{1,0:T(8,128)S(1)} %bitcast.18, f32[8,9216]{1,0:T(8,128)S(1)} %get-tuple-element.20.refs_1_), custom_call_target="tpu_custom_call" | custom-call | tf_op jit(solution)/shard_map/pallas_call | solution.py:44
  (15 shorter events, 0.2 us)
Async XLA Ops:
  0.6 1.3 %copy-start = (bf16[1,8,73728]{2,1,0:T(8,128)(2,1)S(1)}, bf16[1,8,73728]{2,1,0:T(8,128)(2,1)}, u32[]{:S(2)}) copy-start(bf16[1,8,73728]{2,1,0:T(8,128)(2,1)} %param.4) | copy-start | bytes 3538948
  1.9 1.7 %collective-permute-start = (f32[8,9216]{1,0:T(8,128)S(1)}, f32[8,9216]{1,0:T(8,128)S(1)}, u32[]{:S(2)}, u32[]{:S(2)}) collective-permute-start(f32[8,9216]{1,0:T(8,128)S(1)} %shard_map.67), channel_id=1, source_target_pairs={{0,1},{1,0},{8,9},{9,8},{16,17},{17,16},{24,25},{25,24},{2,3},{3,2... | collective-permute-start | bytes 884744 | tf_op jit(solution)/shard_map/ppermute | solution.py:20
  2.5 4.3 %collective-permute-start.4 = (f32[8,9216]{1,0:T(8,128)S(1)}, f32[8,9216]{1,0:T(8,128)S(1)}, u32[]{:S(2)}, u32[]{:S(2)}) collective-permute-start(f32[8,9216]{1,0:T(8,128)S(1)} %shard_map.71), channel_id=1, source_target_pairs={{0,1},{1,0},{8,9},{9,8},{16,17},{17,16},{24,25},{25,24},{2,3},{3,2... | collective-permute-start | bytes 884744 | tf_op jit(solution)/shard_map/ppermute | solution.py:20
  2.6 5.8 %collective-permute-start.2 = (f32[8,9216]{1,0:T(8,128)S(1)}, f32[8,9216]{1,0:T(8,128)S(1)}, u32[]{:S(2)}, u32[]{:S(2)}) collective-permute-start(f32[8,9216]{1,0:T(8,128)S(1)} %shard_map.69), channel_id=1, source_target_pairs={{0,1},{1,0},{8,9},{9,8},{16,17},{17,16},{24,25},{25,24},{2,3},{3,2... | collective-permute-start | bytes 884744 | tf_op jit(solution)/shard_map/ppermute | solution.py:20
  3.7 7.1 %collective-permute-start.1 = (f32[8,9216]{1,0:T(8,128)S(1)}, f32[8,9216]{1,0:T(8,128)S(1)}, u32[]{:S(2)}, u32[]{:S(2)}) collective-permute-start(f32[8,9216]{1,0:T(8,128)S(1)} %shard_map.68), channel_id=1, source_target_pairs={{0,17},{1,8},{8,25},{9,0},{16,1},{17,24},{24,9},{25,16},{2,19},{3,... | collective-permute-start | bytes 884744 | tf_op jit(solution)/shard_map/ppermute | solution.py:20
  6.4 6.3 %collective-permute-start.6 = (f32[8,9216]{1,0:T(8,128)S(1)}, f32[8,9216]{1,0:T(8,128)S(1)}, u32[]{:S(2)}, u32[]{:S(2)}) collective-permute-start(f32[8,9216]{1,0:T(8,128)S(1)} %shard_map.73), channel_id=1, source_target_pairs={{0,1},{1,0},{8,9},{9,8},{16,17},{17,16},{24,25},{25,24},{2,3},{3,2... | collective-permute-start | bytes 884744 | tf_op jit(solution)/shard_map/ppermute | solution.py:20
  6.8 7.7 %collective-permute-start.5 = (f32[8,9216]{1,0:T(8,128)S(1)}, f32[8,9216]{1,0:T(8,128)S(1)}, u32[]{:S(2)}, u32[]{:S(2)}) collective-permute-start(f32[8,9216]{1,0:T(8,128)S(1)} %shard_map.72), channel_id=1, source_target_pairs={{0,16},{1,9},{8,24},{9,1},{16,0},{17,25},{24,8},{25,17},{2,18},{3,... | collective-permute-start | bytes 884744 | tf_op jit(solution)/shard_map/ppermute | solution.py:20
  10.8 11.0 %copy-start.4 = (f32[9216]{0:T(1024)S(1)}, f32[9216]{0:T(1024)}, u32[]{:S(2)}) copy-start(f32[9216]{0:T(1024)} %param.7) | copy-start | bytes 110596
  10.8 11.0 %copy-start.1 = (bf16[8,9216]{1,0:T(8,128)(2,1)S(1)}, bf16[8,9216]{1,0:T(8,128)(2,1)}, u32[]{:S(2)}) copy-start(bf16[8,9216]{1,0:T(8,128)(2,1)} %weight.1) | copy-start | bytes 442372
  10.8 11.0 %copy-start.3 = (f32[8]{0:T(128)S(1)}, f32[8]{0:T(128)}, u32[]{:S(2)}) copy-start(f32[8]{0:T(128)} %param.6) | copy-start | bytes 100
  10.8 6.2 %collective-permute-start.3 = (f32[8,9216]{1,0:T(8,128)S(1)}, f32[8,9216]{1,0:T(8,128)S(1)}, u32[]{:S(2)}, u32[]{:S(2)}) collective-permute-start(f32[8,9216]{1,0:T(8,128)S(1)} %shard_map.70), channel_id=1, source_target_pairs={{0,17},{1,8},{8,25},{9,0},{16,1},{17,24},{24,9},{25,16},{2,19},{3,... | collective-permute-start | bytes 884744 | tf_op jit(solution)/shard_map/ppermute | solution.py:20
  17.2 4.8 %collective-permute-start.10 = (f32[8,9216]{1,0:T(8,128)S(1)}, f32[8,9216]{1,0:T(8,128)S(1)}, u32[]{:S(2)}, u32[]{:S(2)}) collective-permute-start(f32[8,9216]{1,0:T(8,128)S(1)} %get-tuple-element.16), channel_id=1, source_target_pairs={{0,1},{1,0},{8,9},{9,8},{16,17},{17,16},{24,25},{25,24},{2,3},{3,2... | collective-permute-start | bytes 884744 | tf_op jit(solution)/shard_map/ppermute | solution.py:20
  17.7 8.2 %collective-permute-start.7 = (f32[1,9472]{1,0:T(1,128)S(1)}, f32[1,9472]{1,0:T(1,128)S(1)}, u32[]{:S(2)}, u32[]{:S(2)}) collective-permute-start(f32[1,9472]{1,0:T(1,128)S(1)} %get-tuple-element.13), channel_id=1, source_target_pairs={{0,7},{1,6},{2,5},{3,4},{4,3},{5,2},{6,1},{7,0},{8,15},{9,14},{10,... | collective-permute-start | bytes 113672 | tf_op jit(solution)/shard_map/ppermute | solution.py:20
  21.5 4.4 %collective-permute-start.8 = (f32[1,9344]{1,0:T(1,128)S(1)}, f32[1,9344]{1,0:T(1,128)S(1)}, u32[]{:S(2)}, u32[]{:S(2)}) collective-permute-start(f32[1,9344]{1,0:T(1,128)S(1)} %get-tuple-element.14), channel_id=1, source_target_pairs={{0,5},{1,4},{2,7},{3,6},{4,1},{5,0},{6,3},{7,2},{8,13},{9,12},{10,... | collective-permute-start | bytes 112136 | tf_op jit(solution)/shard_map/ppermute | solution.py:20
  21.5 3.4 %collective-permute-start.9 = (f32[1,9216]{1,0:T(1,128)S(1)}, f32[1,9216]{1,0:T(1,128)S(1)}, u32[]{:S(2)}, u32[]{:S(2)}) collective-permute-start(f32[1,9216]{1,0:T(1,128)S(1)} %get-tuple-element.15), channel_id=1, source_target_pairs={{0,3},{1,2},{2,1},{3,0},{4,7},{5,6},{6,5},{7,4},{8,11},{9,10},{10,... | collective-permute-start | bytes 110600 | tf_op jit(solution)/shard_map/ppermute | solution.py:20
  26.0 12.3 %copy-start.2 = (f32[1,9216]{1,0:T(1,128)}, f32[1,9216]{1,0:T(1,128)S(1)}, u32[]{:S(2)}) copy-start(f32[1,9216]{1,0:T(1,128)S(1)} %multiply_add_fusion.state) | copy-start | bytes 110596

commit v6 on v3

--- a/solution.py
+++ b/solution.py
@@ -122,12 +122,6 @@
             col_out[:, cols:] = jnp.zeros((1, col_out.shape[1] - cols), jnp.float32)
 
 
-def square_kernel(grad_in, col_out, row_out):
-    square = grad_in[...] * grad_in[...] + 1e-30
-    col_out[...] = jnp.sum(square, axis=0, keepdims=True)
-    row_out[...] = to_lanes(jnp.sum(square, axis=1, keepdims=True), 0)
-
-
 def fixed_kernel(weight, row_state, out, line):
     rows = weight.shape[0]
     squares = []
@@ -142,12 +136,13 @@
     out[...] = jnp.where(iota(1, 1) == 3 * rows, squares, state)
 
 
-def column_kernel(state, grad_in, row_in, fixed_in, grad_out, message_out):
+def column_kernel(state, grad_in, fixed_in, grad_out, message_out):
     rows = grad_in.shape[0]
+    row = jnp.sum(grad_in[...] * grad_in[...] + 1e-30, axis=1, keepdims=True)
     grad = grad_in[...] * lax.rsqrt(state[...])
     grad_out[...] = grad
     quot = jnp.sum(grad * grad, axis=1, keepdims=True)
-    message = row_in[...] + fixed_in[...] + to_lanes(quot, rows)
+    message = to_lanes(row, 0) + fixed_in[...] + to_lanes(quot, rows)
     message_out[...] = jnp.broadcast_to(message, message_out.shape)
 
 
@@ -231,7 +226,7 @@
     grad, *sends = merge(
         lambda *refs: grad_kernel(inputs, *refs),
         [held[0]],
-        [(rows, cols)] + [(1, cols + LANES * (len(first) - 1 - i)) for i in range(len(first))],
+        [(rows, cols)] + [(1, cols + LANES * (len(first) - i)) for i in range(len(first) + 1)],
     )
 
     def send_wide(x, mask):
@@ -239,8 +234,7 @@
 
     terms = [send_wide(x, mask * narrow ^ 1)[:, :cols] for x, mask in zip(sends, first)]
     grad = send_to(grad, group_axes, size, other)
-    col_sum, row_part = call(square_kernel, [(1, cols), (1, LANES)], [VMEM], grad)
-    col_sum = tree(terms + [col_sum])
+    col_sum = tree(terms + [send_to(sends[-1], group_axes, size, other)])
     for masks in rounds:
         col_sum = tree([send_wide(col_sum, mask * narrow) for mask in masks] + [col_sum])
     new_col_state = BETA * col_state[None] + (1.0 - BETA) * (col_sum / rows_all)
@@ -257,8 +251,8 @@
     grad, message = call(
         column_kernel,
         [(rows, cols), (group, LANES)],
-        [VMEM] * 4,
-        new_col_state, grad, row_part, fixed,
+        [VMEM] * 3,
+        new_col_state, grad, fixed,
     )
     if single:
         sums = lax.all_to_all(message, ("dp", "wide", "narrow"), 0, 0, tiled=True)

time: 38.2 us -> 38.1 us (level)
  waiting for transfers between devices: 10.8 us -> 10.2 us
  starting transfers between devices: 12.3 us -> 12.8 us
    ppermute x11 -> x12, waiting for transfers between devices: 10.8 us -> 10.2 us  [send_to(): return lax.ppermute(x, axes, [(i, target(i)) for i in range(size)])]
    ppermute x11 -> x12, starting transfers between devices: 12.3 us -> 12.8 us  [send_to(): return lax.ppermute(x, axes, [(i, target(i)) for i in range(size)])]
    pallas_call x12 -> x11, Pallas kernels: 2.93 us -> 2.7 us  [call(): pl.pallas_call(kernel, out_shape=[jax.ShapeDtypeStruct(shape, jnp.float32...]
  transfers between devices with their start and end apart: 11 -> 12, of which waited for: 6 -> 7; matrix products, arithmetic and copies ran while one was open for 0% -> 0% of each run, Pallas kernels for 2% -> 1%
where the time goes in v6:
time: 38.1 us; the launch traced here: 37.9 us
  starting transfers between devices  12.8 us (34%)
  blocking collectives  11.4 us (30%)
  waiting for transfers between devices  10.2 us (27%)
  Pallas kernels  2.7 us (7%)
  between operations  0.75 us (2%)
    ppermute x12, starting transfers between devices, send_to(): return lax.ppermute(x, axes, [(i, target(i)) for i in range(size)])  12.8 us
    all_to_all x1, blocking collectives, on_device(): sums = lax.all_to_all(message, ('dp', 'wide', 'narrow'), 0, 0, tiled=True)  11.4 us
    ppermute x12, waiting for transfers between devices, send_to(): return lax.ppermute(x, axes, [(i, target(i)) for i in range(size)])  10.2 us
    pallas_call x11, Pallas kernels, call(): pl.pallas_call(kernel, out_shape=[jax.ShapeDtypeStruct(shape, jnp.float32...  2.7 us
  transfers between devices with their start and end apart: 12, of which 7 were waited for; matrix products, arithmetic and copies ran while one was open for 0% of the time, Pallas kernels for 1%

profile of v6, /device:TPU:0, one launch (start us, length us, event | category | flops | bytes accessed | tf_op | source)
XLA Modules:
  0.0 37.9 jit_solution(7002496377350185932)
XLA Ops:
  0.6 1.1 %shard_map.67 = f32[8,9216]{1,0:T(8,128)S(1)} custom-call(bf16[8,73728]{1,0:T(8,128)(2,1)} %bitcast.9), custom_call_target="tpu_custom_call" | custom-call | tf_op jit(solution)/shard_map/pallas_call | solution.py:46
  1.7 0.5 %collective-permute-start = (f32[8,9216]{1,0:T(8,128)S(1)}, f32[8,9216]{1,0:T(8,128)S(1)}, u32[]{:S(2)}, u32[]{:S(2)}) collective-permute-start(f32[8,9216]{1,0:T(8,128)S(1)} %shard_map.67), channel_id=1, source_target_pairs={{0,1},{1,0},{8,9},{9,8},{16,17},{17,16},{24,25},{25,24},{2,3},{3,2... | collective-permute-start | bytes 884744 | tf_op jit(solution)/shard_map/ppermute | solution.py:22
  2.2 0.3 collective-permute-start.4
  2.5 0.4 collective-permute-start.2
  2.9 0.5 %collective-permute-done.refs_1_ = f32[8,9216]{1,0:T(8,128)S(1)} collective-permute-done((f32[8,9216]{1,0:T(8,128)S(1)}, f32[8,9216]{1,0:T(8,128)S(1)}, u32[]{:S(2)}, u32[]{:S(2)}) %collective-permute-start) | collective-permute-done | bytes 294944 | tf_op jit(solution)/shard_map/ppermute | solution.py:22
  3.5 2.7 %collective-permute-start.1 = (f32[8,9216]{1,0:T(8,128)S(1)}, f32[8,9216]{1,0:T(8,128)S(1)}, u32[]{:S(2)}, u32[]{:S(2)}) collective-permute-start(f32[8,9216]{1,0:T(8,128)S(1)} %shard_map.68), channel_id=1, source_target_pairs={{0,17},{1,8},{8,25},{9,0},{16,1},{17,24},{24,9},{25,16},{2,19},{3,... | collective-permute-start | bytes 884744 | tf_op jit(solution)/shard_map/ppermute | solution.py:22
  6.2 0.4 %collective-permute-start.6 = (f32[8,9216]{1,0:T(8,128)S(1)}, f32[8,9216]{1,0:T(8,128)S(1)}, u32[]{:S(2)}, u32[]{:S(2)}) collective-permute-start(f32[8,9216]{1,0:T(8,128)S(1)} %shard_map.73), channel_id=1, source_target_pairs={{0,1},{1,0},{8,9},{9,8},{16,17},{17,16},{24,25},{25,24},{2,3},{3,2... | collective-permute-start | bytes 884744 | tf_op jit(solution)/shard_map/ppermute | solution.py:22
  6.6 0.0 collective-permute-done.4.refs_1_
  6.6 1.6 %collective-permute-start.5 = (f32[8,9216]{1,0:T(8,128)S(1)}, f32[8,9216]{1,0:T(8,128)S(1)}, u32[]{:S(2)}, u32[]{:S(2)}) collective-permute-start(f32[8,9216]{1,0:T(8,128)S(1)} %shard_map.72), channel_id=1, source_target_pairs={{0,16},{1,9},{8,24},{9,1},{16,0},{17,25},{24,8},{25,17},{2,18},{3,... | collective-permute-start | bytes 884744 | tf_op jit(solution)/shard_map/ppermute | solution.py:22
  8.2 0.0 collective-permute-done.2.refs_2_
  8.2 2.3 %collective-permute-done.1.refs_1_ = f32[8,9216]{1,0:T(8,128)S(1)} collective-permute-done((f32[8,9216]{1,0:T(8,128)S(1)}, f32[8,9216]{1,0:T(8,128)S(1)}, u32[]{:S(2)}, u32[]{:S(2)}) %collective-permute-start.1) | collective-permute-done | bytes 294944 | tf_op jit(solution)/shard_map/ppermute | solution.py:22
  10.6 0.0 copy-start.4
  10.6 0.0 copy-start.1
  10.6 0.0 copy-start.3
  10.6 1.8 %collective-permute-start.3 = (f32[8,9216]{1,0:T(8,128)S(1)}, f32[8,9216]{1,0:T(8,128)S(1)}, u32[]{:S(2)}, u32[]{:S(2)}) collective-permute-start(f32[8,9216]{1,0:T(8,128)S(1)} %shard_map.70), channel_id=1, source_target_pairs={{0,17},{1,8},{8,25},{9,0},{16,1},{17,24},{24,9},{25,16},{2,19},{3,... | collective-permute-start | bytes 884744 | tf_op jit(solution)/shard_map/ppermute | solution.py:22
  12.4 1.8 %collective-permute-done.5.refs_2_ = f32[8,9216]{1,0:T(8,128)S(1)} collective-permute-done((f32[8,9216]{1,0:T(8,128)S(1)}, f32[8,9216]{1,0:T(8,128)S(1)}, u32[]{:S(2)}, u32[]{:S(2)}) %collective-permute-start.5) | collective-permute-done | bytes 294944 | tf_op jit(solution)/shard_map/ppermute | solution.py:22
  14.3 2.6 %collective-permute-done.3.refs_1_ = f32[8,9216]{1,0:T(8,128)S(1)} collective-permute-done((f32[8,9216]{1,0:T(8,128)S(1)}, f32[8,9216]{1,0:T(8,128)S(1)}, u32[]{:S(2)}, u32[]{:S(2)}) %collective-permute-start.3) | collective-permute-done | bytes 294944 | tf_op jit(solution)/shard_map/ppermute | solution.py:22
  16.8 0.1 shard_map.74
  17.0 3.9 %collective-permute-start.7 = (f32[1,9600]{1,0:T(1,128)S(1)}, f32[1,9600]{1,0:T(1,128)S(1)}, u32[]{:S(2)}, u32[]{:S(2)}) collective-permute-start(f32[1,9600]{1,0:T(1,128)S(1)} %get-tuple-element.12), channel_id=1, source_target_pairs={{0,7},{1,6},{2,5},{3,4},{4,3},{5,2},{6,1},{7,0},{8,15},{9,14},{10,... | collective-permute-start | bytes 115208 | tf_op jit(solution)/shard_map/ppermute | solution.py:22
  20.9 0.0 collective-permute-start.8
  20.9 0.6 %collective-permute-start.9 = (f32[1,9344]{1,0:T(1,128)S(1)}, f32[1,9344]{1,0:T(1,128)S(1)}, u32[]{:S(2)}, u32[]{:S(2)}) collective-permute-start(f32[1,9344]{1,0:T(1,128)S(1)} %get-tuple-element.14), channel_id=1, source_target_pairs={{0,3},{1,2},{2,1},{3,0},{4,7},{5,6},{6,5},{7,4},{8,11},{9,10},{10,... | collective-permute-start | bytes 112136 | tf_op jit(solution)/shard_map/ppermute | solution.py:22
  21.5 0.2 collective-permute-start.10
  21.7 0.2 shard_map.75.fixed_in
  21.9 0.4 %collective-permute-start.11 = (f32[8,9216]{1,0:T(8,128)S(1)}, f32[8,9216]{1,0:T(8,128)S(1)}, u32[]{:S(2)}, u32[]{:S(2)}) collective-permute-start(f32[8,9216]{1,0:T(8,128)S(1)} %get-tuple-element.16), channel_id=1, source_target_pairs={{0,1},{1,0},{8,9},{9,8},{16,17},{17,16},{24,25},{25,24},{2,3},{3,2... | collective-permute-start | bytes 884744 | tf_op jit(solution)/shard_map/ppermute | solution.py:22
  22.3 0.4 %collective-permute-done.10 = f32[1,9216]{1,0:T(1,128)S(1)} collective-permute-done((f32[1,9216]{1,0:T(1,128)S(1)}, f32[1,9216]{1,0:T(1,128)S(1)}, u32[]{:S(2)}, u32[]{:S(2)}) %collective-permute-start.10) | collective-permute-done | bytes 36896 | tf_op jit(solution)/shard_map/ppermute | solution.py:22
  22.8 1.6 %collective-permute-done.9 = f32[1,9344]{1,0:T(1,128)S(1)} collective-permute-done((f32[1,9344]{1,0:T(1,128)S(1)}, f32[1,9344]{1,0:T(1,128)S(1)}, u32[]{:S(2)}, u32[]{:S(2)}) %collective-permute-start.9) | collective-permute-done | bytes 37408 | tf_op jit(solution)/shard_map/ppermute | solution.py:22
  24.3 0.9 %collective-permute-done.8 = f32[1,9472]{1,0:T(1,128)S(1)} collective-permute-done((f32[1,9472]{1,0:T(1,128)S(1)}, f32[1,9472]{1,0:T(1,128)S(1)}, u32[]{:S(2)}, u32[]{:S(2)}) %collective-permute-start.8) | collective-permute-done | bytes 37920 | tf_op jit(solution)/shard_map/ppermute | solution.py:22
  25.3 0.1 multiply_add_fusion.state
  25.4 0.0 copy-start.2
  25.4 0.2 shard_map.76
  25.6 11.4 %all_to_all.11 = f32[32,1,128]{2,1,0:T(1,128)S(1)} all-to-all(f32[32,1,128]{2,1,0:T(1,128)S(1)} %bitcast.19), channel_id=1, replica_groups=mesh['dp'=4,'wide'=4,'narrow'=2] {'dp','wide','narrow'}, dimensions={0} | all-to-all | bytes 32768 | tf_op jit(solution)/shard_map/all_to_all | solution.py:258
  37.0 1.0 %shard_map.77 = (f32[8,9216]{1,0:T(8,128)}, f32[1,8]{1,0:T(1,128)}) custom-call(f32[32,128]{1,0:T(8,128)S(1)} %bitcast.18, f32[8,9216]{1,0:T(8,128)S(1)} %get-tuple-element.18.refs_1_), custom_call_target="tpu_custom_call" | custom-call | tf_op jit(solution)/shard_map/pallas_call | solution.py:46
  (16 shorter events, 0.2 us)
Async XLA Ops:
  0.6 1.6 %copy-start = (bf16[1,8,73728]{2,1,0:T(8,128)(2,1)S(1)}, bf16[1,8,73728]{2,1,0:T(8,128)(2,1)}, u32[]{:S(2)}) copy-start(bf16[1,8,73728]{2,1,0:T(8,128)(2,1)} %param.4) | copy-start | bytes 3538948
  1.7 1.7 %collective-permute-start = (f32[8,9216]{1,0:T(8,128)S(1)}, f32[8,9216]{1,0:T(8,128)S(1)}, u32[]{:S(2)}, u32[]{:S(2)}) collective-permute-start(f32[8,9216]{1,0:T(8,128)S(1)} %shard_map.67), channel_id=1, source_target_pairs={{0,1},{1,0},{8,9},{9,8},{16,17},{17,16},{24,25},{25,24},{2,3},{3,2... | collective-permute-start | bytes 884744 | tf_op jit(solution)/shard_map/ppermute | solution.py:22
  2.2 4.3 %collective-permute-start.4 = (f32[8,9216]{1,0:T(8,128)S(1)}, f32[8,9216]{1,0:T(8,128)S(1)}, u32[]{:S(2)}, u32[]{:S(2)}) collective-permute-start(f32[8,9216]{1,0:T(8,128)S(1)} %shard_map.71), channel_id=1, source_target_pairs={{0,1},{1,0},{8,9},{9,8},{16,17},{17,16},{24,25},{25,24},{2,3},{3,2... | collective-permute-start | bytes 884744 | tf_op jit(solution)/shard_map/ppermute | solution.py:22
  2.5 5.7 %collective-permute-start.2 = (f32[8,9216]{1,0:T(8,128)S(1)}, f32[8,9216]{1,0:T(8,128)S(1)}, u32[]{:S(2)}, u32[]{:S(2)}) collective-permute-start(f32[8,9216]{1,0:T(8,128)S(1)} %shard_map.69), channel_id=1, source_target_pairs={{0,1},{1,0},{8,9},{9,8},{16,17},{17,16},{24,25},{25,24},{2,3},{3,2... | collective-permute-start | bytes 884744 | tf_op jit(solution)/shard_map/ppermute | solution.py:22
  3.5 7.1 %collective-permute-start.1 = (f32[8,9216]{1,0:T(8,128)S(1)}, f32[8,9216]{1,0:T(8,128)S(1)}, u32[]{:S(2)}, u32[]{:S(2)}) collective-permute-start(f32[8,9216]{1,0:T(8,128)S(1)} %shard_map.68), channel_id=1, source_target_pairs={{0,17},{1,8},{8,25},{9,0},{16,1},{17,24},{24,9},{25,16},{2,19},{3,... | collective-permute-start | bytes 884744 | tf_op jit(solution)/shard_map/ppermute | solution.py:22
  6.2 6.3 %collective-permute-start.6 = (f32[8,9216]{1,0:T(8,128)S(1)}, f32[8,9216]{1,0:T(8,128)S(1)}, u32[]{:S(2)}, u32[]{:S(2)}) collective-permute-start(f32[8,9216]{1,0:T(8,128)S(1)} %shard_map.73), channel_id=1, source_target_pairs={{0,1},{1,0},{8,9},{9,8},{16,17},{17,16},{24,25},{25,24},{2,3},{3,2... | collective-permute-start | bytes 884744 | tf_op jit(solution)/shard_map/ppermute | solution.py:22
  6.6 7.6 %collective-permute-start.5 = (f32[8,9216]{1,0:T(8,128)S(1)}, f32[8,9216]{1,0:T(8,128)S(1)}, u32[]{:S(2)}, u32[]{:S(2)}) collective-permute-start(f32[8,9216]{1,0:T(8,128)S(1)} %shard_map.72), channel_id=1, source_target_pairs={{0,16},{1,9},{8,24},{9,1},{16,0},{17,25},{24,8},{25,17},{2,18},{3,... | collective-permute-start | bytes 884744 | tf_op jit(solution)/shard_map/ppermute | solution.py:22
  10.6 11.1 %copy-start.4 = (f32[9216]{0:T(1024)S(1)}, f32[9216]{0:T(1024)}, u32[]{:S(2)}) copy-start(f32[9216]{0:T(1024)} %param.7) | copy-start | bytes 110596
  10.6 11.1 %copy-start.1 = (bf16[8,9216]{1,0:T(8,128)(2,1)S(1)}, bf16[8,9216]{1,0:T(8,128)(2,1)}, u32[]{:S(2)}) copy-start(bf16[8,9216]{1,0:T(8,128)(2,1)} %weight.1) | copy-start | bytes 442372
  10.6 11.1 %copy-start.3 = (f32[8]{0:T(128)S(1)}, f32[8]{0:T(128)}, u32[]{:S(2)}) copy-start(f32[8]{0:T(128)} %param.6) | copy-start | bytes 100
  10.6 6.2 %collective-permute-start.3 = (f32[8,9216]{1,0:T(8,128)S(1)}, f32[8,9216]{1,0:T(8,128)S(1)}, u32[]{:S(2)}, u32[]{:S(2)}) collective-permute-start(f32[8,9216]{1,0:T(8,128)S(1)} %shard_map.70), channel_id=1, source_target_pairs={{0,17},{1,8},{8,25},{9,0},{16,1},{17,24},{24,9},{25,16},{2,19},{3,... | collective-permute-start | bytes 884744 | tf_op jit(solution)/shard_map/ppermute | solution.py:22
  17.0 8.3 %collective-permute-start.7 = (f32[1,9600]{1,0:T(1,128)S(1)}, f32[1,9600]{1,0:T(1,128)S(1)}, u32[]{:S(2)}, u32[]{:S(2)}) collective-permute-start(f32[1,9600]{1,0:T(1,128)S(1)} %get-tuple-element.12), channel_id=1, source_target_pairs={{0,7},{1,6},{2,5},{3,4},{4,3},{5,2},{6,1},{7,0},{8,15},{9,14},{10,... | collective-permute-start | bytes 115208 | tf_op jit(solution)/shard_map/ppermute | solution.py:22
  20.9 4.4 %collective-permute-start.8 = (f32[1,9472]{1,0:T(1,128)S(1)}, f32[1,9472]{1,0:T(1,128)S(1)}, u32[]{:S(2)}, u32[]{:S(2)}) collective-permute-start(f32[1,9472]{1,0:T(1,128)S(1)} %get-tuple-element.13), channel_id=1, source_target_pairs={{0,5},{1,4},{2,7},{3,6},{4,1},{5,0},{6,3},{7,2},{8,13},{9,12},{10,... | collective-permute-start | bytes 113672 | tf_op jit(solution)/shard_map/ppermute | solution.py:22
  20.9 3.4 %collective-permute-start.9 = (f32[1,9344]{1,0:T(1,128)S(1)}, f32[1,9344]{1,0:T(1,128)S(1)}, u32[]{:S(2)}, u32[]{:S(2)}) collective-permute-start(f32[1,9344]{1,0:T(1,128)S(1)} %get-tuple-element.14), channel_id=1, source_target_pairs={{0,3},{1,2},{2,1},{3,0},{4,7},{5,6},{6,5},{7,4},{8,11},{9,10},{10,... | collective-permute-start | bytes 112136 | tf_op jit(solution)/shard_map/ppermute | solution.py:22
  21.5 1.2 %collective-permute-start.10 = (f32[1,9216]{1,0:T(1,128)S(1)}, f32[1,9216]{1,0:T(1,128)S(1)}, u32[]{:S(2)}, u32[]{:S(2)}) collective-permute-start(f32[1,9216]{1,0:T(1,128)S(1)} %get-tuple-element.15), channel_id=1, source_target_pairs={{0,1},{1,0},{8,9},{9,8},{16,17},{17,16},{24,25},{25,24},{2,3},{3,2... | collective-permute-start | bytes 110600 | tf_op jit(solution)/shard_map/ppermute | solution.py:22
  21.9 3.5 %collective-permute-start.11 = (f32[8,9216]{1,0:T(8,128)S(1)}, f32[8,9216]{1,0:T(8,128)S(1)}, u32[]{:S(2)}, u32[]{:S(2)}) collective-permute-start(f32[8,9216]{1,0:T(8,128)S(1)} %get-tuple-element.16), channel_id=1, source_target_pairs={{0,1},{1,0},{8,9},{9,8},{16,17},{17,16},{24,25},{25,24},{2,3},{3,2... | collective-permute-start | bytes 884744 | tf_op jit(solution)/shard_map/ppermute | solution.py:22
  25.4 12.6 %copy-start.2 = (f32[1,9216]{1,0:T(1,128)}, f32[1,9216]{1,0:T(1,128)S(1)}, u32[]{:S(2)}) copy-start(f32[1,9216]{1,0:T(1,128)S(1)} %multiply_add_fusion.state) | copy-start | bytes 110596

commit v7 on v6

--- a/solution.py
+++ b/solution.py
@@ -9,7 +9,7 @@
 STEP = 100
 BETA = 1.0 - STEP ** (-0.8)
 LANES = 128
-PIECES = 2
+PIECES = 4
 VMEM = pl.BlockSpec(memory_space=pltpu.VMEM)
 HBM = pl.BlockSpec(memory_space=pltpu.HBM)
 
@@ -91,7 +91,7 @@
             source = part.at[:, pl.ds(pl.multiple_of(start + a, LANES), b - a)]
             copies.append(pltpu.make_async_copy(source, raw.at[:, spans[-1]], sem.at[len(copies)]))
     for copy in copies:
-        copy.start()
+        copy.start(priority=1)
     for copy, span in zip(copies, spans):
         copy.wait()
         out[:, span] = raw[:, span].astype(jnp.float32)

time: 38.1 us -> 38 us (level)
  no operation moved by 1% of the time
where the time goes in v7:
time: 38 us; the launch traced here: 37.8 us
  starting transfers between devices  12.8 us (34%)
  blocking collectives  11.4 us (30%)
  waiting for transfers between devices  10.2 us (27%)
  Pallas kernels  2.61 us (7%)
  between operations  0.75 us (2%)
    ppermute x12, starting transfers between devices, send_to(): return lax.ppermute(x, axes, [(i, target(i)) for i in range(size)])  12.8 us
    all_to_all x1, blocking collectives, on_device(): sums = lax.all_to_all(message, ('dp', 'wide', 'narrow'), 0, 0, tiled=True)  11.4 us
    ppermute x12, waiting for transfers between devices, send_to(): return lax.ppermute(x, axes, [(i, target(i)) for i in range(size)])  10.2 us
    pallas_call x11, Pallas kernels, call(): pl.pallas_call(kernel, out_shape=[jax.ShapeDtypeStruct(shape, jnp.float32...  2.61 us
  transfers between devices with their start and end apart: 12, of which 7 were waited for; matrix products, arithmetic and copies ran while one was open for 0% of the time, Pallas kernels for 1%

profile of v7, /device:TPU:0, one launch (start us, length us, event | category | flops | bytes accessed | tf_op | source)
XLA Modules:
  0.0 37.8 jit_solution(8182363568778145168)
XLA Ops:
  0.6 1.0 %shard_map.67 = f32[8,9216]{1,0:T(8,128)S(1)} custom-call(bf16[8,73728]{1,0:T(8,128)(2,1)} %bitcast.9), custom_call_target="tpu_custom_call" | custom-call | tf_op jit(solution)/shard_map/pallas_call | solution.py:46
  1.6 0.5 %collective-permute-start = (f32[8,9216]{1,0:T(8,128)S(1)}, f32[8,9216]{1,0:T(8,128)S(1)}, u32[]{:S(2)}, u32[]{:S(2)}) collective-permute-start(f32[8,9216]{1,0:T(8,128)S(1)} %shard_map.67), channel_id=1, source_target_pairs={{0,1},{1,0},{8,9},{9,8},{16,17},{17,16},{24,25},{25,24},{2,3},{3,2... | collective-permute-start | bytes 884744 | tf_op jit(solution)/shard_map/ppermute | solution.py:22
  2.2 0.4 collective-permute-start.4
  2.5 0.3 collective-permute-start.2
  2.8 0.5 %collective-permute-done.refs_1_ = f32[8,9216]{1,0:T(8,128)S(1)} collective-permute-done((f32[8,9216]{1,0:T(8,128)S(1)}, f32[8,9216]{1,0:T(8,128)S(1)}, u32[]{:S(2)}, u32[]{:S(2)}) %collective-permute-start) | collective-permute-done | bytes 294944 | tf_op jit(solution)/shard_map/ppermute | solution.py:22
  3.4 2.7 %collective-permute-start.1 = (f32[8,9216]{1,0:T(8,128)S(1)}, f32[8,9216]{1,0:T(8,128)S(1)}, u32[]{:S(2)}, u32[]{:S(2)}) collective-permute-start(f32[8,9216]{1,0:T(8,128)S(1)} %shard_map.68), channel_id=1, source_target_pairs={{0,17},{1,8},{8,25},{9,0},{16,1},{17,24},{24,9},{25,16},{2,19},{3,... | collective-permute-start | bytes 884744 | tf_op jit(solution)/shard_map/ppermute | solution.py:22
  6.1 0.4 %collective-permute-start.6 = (f32[8,9216]{1,0:T(8,128)S(1)}, f32[8,9216]{1,0:T(8,128)S(1)}, u32[]{:S(2)}, u32[]{:S(2)}) collective-permute-start(f32[8,9216]{1,0:T(8,128)S(1)} %shard_map.73), channel_id=1, source_target_pairs={{0,1},{1,0},{8,9},{9,8},{16,17},{17,16},{24,25},{25,24},{2,3},{3,2... | collective-permute-start | bytes 884744 | tf_op jit(solution)/shard_map/ppermute | solution.py:22
  6.5 1.6 %collective-permute-start.5 = (f32[8,9216]{1,0:T(8,128)S(1)}, f32[8,9216]{1,0:T(8,128)S(1)}, u32[]{:S(2)}, u32[]{:S(2)}) collective-permute-start(f32[8,9216]{1,0:T(8,128)S(1)} %shard_map.72), channel_id=1, source_target_pairs={{0,16},{1,9},{8,24},{9,1},{16,0},{17,25},{24,8},{25,17},{2,18},{3,... | collective-permute-start | bytes 884744 | tf_op jit(solution)/shard_map/ppermute | solution.py:22
  8.1 0.0 collective-permute-done.2.refs_2_
  8.1 2.3 %collective-permute-done.1.refs_1_ = f32[8,9216]{1,0:T(8,128)S(1)} collective-permute-done((f32[8,9216]{1,0:T(8,128)S(1)}, f32[8,9216]{1,0:T(8,128)S(1)}, u32[]{:S(2)}, u32[]{:S(2)}) %collective-permute-start.1) | collective-permute-done | bytes 294944 | tf_op jit(solution)/shard_map/ppermute | solution.py:22
  10.5 0.0 copy-start.4
  10.5 0.0 copy-start.1
  10.5 0.0 copy-start.3
  10.5 1.8 %collective-permute-start.3 = (f32[8,9216]{1,0:T(8,128)S(1)}, f32[8,9216]{1,0:T(8,128)S(1)}, u32[]{:S(2)}, u32[]{:S(2)}) collective-permute-start(f32[8,9216]{1,0:T(8,128)S(1)} %shard_map.70), channel_id=1, source_target_pairs={{0,17},{1,8},{8,25},{9,0},{16,1},{17,24},{24,9},{25,16},{2,19},{3,... | collective-permute-start | bytes 884744 | tf_op jit(solution)/shard_map/ppermute | solution.py:22
  12.3 0.0 collective-permute-done.6.refs_3_
  12.3 1.8 %collective-permute-done.5.refs_2_ = f32[8,9216]{1,0:T(8,128)S(1)} collective-permute-done((f32[8,9216]{1,0:T(8,128)S(1)}, f32[8,9216]{1,0:T(8,128)S(1)}, u32[]{:S(2)}, u32[]{:S(2)}) %collective-permute-start.5) | collective-permute-done | bytes 294944 | tf_op jit(solution)/shard_map/ppermute | solution.py:22
  14.2 2.6 %collective-permute-done.3.refs_1_ = f32[8,9216]{1,0:T(8,128)S(1)} collective-permute-done((f32[8,9216]{1,0:T(8,128)S(1)}, f32[8,9216]{1,0:T(8,128)S(1)}, u32[]{:S(2)}, u32[]{:S(2)}) %collective-permute-start.3) | collective-permute-done | bytes 294944 | tf_op jit(solution)/shard_map/ppermute | solution.py:22
  16.8 0.1 shard_map.74
  16.9 3.9 %collective-permute-start.7 = (f32[1,9600]{1,0:T(1,128)S(1)}, f32[1,9600]{1,0:T(1,128)S(1)}, u32[]{:S(2)}, u32[]{:S(2)}) collective-permute-start(f32[1,9600]{1,0:T(1,128)S(1)} %get-tuple-element.12), channel_id=1, source_target_pairs={{0,7},{1,6},{2,5},{3,4},{4,3},{5,2},{6,1},{7,0},{8,15},{9,14},{10,... | collective-permute-start | bytes 115208 | tf_op jit(solution)/shard_map/ppermute | solution.py:22
  20.8 0.0 collective-permute-start.8
  20.8 0.6 %collective-permute-start.9 = (f32[1,9344]{1,0:T(1,128)S(1)}, f32[1,9344]{1,0:T(1,128)S(1)}, u32[]{:S(2)}, u32[]{:S(2)}) collective-permute-start(f32[1,9344]{1,0:T(1,128)S(1)} %get-tuple-element.14), channel_id=1, source_target_pairs={{0,3},{1,2},{2,1},{3,0},{4,7},{5,6},{6,5},{7,4},{8,11},{9,10},{10,... | collective-permute-start | bytes 112136 | tf_op jit(solution)/shard_map/ppermute | solution.py:22
  21.5 0.2 collective-permute-start.10
  21.6 0.2 shard_map.75.fixed_in
  21.8 0.4 %collective-permute-start.11 = (f32[8,9216]{1,0:T(8,128)S(1)}, f32[8,9216]{1,0:T(8,128)S(1)}, u32[]{:S(2)}, u32[]{:S(2)}) collective-permute-start(f32[8,9216]{1,0:T(8,128)S(1)} %get-tuple-element.16), channel_id=1, source_target_pairs={{0,1},{1,0},{8,9},{9,8},{16,17},{17,16},{24,25},{25,24},{2,3},{3,2... | collective-permute-start | bytes 884744 | tf_op jit(solution)/shard_map/ppermute | solution.py:22
  22.2 0.4 %collective-permute-done.10 = f32[1,9216]{1,0:T(1,128)S(1)} collective-permute-done((f32[1,9216]{1,0:T(1,128)S(1)}, f32[1,9216]{1,0:T(1,128)S(1)}, u32[]{:S(2)}, u32[]{:S(2)}) %collective-permute-start.10) | collective-permute-done | bytes 36896 | tf_op jit(solution)/shard_map/ppermute | solution.py:22
  22.7 1.6 %collective-permute-done.9 = f32[1,9344]{1,0:T(1,128)S(1)} collective-permute-done((f32[1,9344]{1,0:T(1,128)S(1)}, f32[1,9344]{1,0:T(1,128)S(1)}, u32[]{:S(2)}, u32[]{:S(2)}) %collective-permute-start.9) | collective-permute-done | bytes 37408 | tf_op jit(solution)/shard_map/ppermute | solution.py:22
  24.2 0.9 %collective-permute-done.8 = f32[1,9472]{1,0:T(1,128)S(1)} collective-permute-done((f32[1,9472]{1,0:T(1,128)S(1)}, f32[1,9472]{1,0:T(1,128)S(1)}, u32[]{:S(2)}, u32[]{:S(2)}) %collective-permute-start.8) | collective-permute-done | bytes 37920 | tf_op jit(solution)/shard_map/ppermute | solution.py:22
  25.2 0.1 multiply_add_fusion.state
  25.3 0.0 copy-start.2
  25.3 0.2 shard_map.76
  25.5 11.4 %all_to_all.11 = f32[32,1,128]{2,1,0:T(1,128)S(1)} all-to-all(f32[32,1,128]{2,1,0:T(1,128)S(1)} %bitcast.19), channel_id=1, replica_groups=mesh['dp'=4,'wide'=4,'narrow'=2] {'dp','wide','narrow'}, dimensions={0} | all-to-all | bytes 32768 | tf_op jit(solution)/shard_map/all_to_all | solution.py:258
  36.9 1.0 %shard_map.77 = (f32[8,9216]{1,0:T(8,128)}, f32[1,8]{1,0:T(1,128)}) custom-call(f32[32,128]{1,0:T(8,128)S(1)} %bitcast.18, f32[8,9216]{1,0:T(8,128)S(1)} %get-tuple-element.18.refs_1_), custom_call_target="tpu_custom_call" | custom-call | tf_op jit(solution)/shard_map/pallas_call | solution.py:46
  (16 shorter events, 0.2 us)
Async XLA Ops:
  0.6 1.5 %copy-start = (bf16[1,8,73728]{2,1,0:T(8,128)(2,1)S(1)}, bf16[1,8,73728]{2,1,0:T(8,128)(2,1)}, u32[]{:S(2)}) copy-start(bf16[1,8,73728]{2,1,0:T(8,128)(2,1)} %param.4) | copy-start | bytes 3538948
  1.6 1.7 %collective-permute-start = (f32[8,9216]{1,0:T(8,128)S(1)}, f32[8,9216]{1,0:T(8,128)S(1)}, u32[]{:S(2)}, u32[]{:S(2)}) collective-permute-start(f32[8,9216]{1,0:T(8,128)S(1)} %shard_map.67), channel_id=1, source_target_pairs={{0,1},{1,0},{8,9},{9,8},{16,17},{17,16},{24,25},{25,24},{2,3},{3,2... | collective-permute-start | bytes 884744 | tf_op jit(solution)/shard_map/ppermute | solution.py:22
  2.2 4.3 %collective-permute-start.4 = (f32[8,9216]{1,0:T(8,128)S(1)}, f32[8,9216]{1,0:T(8,128)S(1)}, u32[]{:S(2)}, u32[]{:S(2)}) collective-permute-start(f32[8,9216]{1,0:T(8,128)S(1)} %shard_map.71), channel_id=1, source_target_pairs={{0,1},{1,0},{8,9},{9,8},{16,17},{17,16},{24,25},{25,24},{2,3},{3,2... | collective-permute-start | bytes 884744 | tf_op jit(solution)/shard_map/ppermute | solution.py:22
  2.5 5.6 %collective-permute-start.2 = (f32[8,9216]{1,0:T(8,128)S(1)}, f32[8,9216]{1,0:T(8,128)S(1)}, u32[]{:S(2)}, u32[]{:S(2)}) collective-permute-start(f32[8,9216]{1,0:T(8,128)S(1)} %shard_map.69), channel_id=1, source_target_pairs={{0,1},{1,0},{8,9},{9,8},{16,17},{17,16},{24,25},{25,24},{2,3},{3,2... | collective-permute-start | bytes 884744 | tf_op jit(solution)/shard_map/ppermute | solution.py:22
  3.4 7.1 %collective-permute-start.1 = (f32[8,9216]{1,0:T(8,128)S(1)}, f32[8,9216]{1,0:T(8,128)S(1)}, u32[]{:S(2)}, u32[]{:S(2)}) collective-permute-start(f32[8,9216]{1,0:T(8,128)S(1)} %shard_map.68), channel_id=1, source_target_pairs={{0,17},{1,8},{8,25},{9,0},{16,1},{17,24},{24,9},{25,16},{2,19},{3,... | collective-permute-start | bytes 884744 | tf_op jit(solution)/shard_map/ppermute | solution.py:22
  6.1 6.3 %collective-permute-start.6 = (f32[8,9216]{1,0:T(8,128)S(1)}, f32[8,9216]{1,0:T(8,128)S(1)}, u32[]{:S(2)}, u32[]{:S(2)}) collective-permute-start(f32[8,9216]{1,0:T(8,128)S(1)} %shard_map.73), channel_id=1, source_target_pairs={{0,1},{1,0},{8,9},{9,8},{16,17},{17,16},{24,25},{25,24},{2,3},{3,2... | collective-permute-start | bytes 884744 | tf_op jit(solution)/shard_map/ppermute | solution.py:22
  6.5 7.6 %collective-permute-start.5 = (f32[8,9216]{1,0:T(8,128)S(1)}, f32[8,9216]{1,0:T(8,128)S(1)}, u32[]{:S(2)}, u32[]{:S(2)}) collective-permute-start(f32[8,9216]{1,0:T(8,128)S(1)} %shard_map.72), channel_id=1, source_target_pairs={{0,16},{1,9},{8,24},{9,1},{16,0},{17,25},{24,8},{25,17},{2,18},{3,... | collective-permute-start | bytes 884744 | tf_op jit(solution)/shard_map/ppermute | solution.py:22
  10.5 11.1 %copy-start.4 = (f32[9216]{0:T(1024)S(1)}, f32[9216]{0:T(1024)}, u32[]{:S(2)}) copy-start(f32[9216]{0:T(1024)} %param.7) | copy-start | bytes 110596
  10.5 11.1 %copy-start.1 = (bf16[8,9216]{1,0:T(8,128)(2,1)S(1)}, bf16[8,9216]{1,0:T(8,128)(2,1)}, u32[]{:S(2)}) copy-start(bf16[8,9216]{1,0:T(8,128)(2,1)} %weight.1) | copy-start | bytes 442372
  10.5 11.1 %copy-start.3 = (f32[8]{0:T(128)S(1)}, f32[8]{0:T(128)}, u32[]{:S(2)}) copy-start(f32[8]{0:T(128)} %param.6) | copy-start | bytes 100
  10.5 6.2 %collective-permute-start.3 = (f32[8,9216]{1,0:T(8,128)S(1)}, f32[8,9216]{1,0:T(8,128)S(1)}, u32[]{:S(2)}, u32[]{:S(2)}) collective-permute-start(f32[8,9216]{1,0:T(8,128)S(1)} %shard_map.70), channel_id=1, source_target_pairs={{0,17},{1,8},{8,25},{9,0},{16,1},{17,24},{24,9},{25,16},{2,19},{3,... | collective-permute-start | bytes 884744 | tf_op jit(solution)/shard_map/ppermute | solution.py:22
  16.9 8.3 %collective-permute-start.7 = (f32[1,9600]{1,0:T(1,128)S(1)}, f32[1,9600]{1,0:T(1,128)S(1)}, u32[]{:S(2)}, u32[]{:S(2)}) collective-permute-start(f32[1,9600]{1,0:T(1,128)S(1)} %get-tuple-element.12), channel_id=1, source_target_pairs={{0,7},{1,6},{2,5},{3,4},{4,3},{5,2},{6,1},{7,0},{8,15},{9,14},{10,... | collective-permute-start | bytes 115208 | tf_op jit(solution)/shard_map/ppermute | solution.py:22
  20.8 4.4 %collective-permute-start.8 = (f32[1,9472]{1,0:T(1,128)S(1)}, f32[1,9472]{1,0:T(1,128)S(1)}, u32[]{:S(2)}, u32[]{:S(2)}) collective-permute-start(f32[1,9472]{1,0:T(1,128)S(1)} %get-tuple-element.13), channel_id=1, source_target_pairs={{0,5},{1,4},{2,7},{3,6},{4,1},{5,0},{6,3},{7,2},{8,13},{9,12},{10,... | collective-permute-start | bytes 113672 | tf_op jit(solution)/shard_map/ppermute | solution.py:22
  20.8 3.4 %collective-permute-start.9 = (f32[1,9344]{1,0:T(1,128)S(1)}, f32[1,9344]{1,0:T(1,128)S(1)}, u32[]{:S(2)}, u32[]{:S(2)}) collective-permute-start(f32[1,9344]{1,0:T(1,128)S(1)} %get-tuple-element.14), channel_id=1, source_target_pairs={{0,3},{1,2},{2,1},{3,0},{4,7},{5,6},{6,5},{7,4},{8,11},{9,10},{10,... | collective-permute-start | bytes 112136 | tf_op jit(solution)/shard_map/ppermute | solution.py:22
  21.5 1.2 %collective-permute-start.10 = (f32[1,9216]{1,0:T(1,128)S(1)}, f32[1,9216]{1,0:T(1,128)S(1)}, u32[]{:S(2)}, u32[]{:S(2)}) collective-permute-start(f32[1,9216]{1,0:T(1,128)S(1)} %get-tuple-element.15), channel_id=1, source_target_pairs={{0,1},{1,0},{8,9},{9,8},{16,17},{17,16},{24,25},{25,24},{2,3},{3,2... | collective-permute-start | bytes 110600 | tf_op jit(solution)/shard_map/ppermute | solution.py:22
  21.8 3.5 %collective-permute-start.11 = (f32[8,9216]{1,0:T(8,128)S(1)}, f32[8,9216]{1,0:T(8,128)S(1)}, u32[]{:S(2)}, u32[]{:S(2)}) collective-permute-start(f32[8,9216]{1,0:T(8,128)S(1)} %get-tuple-element.16), channel_id=1, source_target_pairs={{0,1},{1,0},{8,9},{9,8},{16,17},{17,16},{24,25},{25,24},{2,3},{3,2... | collective-permute-start | bytes 884744 | tf_op jit(solution)/shard_map/ppermute | solution.py:22
  25.3 12.6 %copy-start.2 = (f32[1,9216]{1,0:T(1,128)}, f32[1,9216]{1,0:T(1,128)S(1)}, u32[]{:S(2)}) copy-start(f32[1,9216]{1,0:T(1,128)S(1)} %multiply_add_fusion.state) | copy-start | bytes 110596

commit v8 on v7

--- a/solution.py
+++ b/solution.py
@@ -90,8 +90,8 @@
             spans.append(pl.ds(i * blocks.cols + a, b - a))
             source = part.at[:, pl.ds(pl.multiple_of(start + a, LANES), b - a)]
             copies.append(pltpu.make_async_copy(source, raw.at[:, spans[-1]], sem.at[len(copies)]))
-    for copy in copies:
-        copy.start(priority=1)
+    for i, copy in enumerate(copies):
+        copy.start(priority=1 - i % 2)
     for copy, span in zip(copies, spans):
         copy.wait()
         out[:, span] = raw[:, span].astype(jnp.float32)

time: 38 us -> 38 us (level)
  no operation moved by 1% of the time
where the time goes in v8:
time: 38 us; the launch traced here: 37.8 us
  starting transfers between devices  12.8 us (34%)
  blocking collectives  11.4 us (30%)
  waiting for transfers between devices  10.2 us (27%)
  Pallas kernels  2.62 us (7%)
  between operations  0.75 us (2%)
    ppermute x12, starting transfers between devices, send_to(): return lax.ppermute(x, axes, [(i, target(i)) for i in range(size)])  12.8 us
    all_to_all x1, blocking collectives, on_device(): sums = lax.all_to_all(message, ('dp', 'wide', 'narrow'), 0, 0, tiled=True)  11.4 us
    ppermute x12, waiting for transfers between devices, send_to(): return lax.ppermute(x, axes, [(i, target(i)) for i in range(size)])  10.2 us
    pallas_call x11, Pallas kernels, call(): pl.pallas_call(kernel, out_shape=[jax.ShapeDtypeStruct(shape, jnp.float32...  2.62 us
  transfers between devices with their start and end apart: 12, of which 7 were waited for; matrix products, arithmetic and copies ran while one was open for 0% of the time, Pallas kernels for 1%

profile of v8, /device:TPU:0, one launch (start us, length us, event | category | flops | bytes accessed | tf_op | source)
XLA Modules:
  0.0 37.8 jit_solution(1440876800700179246)
XLA Ops:
  0.6 1.0 %shard_map.67 = f32[8,9216]{1,0:T(8,128)S(1)} custom-call(bf16[8,73728]{1,0:T(8,128)(2,1)} %bitcast.9), custom_call_target="tpu_custom_call" | custom-call | tf_op jit(solution)/shard_map/pallas_call | solution.py:46
  1.6 0.5 %collective-permute-start = (f32[8,9216]{1,0:T(8,128)S(1)}, f32[8,9216]{1,0:T(8,128)S(1)}, u32[]{:S(2)}, u32[]{:S(2)}) collective-permute-start(f32[8,9216]{1,0:T(8,128)S(1)} %shard_map.67), channel_id=1, source_target_pairs={{0,1},{1,0},{8,9},{9,8},{16,17},{17,16},{24,25},{25,24},{2,3},{3,2... | collective-permute-start | bytes 884744 | tf_op jit(solution)/shard_map/ppermute | solution.py:22
  2.2 0.3 collective-permute-start.4
  2.5 0.3 collective-permute-start.2
  2.8 0.5 %collective-permute-done.refs_1_ = f32[8,9216]{1,0:T(8,128)S(1)} collective-permute-done((f32[8,9216]{1,0:T(8,128)S(1)}, f32[8,9216]{1,0:T(8,128)S(1)}, u32[]{:S(2)}, u32[]{:S(2)}) %collective-permute-start) | collective-permute-done | bytes 294944 | tf_op jit(solution)/shard_map/ppermute | solution.py:22
  3.4 2.7 %collective-permute-start.1 = (f32[8,9216]{1,0:T(8,128)S(1)}, f32[8,9216]{1,0:T(8,128)S(1)}, u32[]{:S(2)}, u32[]{:S(2)}) collective-permute-start(f32[8,9216]{1,0:T(8,128)S(1)} %shard_map.68), channel_id=1, source_target_pairs={{0,17},{1,8},{8,25},{9,0},{16,1},{17,24},{24,9},{25,16},{2,19},{3,... | collective-permute-start | bytes 884744 | tf_op jit(solution)/shard_map/ppermute | solution.py:22
  6.1 0.4 %collective-permute-start.6 = (f32[8,9216]{1,0:T(8,128)S(1)}, f32[8,9216]{1,0:T(8,128)S(1)}, u32[]{:S(2)}, u32[]{:S(2)}) collective-permute-start(f32[8,9216]{1,0:T(8,128)S(1)} %shard_map.73), channel_id=1, source_target_pairs={{0,1},{1,0},{8,9},{9,8},{16,17},{17,16},{24,25},{25,24},{2,3},{3,2... | collective-permute-start | bytes 884744 | tf_op jit(solution)/shard_map/ppermute | solution.py:22
  6.5 0.0 collective-permute-done.4.refs_1_
  6.5 1.6 %collective-permute-start.5 = (f32[8,9216]{1,0:T(8,128)S(1)}, f32[8,9216]{1,0:T(8,128)S(1)}, u32[]{:S(2)}, u32[]{:S(2)}) collective-permute-start(f32[8,9216]{1,0:T(8,128)S(1)} %shard_map.72), channel_id=1, source_target_pairs={{0,16},{1,9},{8,24},{9,1},{16,0},{17,25},{24,8},{25,17},{2,18},{3,... | collective-permute-start | bytes 884744 | tf_op jit(solution)/shard_map/ppermute | solution.py:22
  8.1 2.3 %collective-permute-done.1.refs_1_ = f32[8,9216]{1,0:T(8,128)S(1)} collective-permute-done((f32[8,9216]{1,0:T(8,128)S(1)}, f32[8,9216]{1,0:T(8,128)S(1)}, u32[]{:S(2)}, u32[]{:S(2)}) %collective-permute-start.1) | collective-permute-done | bytes 294944 | tf_op jit(solution)/shard_map/ppermute | solution.py:22
  10.5 0.0 copy-start.4
  10.5 0.0 copy-start.1
  10.5 0.0 copy-start.3
  10.5 1.8 %collective-permute-start.3 = (f32[8,9216]{1,0:T(8,128)S(1)}, f32[8,9216]{1,0:T(8,128)S(1)}, u32[]{:S(2)}, u32[]{:S(2)}) collective-permute-start(f32[8,9216]{1,0:T(8,128)S(1)} %shard_map.70), channel_id=1, source_target_pairs={{0,17},{1,8},{8,25},{9,0},{16,1},{17,24},{24,9},{25,16},{2,19},{3,... | collective-permute-start | bytes 884744 | tf_op jit(solution)/shard_map/ppermute | solution.py:22
  12.4 0.0 collective-permute-done.6.refs_3_
  12.4 1.8 %collective-permute-done.5.refs_2_ = f32[8,9216]{1,0:T(8,128)S(1)} collective-permute-done((f32[8,9216]{1,0:T(8,128)S(1)}, f32[8,9216]{1,0:T(8,128)S(1)}, u32[]{:S(2)}, u32[]{:S(2)}) %collective-permute-start.5) | collective-permute-done | bytes 294944 | tf_op jit(solution)/shard_map/ppermute | solution.py:22
  14.2 2.6 %collective-permute-done.3.refs_1_ = f32[8,9216]{1,0:T(8,128)S(1)} collective-permute-done((f32[8,9216]{1,0:T(8,128)S(1)}, f32[8,9216]{1,0:T(8,128)S(1)}, u32[]{:S(2)}, u32[]{:S(2)}) %collective-permute-start.3) | collective-permute-done | bytes 294944 | tf_op jit(solution)/shard_map/ppermute | solution.py:22
  16.8 0.1 shard_map.74
  16.9 3.9 %collective-permute-start.7 = (f32[1,9600]{1,0:T(1,128)S(1)}, f32[1,9600]{1,0:T(1,128)S(1)}, u32[]{:S(2)}, u32[]{:S(2)}) collective-permute-start(f32[1,9600]{1,0:T(1,128)S(1)} %get-tuple-element.12), channel_id=1, source_target_pairs={{0,7},{1,6},{2,5},{3,4},{4,3},{5,2},{6,1},{7,0},{8,15},{9,14},{10,... | collective-permute-start | bytes 115208 | tf_op jit(solution)/shard_map/ppermute | solution.py:22
  20.8 0.6 %collective-permute-start.9 = (f32[1,9344]{1,0:T(1,128)S(1)}, f32[1,9344]{1,0:T(1,128)S(1)}, u32[]{:S(2)}, u32[]{:S(2)}) collective-permute-start(f32[1,9344]{1,0:T(1,128)S(1)} %get-tuple-element.14), channel_id=1, source_target_pairs={{0,3},{1,2},{2,1},{3,0},{4,7},{5,6},{6,5},{7,4},{8,11},{9,10},{10,... | collective-permute-start | bytes 112136 | tf_op jit(solution)/shard_map/ppermute | solution.py:22
  21.5 0.2 collective-permute-start.10
  21.6 0.2 shard_map.75.fixed_in
  21.8 0.4 %collective-permute-start.11 = (f32[8,9216]{1,0:T(8,128)S(1)}, f32[8,9216]{1,0:T(8,128)S(1)}, u32[]{:S(2)}, u32[]{:S(2)}) collective-permute-start(f32[8,9216]{1,0:T(8,128)S(1)} %get-tuple-element.16), channel_id=1, source_target_pairs={{0,1},{1,0},{8,9},{9,8},{16,17},{17,16},{24,25},{25,24},{2,3},{3,2... | collective-permute-start | bytes 884744 | tf_op jit(solution)/shard_map/ppermute | solution.py:22
  22.2 0.4 %collective-permute-done.10 = f32[1,9216]{1,0:T(1,128)S(1)} collective-permute-done((f32[1,9216]{1,0:T(1,128)S(1)}, f32[1,9216]{1,0:T(1,128)S(1)}, u32[]{:S(2)}, u32[]{:S(2)}) %collective-permute-start.10) | collective-permute-done | bytes 36896 | tf_op jit(solution)/shard_map/ppermute | solution.py:22
  22.7 1.6 %collective-permute-done.9 = f32[1,9344]{1,0:T(1,128)S(1)} collective-permute-done((f32[1,9344]{1,0:T(1,128)S(1)}, f32[1,9344]{1,0:T(1,128)S(1)}, u32[]{:S(2)}, u32[]{:S(2)}) %collective-permute-start.9) | collective-permute-done | bytes 37408 | tf_op jit(solution)/shard_map/ppermute | solution.py:22
  24.2 0.9 %collective-permute-done.8 = f32[1,9472]{1,0:T(1,128)S(1)} collective-permute-done((f32[1,9472]{1,0:T(1,128)S(1)}, f32[1,9472]{1,0:T(1,128)S(1)}, u32[]{:S(2)}, u32[]{:S(2)}) %collective-permute-start.8) | collective-permute-done | bytes 37920 | tf_op jit(solution)/shard_map/ppermute | solution.py:22
  25.2 0.0 collective-permute-done.7
  25.2 0.1 multiply_add_fusion.state
  25.3 0.0 copy-start.2
  25.3 0.2 shard_map.76
  25.5 11.4 %all_to_all.11 = f32[32,1,128]{2,1,0:T(1,128)S(1)} all-to-all(f32[32,1,128]{2,1,0:T(1,128)S(1)} %bitcast.19), channel_id=1, replica_groups=mesh['dp'=4,'wide'=4,'narrow'=2] {'dp','wide','narrow'}, dimensions={0} | all-to-all | bytes 32768 | tf_op jit(solution)/shard_map/all_to_all | solution.py:258
  36.9 1.0 %shard_map.77 = (f32[8,9216]{1,0:T(8,128)}, f32[1,8]{1,0:T(1,128)}) custom-call(f32[32,128]{1,0:T(8,128)S(1)} %bitcast.18, f32[8,9216]{1,0:T(8,128)S(1)} %get-tuple-element.18.refs_1_), custom_call_target="tpu_custom_call" | custom-call | tf_op jit(solution)/shard_map/pallas_call | solution.py:46
  (16 shorter events, 0.2 us)
Async XLA Ops:
  0.6 1.5 %copy-start = (bf16[1,8,73728]{2,1,0:T(8,128)(2,1)S(1)}, bf16[1,8,73728]{2,1,0:T(8,128)(2,1)}, u32[]{:S(2)}) copy-start(bf16[1,8,73728]{2,1,0:T(8,128)(2,1)} %param.4) | copy-start | bytes 3538948
  1.6 1.7 %collective-permute-start = (f32[8,9216]{1,0:T(8,128)S(1)}, f32[8,9216]{1,0:T(8,128)S(1)}, u32[]{:S(2)}, u32[]{:S(2)}) collective-permute-start(f32[8,9216]{1,0:T(8,128)S(1)} %shard_map.67), channel_id=1, source_target_pairs={{0,1},{1,0},{8,9},{9,8},{16,17},{17,16},{24,25},{25,24},{2,3},{3,2... | collective-permute-start | bytes 884744 | tf_op jit(solution)/shard_map/ppermute | solution.py:22
  2.2 4.3 %collective-permute-start.4 = (f32[8,9216]{1,0:T(8,128)S(1)}, f32[8,9216]{1,0:T(8,128)S(1)}, u32[]{:S(2)}, u32[]{:S(2)}) collective-permute-start(f32[8,9216]{1,0:T(8,128)S(1)} %shard_map.71), channel_id=1, source_target_pairs={{0,1},{1,0},{8,9},{9,8},{16,17},{17,16},{24,25},{25,24},{2,3},{3,2... | collective-permute-start | bytes 884744 | tf_op jit(solution)/shard_map/ppermute | solution.py:22
  2.5 5.6 %collective-permute-start.2 = (f32[8,9216]{1,0:T(8,128)S(1)}, f32[8,9216]{1,0:T(8,128)S(1)}, u32[]{:S(2)}, u32[]{:S(2)}) collective-permute-start(f32[8,9216]{1,0:T(8,128)S(1)} %shard_map.69), channel_id=1, source_target_pairs={{0,1},{1,0},{8,9},{9,8},{16,17},{17,16},{24,25},{25,24},{2,3},{3,2... | collective-permute-start | bytes 884744 | tf_op jit(solution)/shard_map/ppermute | solution.py:22
  3.4 7.1 %collective-permute-start.1 = (f32[8,9216]{1,0:T(8,128)S(1)}, f32[8,9216]{1,0:T(8,128)S(1)}, u32[]{:S(2)}, u32[]{:S(2)}) collective-permute-start(f32[8,9216]{1,0:T(8,128)S(1)} %shard_map.68), channel_id=1, source_target_pairs={{0,17},{1,8},{8,25},{9,0},{16,1},{17,24},{24,9},{25,16},{2,19},{3,... | collective-permute-start | bytes 884744 | tf_op jit(solution)/shard_map/ppermute | solution.py:22
  6.1 6.3 %collective-permute-start.6 = (f32[8,9216]{1,0:T(8,128)S(1)}, f32[8,9216]{1,0:T(8,128)S(1)}, u32[]{:S(2)}, u32[]{:S(2)}) collective-permute-start(f32[8,9216]{1,0:T(8,128)S(1)} %shard_map.73), channel_id=1, source_target_pairs={{0,1},{1,0},{8,9},{9,8},{16,17},{17,16},{24,25},{25,24},{2,3},{3,2... | collective-permute-start | bytes 884744 | tf_op jit(solution)/shard_map/ppermute | solution.py:22
  6.5 7.6 %collective-permute-start.5 = (f32[8,9216]{1,0:T(8,128)S(1)}, f32[8,9216]{1,0:T(8,128)S(1)}, u32[]{:S(2)}, u32[]{:S(2)}) collective-permute-start(f32[8,9216]{1,0:T(8,128)S(1)} %shard_map.72), channel_id=1, source_target_pairs={{0,16},{1,9},{8,24},{9,1},{16,0},{17,25},{24,8},{25,17},{2,18},{3,... | collective-permute-start | bytes 884744 | tf_op jit(solution)/shard_map/ppermute | solution.py:22
  10.5 11.1 %copy-start.4 = (f32[9216]{0:T(1024)S(1)}, f32[9216]{0:T(1024)}, u32[]{:S(2)}) copy-start(f32[9216]{0:T(1024)} %param.7) | copy-start | bytes 110596
  10.5 11.1 %copy-start.1 = (bf16[8,9216]{1,0:T(8,128)(2,1)S(1)}, bf16[8,9216]{1,0:T(8,128)(2,1)}, u32[]{:S(2)}) copy-start(bf16[8,9216]{1,0:T(8,128)(2,1)} %weight.1) | copy-start | bytes 442372
  10.5 11.1 %copy-start.3 = (f32[8]{0:T(128)S(1)}, f32[8]{0:T(128)}, u32[]{:S(2)}) copy-start(f32[8]{0:T(128)} %param.6) | copy-start | bytes 100
  10.5 6.2 %collective-permute-start.3 = (f32[8,9216]{1,0:T(8,128)S(1)}, f32[8,9216]{1,0:T(8,128)S(1)}, u32[]{:S(2)}, u32[]{:S(2)}) collective-permute-start(f32[8,9216]{1,0:T(8,128)S(1)} %shard_map.70), channel_id=1, source_target_pairs={{0,17},{1,8},{8,25},{9,0},{16,1},{17,24},{24,9},{25,16},{2,19},{3,... | collective-permute-start | bytes 884744 | tf_op jit(solution)/shard_map/ppermute | solution.py:22
  16.9 8.3 %collective-permute-start.7 = (f32[1,9600]{1,0:T(1,128)S(1)}, f32[1,9600]{1,0:T(1,128)S(1)}, u32[]{:S(2)}, u32[]{:S(2)}) collective-permute-start(f32[1,9600]{1,0:T(1,128)S(1)} %get-tuple-element.12), channel_id=1, source_target_pairs={{0,7},{1,6},{2,5},{3,4},{4,3},{5,2},{6,1},{7,0},{8,15},{9,14},{10,... | collective-permute-start | bytes 115208 | tf_op jit(solution)/shard_map/ppermute | solution.py:22
  20.8 4.4 %collective-permute-start.8 = (f32[1,9472]{1,0:T(1,128)S(1)}, f32[1,9472]{1,0:T(1,128)S(1)}, u32[]{:S(2)}, u32[]{:S(2)}) collective-permute-start(f32[1,9472]{1,0:T(1,128)S(1)} %get-tuple-element.13), channel_id=1, source_target_pairs={{0,5},{1,4},{2,7},{3,6},{4,1},{5,0},{6,3},{7,2},{8,13},{9,12},{10,... | collective-permute-start | bytes 113672 | tf_op jit(solution)/shard_map/ppermute | solution.py:22
  20.8 3.4 %collective-permute-start.9 = (f32[1,9344]{1,0:T(1,128)S(1)}, f32[1,9344]{1,0:T(1,128)S(1)}, u32[]{:S(2)}, u32[]{:S(2)}) collective-permute-start(f32[1,9344]{1,0:T(1,128)S(1)} %get-tuple-element.14), channel_id=1, source_target_pairs={{0,3},{1,2},{2,1},{3,0},{4,7},{5,6},{6,5},{7,4},{8,11},{9,10},{10,... | collective-permute-start | bytes 112136 | tf_op jit(solution)/shard_map/ppermute | solution.py:22
  21.5 1.2 %collective-permute-start.10 = (f32[1,9216]{1,0:T(1,128)S(1)}, f32[1,9216]{1,0:T(1,128)S(1)}, u32[]{:S(2)}, u32[]{:S(2)}) collective-permute-start(f32[1,9216]{1,0:T(1,128)S(1)} %get-tuple-element.15), channel_id=1, source_target_pairs={{0,1},{1,0},{8,9},{9,8},{16,17},{17,16},{24,25},{25,24},{2,3},{3,2... | collective-permute-start | bytes 110600 | tf_op jit(solution)/shard_map/ppermute | solution.py:22
  21.8 3.5 %collective-permute-start.11 = (f32[8,9216]{1,0:T(8,128)S(1)}, f32[8,9216]{1,0:T(8,128)S(1)}, u32[]{:S(2)}, u32[]{:S(2)}) collective-permute-start(f32[8,9216]{1,0:T(8,128)S(1)} %get-tuple-element.16), channel_id=1, source_target_pairs={{0,1},{1,0},{8,9},{9,8},{16,17},{17,16},{24,25},{25,24},{2,3},{3,2... | collective-permute-start | bytes 884744 | tf_op jit(solution)/shard_map/ppermute | solution.py:22
  25.3 12.6 %copy-start.2 = (f32[1,9216]{1,0:T(1,128)}, f32[1,9216]{1,0:T(1,128)S(1)}, u32[]{:S(2)}) copy-start(f32[1,9216]{1,0:T(1,128)S(1)} %multiply_add_fusion.state) | copy-start | bytes 110596

commit v9 on v7

--- a/solution.py
+++ b/solution.py
@@ -9,7 +9,7 @@
 STEP = 100
 BETA = 1.0 - STEP ** (-0.8)
 LANES = 128
-PIECES = 4
+PIECES = 3
 VMEM = pl.BlockSpec(memory_space=pltpu.VMEM)
 HBM = pl.BlockSpec(memory_space=pltpu.HBM)
 

time: 38 us -> 38 us (level)
  no operation moved by 1% of the time
where the time goes in v9:
time: 38 us; the launch traced here: 37.9 us
  starting transfers between devices  12.8 us (34%)
  blocking collectives  11.4 us (30%)
  waiting for transfers between devices  10.2 us (27%)
  Pallas kernels  2.63 us (7%)
  between operations  0.75 us (2%)
    ppermute x12, starting transfers between devices, send_to(): return lax.ppermute(x, axes, [(i, target(i)) for i in range(size)])  12.8 us
    all_to_all x1, blocking collectives, on_device(): sums = lax.all_to_all(message, ('dp', 'wide', 'narrow'), 0, 0, tiled=True)  11.4 us
    ppermute x12, waiting for transfers between devices, send_to(): return lax.ppermute(x, axes, [(i, target(i)) for i in range(size)])  10.2 us
    pallas_call x11, Pallas kernels, call(): pl.pallas_call(kernel, out_shape=[jax.ShapeDtypeStruct(shape, jnp.float32...  2.63 us
  transfers between devices with their start and end apart: 12, of which 7 were waited for; matrix products, arithmetic and copies ran while one was open for 0% of the time, Pallas kernels for 1%

profile of v9, /device:TPU:0, one launch (start us, length us, event | category | flops | bytes accessed | tf_op | source)
XLA Modules:
  0.0 37.9 jit_solution(11089981164019325884)
XLA Ops:
  0.6 1.0 %shard_map.67 = f32[8,9216]{1,0:T(8,128)S(1)} custom-call(bf16[8,73728]{1,0:T(8,128)(2,1)} %bitcast.9), custom_call_target="tpu_custom_call" | custom-call | tf_op jit(solution)/shard_map/pallas_call | solution.py:46
  1.6 0.5 %collective-permute-start = (f32[8,9216]{1,0:T(8,128)S(1)}, f32[8,9216]{1,0:T(8,128)S(1)}, u32[]{:S(2)}, u32[]{:S(2)}) collective-permute-start(f32[8,9216]{1,0:T(8,128)S(1)} %shard_map.67), channel_id=1, source_target_pairs={{0,1},{1,0},{8,9},{9,8},{16,17},{17,16},{24,25},{25,24},{2,3},{3,2... | collective-permute-start | bytes 884744 | tf_op jit(solution)/shard_map/ppermute | solution.py:22
  2.2 0.3 collective-permute-start.4
  2.5 0.3 collective-permute-start.2
  2.8 0.5 %collective-permute-done.refs_1_ = f32[8,9216]{1,0:T(8,128)S(1)} collective-permute-done((f32[8,9216]{1,0:T(8,128)S(1)}, f32[8,9216]{1,0:T(8,128)S(1)}, u32[]{:S(2)}, u32[]{:S(2)}) %collective-permute-start) | collective-permute-done | bytes 294944 | tf_op jit(solution)/shard_map/ppermute | solution.py:22
  3.4 2.7 %collective-permute-start.1 = (f32[8,9216]{1,0:T(8,128)S(1)}, f32[8,9216]{1,0:T(8,128)S(1)}, u32[]{:S(2)}, u32[]{:S(2)}) collective-permute-start(f32[8,9216]{1,0:T(8,128)S(1)} %shard_map.68), channel_id=1, source_target_pairs={{0,17},{1,8},{8,25},{9,0},{16,1},{17,24},{24,9},{25,16},{2,19},{3,... | collective-permute-start | bytes 884744 | tf_op jit(solution)/shard_map/ppermute | solution.py:22
  6.1 0.4 %collective-permute-start.6 = (f32[8,9216]{1,0:T(8,128)S(1)}, f32[8,9216]{1,0:T(8,128)S(1)}, u32[]{:S(2)}, u32[]{:S(2)}) collective-permute-start(f32[8,9216]{1,0:T(8,128)S(1)} %shard_map.73), channel_id=1, source_target_pairs={{0,1},{1,0},{8,9},{9,8},{16,17},{17,16},{24,25},{25,24},{2,3},{3,2... | collective-permute-start | bytes 884744 | tf_op jit(solution)/shard_map/ppermute | solution.py:22
  6.5 0.0 collective-permute-done.4.refs_1_
  6.6 1.6 %collective-permute-start.5 = (f32[8,9216]{1,0:T(8,128)S(1)}, f32[8,9216]{1,0:T(8,128)S(1)}, u32[]{:S(2)}, u32[]{:S(2)}) collective-permute-start(f32[8,9216]{1,0:T(8,128)S(1)} %shard_map.72), channel_id=1, source_target_pairs={{0,16},{1,9},{8,24},{9,1},{16,0},{17,25},{24,8},{25,17},{2,18},{3,... | collective-permute-start | bytes 884744 | tf_op jit(solution)/shard_map/ppermute | solution.py:22
  8.1 2.3 %collective-permute-done.1.refs_1_ = f32[8,9216]{1,0:T(8,128)S(1)} collective-permute-done((f32[8,9216]{1,0:T(8,128)S(1)}, f32[8,9216]{1,0:T(8,128)S(1)}, u32[]{:S(2)}, u32[]{:S(2)}) %collective-permute-start.1) | collective-permute-done | bytes 294944 | tf_op jit(solution)/shard_map/ppermute | solution.py:22
  10.5 0.0 copy-start.4
  10.5 0.0 copy-start.1
  10.5 0.0 copy-start.3
  10.5 1.8 %collective-permute-start.3 = (f32[8,9216]{1,0:T(8,128)S(1)}, f32[8,9216]{1,0:T(8,128)S(1)}, u32[]{:S(2)}, u32[]{:S(2)}) collective-permute-start(f32[8,9216]{1,0:T(8,128)S(1)} %shard_map.70), channel_id=1, source_target_pairs={{0,17},{1,8},{8,25},{9,0},{16,1},{17,24},{24,9},{25,16},{2,19},{3,... | collective-permute-start | bytes 884744 | tf_op jit(solution)/shard_map/ppermute | solution.py:22
  12.4 0.0 collective-permute-done.6.refs_3_
  12.4 1.8 %collective-permute-done.5.refs_2_ = f32[8,9216]{1,0:T(8,128)S(1)} collective-permute-done((f32[8,9216]{1,0:T(8,128)S(1)}, f32[8,9216]{1,0:T(8,128)S(1)}, u32[]{:S(2)}, u32[]{:S(2)}) %collective-permute-start.5) | collective-permute-done | bytes 294944 | tf_op jit(solution)/shard_map/ppermute | solution.py:22
  14.2 2.6 %collective-permute-done.3.refs_1_ = f32[8,9216]{1,0:T(8,128)S(1)} collective-permute-done((f32[8,9216]{1,0:T(8,128)S(1)}, f32[8,9216]{1,0:T(8,128)S(1)}, u32[]{:S(2)}, u32[]{:S(2)}) %collective-permute-start.3) | collective-permute-done | bytes 294944 | tf_op jit(solution)/shard_map/ppermute | solution.py:22
  16.8 0.1 shard_map.74
  16.9 3.9 %collective-permute-start.7 = (f32[1,9600]{1,0:T(1,128)S(1)}, f32[1,9600]{1,0:T(1,128)S(1)}, u32[]{:S(2)}, u32[]{:S(2)}) collective-permute-start(f32[1,9600]{1,0:T(1,128)S(1)} %get-tuple-element.12), channel_id=1, source_target_pairs={{0,7},{1,6},{2,5},{3,4},{4,3},{5,2},{6,1},{7,0},{8,15},{9,14},{10,... | collective-permute-start | bytes 115208 | tf_op jit(solution)/shard_map/ppermute | solution.py:22
  20.9 0.6 %collective-permute-start.9 = (f32[1,9344]{1,0:T(1,128)S(1)}, f32[1,9344]{1,0:T(1,128)S(1)}, u32[]{:S(2)}, u32[]{:S(2)}) collective-permute-start(f32[1,9344]{1,0:T(1,128)S(1)} %get-tuple-element.14), channel_id=1, source_target_pairs={{0,3},{1,2},{2,1},{3,0},{4,7},{5,6},{6,5},{7,4},{8,11},{9,10},{10,... | collective-permute-start | bytes 112136 | tf_op jit(solution)/shard_map/ppermute | solution.py:22
  21.5 0.2 collective-permute-start.10
  21.7 0.2 shard_map.75.fixed_in
  21.8 0.4 %collective-permute-start.11 = (f32[8,9216]{1,0:T(8,128)S(1)}, f32[8,9216]{1,0:T(8,128)S(1)}, u32[]{:S(2)}, u32[]{:S(2)}) collective-permute-start(f32[8,9216]{1,0:T(8,128)S(1)} %get-tuple-element.16), channel_id=1, source_target_pairs={{0,1},{1,0},{8,9},{9,8},{16,17},{17,16},{24,25},{25,24},{2,3},{3,2... | collective-permute-start | bytes 884744 | tf_op jit(solution)/shard_map/ppermute | solution.py:22
  22.2 0.4 %collective-permute-done.10 = f32[1,9216]{1,0:T(1,128)S(1)} collective-permute-done((f32[1,9216]{1,0:T(1,128)S(1)}, f32[1,9216]{1,0:T(1,128)S(1)}, u32[]{:S(2)}, u32[]{:S(2)}) %collective-permute-start.10) | collective-permute-done | bytes 36896 | tf_op jit(solution)/shard_map/ppermute | solution.py:22
  22.7 1.6 %collective-permute-done.9 = f32[1,9344]{1,0:T(1,128)S(1)} collective-permute-done((f32[1,9344]{1,0:T(1,128)S(1)}, f32[1,9344]{1,0:T(1,128)S(1)}, u32[]{:S(2)}, u32[]{:S(2)}) %collective-permute-start.9) | collective-permute-done | bytes 37408 | tf_op jit(solution)/shard_map/ppermute | solution.py:22
  24.3 0.9 %collective-permute-done.8 = f32[1,9472]{1,0:T(1,128)S(1)} collective-permute-done((f32[1,9472]{1,0:T(1,128)S(1)}, f32[1,9472]{1,0:T(1,128)S(1)}, u32[]{:S(2)}, u32[]{:S(2)}) %collective-permute-start.8) | collective-permute-done | bytes 37920 | tf_op jit(solution)/shard_map/ppermute | solution.py:22
  25.2 0.0 collective-permute-done.7
  25.2 0.1 multiply_add_fusion.state
  25.3 0.0 copy-start.2
  25.3 0.2 shard_map.76
  25.5 11.4 %all_to_all.11 = f32[32,1,128]{2,1,0:T(1,128)S(1)} all-to-all(f32[32,1,128]{2,1,0:T(1,128)S(1)} %bitcast.19), channel_id=1, replica_groups=mesh['dp'=4,'wide'=4,'narrow'=2] {'dp','wide','narrow'}, dimensions={0} | all-to-all | bytes 32768 | tf_op jit(solution)/shard_map/all_to_all | solution.py:258
  36.9 1.0 %shard_map.77 = (f32[8,9216]{1,0:T(8,128)}, f32[1,8]{1,0:T(1,128)}) custom-call(f32[32,128]{1,0:T(8,128)S(1)} %bitcast.18, f32[8,9216]{1,0:T(8,128)S(1)} %get-tuple-element.18.refs_1_), custom_call_target="tpu_custom_call" | custom-call | tf_op jit(solution)/shard_map/pallas_call | solution.py:46
  (16 shorter events, 0.2 us)
Async XLA Ops:
  0.6 1.5 %copy-start = (bf16[1,8,73728]{2,1,0:T(8,128)(2,1)S(1)}, bf16[1,8,73728]{2,1,0:T(8,128)(2,1)}, u32[]{:S(2)}) copy-start(bf16[1,8,73728]{2,1,0:T(8,128)(2,1)} %param.4) | copy-start | bytes 3538948
  1.6 1.7 %collective-permute-start = (f32[8,9216]{1,0:T(8,128)S(1)}, f32[8,9216]{1,0:T(8,128)S(1)}, u32[]{:S(2)}, u32[]{:S(2)}) collective-permute-start(f32[8,9216]{1,0:T(8,128)S(1)} %shard_map.67), channel_id=1, source_target_pairs={{0,1},{1,0},{8,9},{9,8},{16,17},{17,16},{24,25},{25,24},{2,3},{3,2... | collective-permute-start | bytes 884744 | tf_op jit(solution)/shard_map/ppermute | solution.py:22
  2.2 4.3 %collective-permute-start.4 = (f32[8,9216]{1,0:T(8,128)S(1)}, f32[8,9216]{1,0:T(8,128)S(1)}, u32[]{:S(2)}, u32[]{:S(2)}) collective-permute-start(f32[8,9216]{1,0:T(8,128)S(1)} %shard_map.71), channel_id=1, source_target_pairs={{0,1},{1,0},{8,9},{9,8},{16,17},{17,16},{24,25},{25,24},{2,3},{3,2... | collective-permute-start | bytes 884744 | tf_op jit(solution)/shard_map/ppermute | solution.py:22
  2.5 5.6 %collective-permute-start.2 = (f32[8,9216]{1,0:T(8,128)S(1)}, f32[8,9216]{1,0:T(8,128)S(1)}, u32[]{:S(2)}, u32[]{:S(2)}) collective-permute-start(f32[8,9216]{1,0:T(8,128)S(1)} %shard_map.69), channel_id=1, source_target_pairs={{0,1},{1,0},{8,9},{9,8},{16,17},{17,16},{24,25},{25,24},{2,3},{3,2... | collective-permute-start | bytes 884744 | tf_op jit(solution)/shard_map/ppermute | solution.py:22
  3.4 7.1 %collective-permute-start.1 = (f32[8,9216]{1,0:T(8,128)S(1)}, f32[8,9216]{1,0:T(8,128)S(1)}, u32[]{:S(2)}, u32[]{:S(2)}) collective-permute-start(f32[8,9216]{1,0:T(8,128)S(1)} %shard_map.68), channel_id=1, source_target_pairs={{0,17},{1,8},{8,25},{9,0},{16,1},{17,24},{24,9},{25,16},{2,19},{3,... | collective-permute-start | bytes 884744 | tf_op jit(solution)/shard_map/ppermute | solution.py:22
  6.1 6.3 %collective-permute-start.6 = (f32[8,9216]{1,0:T(8,128)S(1)}, f32[8,9216]{1,0:T(8,128)S(1)}, u32[]{:S(2)}, u32[]{:S(2)}) collective-permute-start(f32[8,9216]{1,0:T(8,128)S(1)} %shard_map.73), channel_id=1, source_target_pairs={{0,1},{1,0},{8,9},{9,8},{16,17},{17,16},{24,25},{25,24},{2,3},{3,2... | collective-permute-start | bytes 884744 | tf_op jit(solution)/shard_map/ppermute | solution.py:22
  6.6 7.6 %collective-permute-start.5 = (f32[8,9216]{1,0:T(8,128)S(1)}, f32[8,9216]{1,0:T(8,128)S(1)}, u32[]{:S(2)}, u32[]{:S(2)}) collective-permute-start(f32[8,9216]{1,0:T(8,128)S(1)} %shard_map.72), channel_id=1, source_target_pairs={{0,16},{1,9},{8,24},{9,1},{16,0},{17,25},{24,8},{25,17},{2,18},{3,... | collective-permute-start | bytes 884744 | tf_op jit(solution)/shard_map/ppermute | solution.py:22
  10.5 11.1 %copy-start.4 = (f32[9216]{0:T(1024)S(1)}, f32[9216]{0:T(1024)}, u32[]{:S(2)}) copy-start(f32[9216]{0:T(1024)} %param.7) | copy-start | bytes 110596
  10.5 11.1 %copy-start.1 = (bf16[8,9216]{1,0:T(8,128)(2,1)S(1)}, bf16[8,9216]{1,0:T(8,128)(2,1)}, u32[]{:S(2)}) copy-start(bf16[8,9216]{1,0:T(8,128)(2,1)} %weight.1) | copy-start | bytes 442372
  10.5 11.1 %copy-start.3 = (f32[8]{0:T(128)S(1)}, f32[8]{0:T(128)}, u32[]{:S(2)}) copy-start(f32[8]{0:T(128)} %param.6) | copy-start | bytes 100
  10.5 6.2 %collective-permute-start.3 = (f32[8,9216]{1,0:T(8,128)S(1)}, f32[8,9216]{1,0:T(8,128)S(1)}, u32[]{:S(2)}, u32[]{:S(2)}) collective-permute-start(f32[8,9216]{1,0:T(8,128)S(1)} %shard_map.70), channel_id=1, source_target_pairs={{0,17},{1,8},{8,25},{9,0},{16,1},{17,24},{24,9},{25,16},{2,19},{3,... | collective-permute-start | bytes 884744 | tf_op jit(solution)/shard_map/ppermute | solution.py:22
  16.9 8.3 %collective-permute-start.7 = (f32[1,9600]{1,0:T(1,128)S(1)}, f32[1,9600]{1,0:T(1,128)S(1)}, u32[]{:S(2)}, u32[]{:S(2)}) collective-permute-start(f32[1,9600]{1,0:T(1,128)S(1)} %get-tuple-element.12), channel_id=1, source_target_pairs={{0,7},{1,6},{2,5},{3,4},{4,3},{5,2},{6,1},{7,0},{8,15},{9,14},{10,... | collective-permute-start | bytes 115208 | tf_op jit(solution)/shard_map/ppermute | solution.py:22
  20.8 4.4 %collective-permute-start.8 = (f32[1,9472]{1,0:T(1,128)S(1)}, f32[1,9472]{1,0:T(1,128)S(1)}, u32[]{:S(2)}, u32[]{:S(2)}) collective-permute-start(f32[1,9472]{1,0:T(1,128)S(1)} %get-tuple-element.13), channel_id=1, source_target_pairs={{0,5},{1,4},{2,7},{3,6},{4,1},{5,0},{6,3},{7,2},{8,13},{9,12},{10,... | collective-permute-start | bytes 113672 | tf_op jit(solution)/shard_map/ppermute | solution.py:22
  20.9 3.4 %collective-permute-start.9 = (f32[1,9344]{1,0:T(1,128)S(1)}, f32[1,9344]{1,0:T(1,128)S(1)}, u32[]{:S(2)}, u32[]{:S(2)}) collective-permute-start(f32[1,9344]{1,0:T(1,128)S(1)} %get-tuple-element.14), channel_id=1, source_target_pairs={{0,3},{1,2},{2,1},{3,0},{4,7},{5,6},{6,5},{7,4},{8,11},{9,10},{10,... | collective-permute-start | bytes 112136 | tf_op jit(solution)/shard_map/ppermute | solution.py:22
  21.5 1.2 %collective-permute-start.10 = (f32[1,9216]{1,0:T(1,128)S(1)}, f32[1,9216]{1,0:T(1,128)S(1)}, u32[]{:S(2)}, u32[]{:S(2)}) collective-permute-start(f32[1,9216]{1,0:T(1,128)S(1)} %get-tuple-element.15), channel_id=1, source_target_pairs={{0,1},{1,0},{8,9},{9,8},{16,17},{17,16},{24,25},{25,24},{2,3},{3,2... | collective-permute-start | bytes 110600 | tf_op jit(solution)/shard_map/ppermute | solution.py:22
  21.8 3.5 %collective-permute-start.11 = (f32[8,9216]{1,0:T(8,128)S(1)}, f32[8,9216]{1,0:T(8,128)S(1)}, u32[]{:S(2)}, u32[]{:S(2)}) collective-permute-start(f32[8,9216]{1,0:T(8,128)S(1)} %get-tuple-element.16), channel_id=1, source_target_pairs={{0,1},{1,0},{8,9},{9,8},{16,17},{17,16},{24,25},{25,24},{2,3},{3,2... | collective-permute-start | bytes 884744 | tf_op jit(solution)/shard_map/ppermute | solution.py:22
  25.3 12.6 %copy-start.2 = (f32[1,9216]{1,0:T(1,128)}, f32[1,9216]{1,0:T(1,128)S(1)}, u32[]{:S(2)}) copy-start(f32[1,9216]{1,0:T(1,128)S(1)} %multiply_add_fusion.state) | copy-start | bytes 110596
